TPU v7x, 32 devices: a whole 2x2x4 slice. The times are simulated.
32 devices in a mesh: gx: 4 (over y, core), gy: 8 (over z, x).
Axes of the slice: x: 2, y: 2, z: 4, core: 2. Of those that a mesh axis runs over, the one named last changes fastest.
Arguments:
- tiles: float32 [2, 3, 16384, 128], P(None, None, ('gx', 'gy')), may hold values from -6 to 6
- tile_owner: int32 [16384, 1], P(('gx', 'gy')), may hold values from 0 to 31; in each aligned block of 512 rows (0 to 511, 512 to 1023, ...) at most 32 rows name the same one
- tile_slot: int32 [16384], P(('gx', 'gy')), may hold values from 0 to 1023
- tile_count: int32 [32], P(('gx', 'gy')), may hold values from 384 to 512, as said below
- green: float32 [2, 6, 1, 2048, 2048], P(None, None, None, ('gx', 'gy')), may hold values from -6 to 6
Outputs:
- field_hat: float32 [2, 3, 1, 2048, 2048], P(None, None, None, ('gx', 'gy'))
Inputs may be any that keep to these rules, and one draw needn't show every extreme that they name: `tile_owner`: within the 512 entries of one device, live or not, no owner is named by more than 32; that many is reached. `tile_count`: some device has all 512 entries live.
All inputs are finite; a program needn't handle non-finite values.
Results may differ from a plain program's by a relative error of at most 0.00007.
Values sent between devices are 32-bit elements; how exact they have to be, the bound alone decides.
No kernel may reach another device: no remote copies, remote signals or barrier semaphores. Data moves between devices by JAX's collectives and lax.ppermute only.
A program may use at most 128 MiB of HBM per device.

v0:
```python
import functools
import math

import jax
import jax.numpy as jnp
import ml_dtypes
import numpy as np
from jax import lax
from jax.experimental import pallas as pl
from jax.experimental.pallas import tpu as pltpu
from jax.sharding import PartitionSpec as P

pair_index = ((0, 3, 4), (3, 1, 5), (4, 5, 2))
by_rows = (((1,), (1,)), ((), ()))


def params(mebibytes):
    return pltpu.CompilerParams(vmem_limit_bytes=mebibytes * 1024 * 1024)


def in_hbm(array):
    return pltpu.with_memory_space_constraint(array, pltpu.HBM)


def in_vmem(array):
    return pltpu.with_memory_space_constraint(array, pltpu.VMEM)


def cost(flops, moved):
    return pl.CostEstimate(flops=flops, bytes_accessed=moved, transcendentals=0)


def angles(rows, columns, length):
    products = np.outer(np.arange(rows), np.arange(columns)) % length
    return 2.0 * math.pi / length * products


def halves(table):
    wide = np.asarray(table, np.float32)
    high = wide.astype(ml_dtypes.bfloat16)
    low = (wide - high.astype(np.float32)).astype(ml_dtypes.bfloat16)
    return jnp.asarray(high), jnp.asarray(low)


def split_two(data):
    high = data.astype(jnp.bfloat16)
    return high, (data - high.astype(jnp.float32)).astype(jnp.bfloat16)


def split_three(data):
    high = data.astype(jnp.bfloat16)
    rest = data - high.astype(jnp.float32)
    middle = rest.astype(jnp.bfloat16)
    return high, middle, (rest - middle.astype(jnp.float32)).astype(jnp.bfloat16)


def dot_rows(left, right):
    return lax.dot_general(left, right, by_rows, preferred_element_type=jnp.float32)


def dot_rows_split(table, data):
    rows, depth = table.shape
    table_high, table_low = split_two(table)
    high, low = split_two(data)
    if depth > 128:
        both = dot_rows(jnp.concatenate([table_high, table_low]), high)
        return both[:rows] + both[rows:] + dot_rows(table_high, low)
    left = jnp.concatenate(
        [
            jnp.concatenate([table_high, table_high], axis=1),
            jnp.concatenate([table_low, jnp.zeros_like(table_low)], axis=1),
        ]
    )
    both = dot_rows(left, jnp.concatenate([high, low], axis=1))
    return both[:rows] + both[rows:]


def flat_fft(values, times):
    length = len(values)
    if length == 1:
        return values
    even = flat_fft(values[0::2], times)
    odd = flat_fft(values[1::2], times)
    lower, upper = [], []
    for k in range(length // 2):
        turned = times(odd[k], k, length)
        lower.append(jax.tree.map(lambda a, b: a + b, even[k], turned))
        upper.append(jax.tree.map(lambda a, b: a - b, even[k], turned))
    return lower + upper


def times_pair(value, k, length):
    real, imag = value
    if k == 0:
        return value
    if 4 * k == length:
        return (imag, -real)
    cos_k = math.cos(2.0 * math.pi * k / length)
    sin_k = math.sin(2.0 * math.pi * k / length)
    return (real * cos_k + imag * sin_k, imag * cos_k - real * sin_k)


def place_of(owner, count_gl):
    shift = count_gl.bit_length() - 1
    z = ((owner >> shift) & 1) * 2 + ((owner >> (shift + 1)) & 1)
    return (((owner >> (shift + 2)) << shift) + (owner & (count_gl - 1))) * 4 + z


def owner_order(devices, count_gl):
    order = [0] * devices
    for owner in range(devices):
        order[place_of(owner, count_gl)] = owner
    return order


def pack_kernel(
    devices, count_gl, per_owner, comps, with_slots, count, me, owner_row, slot_row, tiles, *refs
):
    out, held, made, lists, sems, out_sems = refs[-6:]
    listed = owner_row.shape[1]
    fetches = [
        pltpu.make_async_copy(owner_row, lists.at[0], sems.at[0]),
        pltpu.make_async_copy(slot_row, lists.at[1], sems.at[1]),
    ]
    fetches += [
        pltpu.make_async_copy(tiles.at[:, comp], held.at[i], sems.at[2 + i])
        for i, comp in enumerate(comps)
    ]
    for fetch in fetches:
        fetch.start()
    sender = lax.broadcasted_iota(jnp.int32, (listed, listed), 0)
    reader = lax.broadcasted_iota(jnp.int32, (listed, listed), 1)
    before = jnp.where(sender < reader, 1.0, 0.0).astype(jnp.bfloat16)
    live = lax.broadcasted_iota(jnp.int32, (1, listed), 1) < count[0]
    fetches[0].wait()
    place = jnp.where(live, place_of(lists[0], count_gl), -1)
    place_at = lax.broadcasted_iota(jnp.int32, (devices, listed), 0)
    named = jnp.where(place_at == place, 1.0, 0.0)
    counted = jnp.dot(named.astype(jnp.bfloat16), before, preferred_element_type=jnp.float32)
    rank = jnp.sum(counted * named, axis=0, keepdims=True).astype(jnp.int32)
    target = jnp.where(live, place * per_owner + rank, -1)
    target_at = lax.broadcasted_iota(jnp.int32, (devices * per_owner, listed), 0)
    chosen = jnp.where(target_at == target, 1.0, 0.0).astype(jnp.bfloat16)
    fetches[1].wait()
    sends = []

    def send(start, rows):
        part = pl.ds(start, rows)
        copy = pltpu.make_async_copy(
            made.at[:, part], out.at[:, part], out_sems.at[len(sends)]
        )
        copy.start()
        sends.append(copy)

    if with_slots:
        stated = lists[1] + 1
        lane = rank + (me[0] & (128 // per_owner - 1)) * per_owner
        lane_at = lax.broadcasted_iota(jnp.int32, (128, listed), 0)
        laned = jnp.where(lane_at == lane, 1.0, 0.0).astype(jnp.bfloat16)
        coarse = (named * (stated >> 5).astype(jnp.float32)).astype(jnp.bfloat16)
        fine = (named * (stated & 31).astype(jnp.float32)).astype(jnp.bfloat16)
        slots = 32.0 * dot_rows(coarse, laned) + dot_rows(fine, laned)
        start = 2 * len(comps) * per_owner
        made[:, start:, :] = jnp.broadcast_to(slots[:, None, :], (devices, 8, 128))
        send(start, 8)
    for i in range(len(comps)):
        fetches[2 + i].wait()
        parts = [part for r in range(2) for part in split_two(held[i, r])]
        got = jnp.dot(
            chosen, jnp.concatenate(parts, axis=1), preferred_element_type=jnp.float32
        )
        for r in range(2):
            whole = got[:, 256 * r : 256 * r + 128] + got[:, 256 * r + 128 : 256 * r + 256]
            start = (2 * i + r) * per_owner
            made[:, start : start + per_owner, :] = whole.reshape(devices, per_owner, 128)
            send(start, per_owner)
    for copy in sends:
        copy.wait()


def pack(tiles, comps, owner_row, slot_row, count, me, after, devices, count_gl, per_owner):
    listed = tiles.shape[2]
    with_slots = after is None
    rows = 2 * len(comps) * per_owner + (8 if with_slots else 0)
    extra = () if with_slots else (after,)
    return pl.pallas_call(
        functools.partial(pack_kernel, devices, count_gl, per_owner, comps, with_slots),
        out_shape=pltpu.HBM((devices, rows, 128), jnp.float32),
        in_specs=[pl.BlockSpec(memory_space=pltpu.SMEM)] * 2
        + [pl.BlockSpec(memory_space=pltpu.HBM)] * (3 + len(extra)),
        out_specs=pl.BlockSpec(memory_space=pltpu.HBM),
        scratch_shapes=[
            pltpu.VMEM((len(comps), 2, listed, 128), jnp.float32),
            pltpu.VMEM((devices, rows, 128), jnp.float32),
            pltpu.VMEM((2, 1, listed), jnp.int32),
            pltpu.SemaphoreType.DMA((2 + len(comps),)),
            pltpu.SemaphoreType.DMA((1 + 2 * len(comps),)),
        ],
        compiler_params=params(24),
        cost_estimate=cost(
            devices * per_owner * listed * 512 * 2 * len(comps), devices * rows * 1024
        ),
    )(count, me, *[in_hbm(a) for a in (owner_row, slot_row, tiles, *extra)])


def complex_table(cos_part, sin_part):
    return np.concatenate(
        [
            np.concatenate([cos_part, sin_part], axis=1),
            np.concatenate([-sin_part, cos_part], axis=1),
        ]
    ).astype(np.float32)


def slab_kernel(count, x_local, blocks, per_owner, first, table, twist, data, *refs):
    if first:
        out, landings, made, slab, turned, out_sems = refs
    else:
        landings, out, made, slab, turned, out_sems = refs
    devices = data.shape[0]
    entries = devices * per_owner
    group = 128 // x_local
    pairs = blocks // group
    shift = blocks.bit_length() - 1
    if first:
        every = 128 // per_owner
        stated = [
            sum([data[o, data.shape[1] - 8 :][:1] for o in range(start, start + every)])
            for start in range(0, devices, every)
        ]
        slot = jnp.concatenate(stated, axis=1).astype(jnp.int32) - 1
        landing = jnp.where(slot >= 0, (slot & (blocks - 1)) * x_local + (slot >> shift), -1)
        landings[...] = landing
    else:
        landing = landings[...]
    parts = []
    for i in range(2 * count):
        one = data[:, i * per_owner : (i + 1) * per_owner, :]
        parts.extend(split_two(one.reshape(entries, 128)))
    parts = jnp.concatenate(parts, axis=1)
    for start in range(0, blocks * x_local, 256):
        place = start + lax.broadcasted_iota(jnp.int32, (256, entries), 0)
        chosen = jnp.where(place == landing, 1.0, 0.0).astype(jnp.bfloat16)
        got = jnp.dot(chosen, parts, preferred_element_type=jnp.float32)
        for i in range(2 * count):
            slab[i // 2, i % 2, start : start + 256, :] = (
                got[:, 256 * i : 256 * i + 128] + got[:, 256 * i + 128 : 256 * i + 256]
            )
    sends = []
    for index in range(count):

        @pl.loop(0, x_local // 8)
        def _(step):
            at = pl.multiple_of(step * 8, 8)
            values = [
                tuple(slab[index, r, pl.ds(t * x_local + at, 8), :] for r in range(2))
                for t in range(blocks)
            ]
            waves = flat_fft(values, times_pair)
            for k in range(blocks):
                real, imag = waves[k]
                cos_k, sin_k = twist[0, k : k + 1, :], twist[1, k : k + 1, :]
                rows = pl.ds(((k % pairs) * group + k // pairs) * x_local + at, 8)
                turned[rows, :128] = real * cos_k + imag * sin_k
                turned[rows, 128:] = imag * cos_k - real * sin_k

        for start in range(0, pairs, 2):
            moved = dot_rows_split(table[...], turned[start * 128 : (start + 2) * 128, :])
            for k in range(2):
                for r in range(2):
                    rows = pl.ds(r * pairs + start + k, 128, stride=2 * pairs)
                    made[index, rows, :] = moved[
                        r * 128 : (r + 1) * 128, k * 128 : (k + 1) * 128
                    ]
        send = pltpu.make_async_copy(
            made.at[index].reshape(devices, made.shape[1] // devices, 128),
            out.at[:, index],
            out_sems.at[index],
        )
        send.start()
        sends.append(send)
    for send in sends:
        send.wait()


def slab_waves(data, landings, x_local, blocks, count_gl, per_owner):
    devices = data.shape[0]
    count = data.shape[1] // (2 * per_owner)
    first = landings is None
    fine = angles(128, 128, 128)
    order = owner_order(devices, count_gl)
    fine = fine.reshape(devices, 128 // devices, 128)[order].reshape(128, 128)
    table = complex_table(np.cos(fine), np.sin(fine))
    twist_angle = angles(blocks, 128, blocks * 128)
    twist = np.stack([np.cos(twist_angle), np.sin(twist_angle)]).astype(np.float32)
    entries = devices * per_owner
    rows = blocks * x_local * 2
    out = pltpu.HBM((devices, count, rows // devices, 128), jnp.float32)
    landing = jax.ShapeDtypeStruct((1, entries), jnp.int32)
    in_place = pl.BlockSpec(memory_space=pltpu.VMEM)
    return pl.pallas_call(
        functools.partial(slab_kernel, count, x_local, blocks, per_owner, first),
        out_shape=(out, landing) if first else out,
        in_specs=[in_place] * (3 if first else 4),
        out_specs=(
            (pl.BlockSpec(memory_space=pltpu.HBM), in_place)
            if first
            else pl.BlockSpec(memory_space=pltpu.HBM)
        ),
        scratch_shapes=[
            pltpu.VMEM((count, rows, 128), jnp.float32),
            pltpu.VMEM((count, 2, blocks * x_local, 128), jnp.float32),
            pltpu.VMEM((blocks * x_local, 256), jnp.float32),
            pltpu.SemaphoreType.DMA((count,)),
        ],
        compiler_params=params(24),
        cost_estimate=cost(
            count * blocks * x_local * (entries * 1024 + 512 * 1024),
            count * (entries * 1024 + rows * 512),
        ),
    )(jnp.asarray(table), jnp.asarray(twist), in_vmem(data), *(() if first else (landings,)))


def choose(options, mask_of):
    made = options[0]
    for i in range(1, len(options)):
        made = jnp.where(mask_of(i), options[i], made)
    return made


def x_steps(
    devices, x_local, y_local, blocks, order, index, twist, table, data, turned, columns, store
):
    group = 128 // x_local
    pairs = blocks // group
    kept = y_local // blocks
    narrow = kept * pairs
    banks = 2 * group

    @pl.loop(0, kept)
    def _(step):
        at = pl.multiple_of(step * 2 * pairs, 2 * pairs)
        values = [
            tuple(
                data[order.index(o), index, pl.ds(at + r * pairs, pairs), :] for r in range(2)
            )
            for o in range(devices)
        ]
        waves = flat_fft(values, times_pair)
        rows = pl.ds(pl.multiple_of(step * pairs, pairs), pairs)
        for k in range(devices):
            real, imag = waves[k]
            cos_k, sin_k = twist[0, k : k + 1, :], twist[1, k : k + 1, :]
            turned[k, rows, :128] = real * cos_k + imag * sin_k
            turned[k, rows, 128:] = imag * cos_k - real * sin_k

    lane = lax.broadcasted_iota(jnp.int32, (1, 128), 1)
    square = banks * narrow == 128 and 128 // narrow == banks
    together = min(devices, 256 // narrow)
    for start in range(0, devices, together):
        stacked = turned[start : start + together].reshape(together * narrow, 256)
        moved = dot_rows_split(table[...], stacked)
        if square:
            for base in range(0, together, banks):
                rolled = []
                for bank in range(banks):
                    one = moved[bank * x_local : (bank + 1) * x_local, base * narrow :][:, :128]
                    rolled.append(pltpu.roll(one, bank * narrow, 1) if bank else one)
                for k in range(banks):
                    options = [rolled[(place - k) % banks] for place in range(banks)]
                    rows = pl.ds(start + base + k, x_local, stride=devices)
                    columns[rows, :] = choose(options, lambda i: lane // narrow == i)
        else:
            for k in range(together):
                one = jnp.concatenate(
                    [
                        moved[bank * x_local : (bank + 1) * x_local, k * narrow : (k + 1) * narrow]
                        for bank in range(banks)
                    ],
                    axis=1,
                )
                columns[pl.ds(start + k, x_local, stride=devices), :] = one
    for start in range(0, devices * x_local, 128):
        block = columns[start : start + 128, :].T
        pieces = [block[bank * narrow : (bank + 1) * narrow] for bank in range(banks)]
        for bank in range(banks):
            one = pieces[bank]
            if square:
                options = [pieces[(bank + k) % banks] for k in range(banks)]
                one = choose(options, lambda i: lane % banks == i)
            for step in range(kept):
                row = step * blocks + (bank % group) * pairs
                store(bank // group, row, start, one[step * pairs : (step + 1) * pairs])


def mix_rows(rows, columns, tensor, waves, sums, terms):
    for row, entry, wave in terms:
        green_real, green_imag = tensor[entry, 0, rows, columns], tensor[entry, 1, rows, columns]
        real, imag = waves[wave][0, rows, columns], waves[wave][1, rows, columns]
        real_term = green_real * real - green_imag * imag
        imag_term = green_real * imag + green_imag * real
        old = sums[row]
        sums[row] = (
            (real_term, imag_term) if old is None else (old[0] + real_term, old[1] + imag_term)
        )
    return sums


def mix_pieces(y_local, width, made, out, out_sems, sums_of):
    sends = []
    for piece in range(made.shape[0]):
        columns = pl.ds(piece * width, width)

        @pl.loop(0, y_local // 8)
        def _(step):
            rows = pl.ds(pl.multiple_of(step * 8, 8), 8)
            for row, pair in enumerate(sums_of(rows, columns)):
                for r in range(2):
                    made[piece, r, row, rows, :] = pair[r]

        send = pltpu.make_async_copy(
            made.at[piece], out.at[:, :, :, columns], out_sems.at[piece]
        )
        send.start()
        sends.append(send)
    for send in sends:
        send.wait()


def fetch_entries(green, tensor, entries, sems):
    fetches = [
        pltpu.make_async_copy(green.at[:, entry], tensor.at[i], sems.at[i])
        for i, entry in enumerate(entries)
    ]
    for fetch in fetches:
        fetch.start()
    return fetches


early_entries, late_entries = (0, 1, 3, 4, 5), (4, 5, 2)


def early_kernel(sizes, twist, table, data, green, out, *scratch):
    y_local, x_cells = green.shape[2:]
    turned, columns, tensor, kept, made, in_sems, out_sems = scratch
    fetches = fetch_entries(green, tensor, early_entries, in_sems)
    for comp in range(2):

        def store(r, row, start, block):
            kept[comp, r, row : row + block.shape[0], start : start + 128] = block

        x_steps(*sizes, comp, twist, table, data, turned, columns, store)
    for fetch in fetches:
        fetch.wait()
    terms = [
        (row, early_entries.index(pair_index[row][comp]), comp)
        for row in range(3)
        for comp in range(2)
    ]
    waves = [kept.at[0], kept.at[1]]

    def sums_of(rows, columns):
        return mix_rows(rows, columns, tensor, waves, [None] * 3, terms)

    mix_pieces(y_local, x_cells // made.shape[0], made, out, out_sems, sums_of)


def last_kernel(sizes, twist, table, data, green, partial, out, *scratch):
    y_local, x_cells = green.shape[2:]
    turned, columns, tensor, kept, held, made, in_sems, out_sems = scratch
    fetches = fetch_entries(green, tensor, late_entries, in_sems)
    fetches.append(pltpu.make_async_copy(partial, held, in_sems.at[len(late_entries)]))
    fetches[-1].start()

    def store(r, row, start, block):
        kept[r, row : row + block.shape[0], start : start + 128] = block

    x_steps(*sizes, 0, twist, table, data, turned, columns, store)
    for fetch in fetches:
        fetch.wait()

    def sums_of(rows, columns):
        sums = [(held[0, row, rows, columns], held[1, row, rows, columns]) for row in range(3)]
        return mix_rows(rows, columns, tensor, [kept], sums, [(row, row, 0) for row in range(3)])

    mix_pieces(y_local, x_cells // made.shape[0], made, out, out_sems, sums_of)


def x_tables(devices, x_local, y_cells):
    x_cells = devices * x_local
    group = 128 // x_local
    fine = angles(x_local, x_local, x_local)
    scale = 1.0 / math.sqrt(x_cells * y_cells)
    apart = np.eye(group) * scale
    table = complex_table(np.kron(apart, np.cos(fine)), np.kron(apart, np.sin(fine)))
    angle = np.tile(angles(devices, x_local, x_cells), (1, group))
    twist = np.stack([np.cos(angle), np.sin(angle)]).astype(np.float32)
    return jnp.asarray(twist), jnp.asarray(table)


def x_scratch(devices, x_local, y_local):
    return [
        pltpu.VMEM((devices, y_local * x_local // 128, 256), jnp.float32),
        pltpu.VMEM((devices * x_local, 2 * y_local), jnp.float32),
    ]


def mixed_waves(data, green, partial, devices, x_local, y_local, y_cells, count_gl):
    x_cells = devices * x_local
    pieces = 8
    sizes = (devices, x_local, y_local, y_cells // 128, owner_order(devices, count_gl))
    first = partial is None
    comps, entries = (2, 5) if first else (1, 3)
    plane = (y_local, x_cells)
    held = [pltpu.VMEM((entries, 2) + plane, jnp.float32)]
    if first:
        held += [pltpu.VMEM((2, 2) + plane, jnp.float32)]
    else:
        held += [
            pltpu.VMEM((2,) + plane, jnp.float32),
            pltpu.VMEM((2, 3) + plane, jnp.float32),
        ]
    operands = (green,) if first else (green, partial)
    return pl.pallas_call(
        functools.partial(early_kernel if first else last_kernel, sizes),
        out_shape=pltpu.HBM((2, 3) + plane, jnp.float32),
        in_specs=[pl.BlockSpec(memory_space=pltpu.VMEM)] * 3
        + [pl.BlockSpec(memory_space=pltpu.HBM)] * len(operands),
        out_specs=pl.BlockSpec(memory_space=pltpu.HBM),
        scratch_shapes=x_scratch(devices, x_local, y_local)
        + held
        + [
            pltpu.VMEM((pieces, 2, 3, y_local, x_cells // pieces), jnp.float32),
            pltpu.SemaphoreType.DMA((5,)),
            pltpu.SemaphoreType.DMA((pieces,)),
        ],
        compiler_params=params(40),
        cost_estimate=cost(
            comps * x_cells * y_local * (x_local * 24 + 24), x_cells * y_local * 64
        ),
    )(
        *x_tables(devices, x_local, y_cells),
        in_vmem(data),
        *[in_hbm(a) for a in operands],
    )


def gate_kernel(data, after, out):
    del data, after, out


def once_after(data, after):
    return pl.pallas_call(
        gate_kernel,
        out_shape=pltpu.HBM(data.shape, data.dtype),
        in_specs=[pl.BlockSpec(memory_space=pltpu.HBM), pl.BlockSpec(memory_space=pl.ANY)],
        out_specs=pl.BlockSpec(memory_space=pltpu.HBM),
        input_output_aliases={0: 0},
        compiler_params=params(1),
        cost_estimate=cost(0, 0),
    )(in_hbm(data), after)


places = ("gx", "gl", "zl", "zh")


def exchange(data):
    return lax.all_to_all(data, places, split_axis=0, concat_axis=0, tiled=True)


def per_device(tiles, tile_owner, tile_slot, tile_count, green):
    count_gl = lax.axis_size("gl")
    devices = lax.axis_size("gx") * 4 * count_gl
    tile_total, tile_len = tiles.shape[2], tiles.shape[3]
    planes, y_local, x_cells = green.shape[2:]
    y_cells = y_local * devices
    x_local = x_cells // devices
    blocks = y_cells // tile_len
    per_owner = max(2, 2 * tile_total // devices)
    assert planes == 1 and tile_len == 128
    owner_row, slot_row = tile_owner.reshape(1, tile_total), tile_slot.reshape(1, tile_total)
    green = green.reshape(2, 6, y_local, x_cells)
    me = lax.axis_index(places).reshape(1).astype(jnp.int32)
    lists = (owner_row, slot_row, tile_count, me)
    early = pack(tiles, (0, 1), *lists, None, devices, count_gl, per_owner)
    late = pack(tiles, (2,), *lists, early, devices, count_gl, per_owner)
    early = exchange(early)
    late = exchange(once_after(late, early))
    grid = (x_local, blocks, count_gl, per_owner)
    early, landings = slab_waves(early, None, *grid)
    early = exchange(once_after(early, late))
    late = slab_waves(late, landings, *grid)
    late = exchange(once_after(late, early))
    sizes = (devices, x_local, y_local, y_cells, count_gl)
    mixed = mixed_waves(early, green, None, *sizes)
    mixed = mixed_waves(late, green, mixed, *sizes)
    return mixed.reshape(2, 3, planes, y_local, x_cells)


def solution(mesh):
    count_gx, count_gy = mesh.devices.shape
    fine_mesh = jax.sharding.Mesh(
        mesh.devices.reshape(count_gx, 2, 2, count_gy // 4), ("gx", "zh", "zl", "gl")
    )
    every = ("gx", "zh", "zl", "gl")
    in_specs = (
        P(None, None, every, None),
        P(every, None),
        P(every),
        P(every),
        P(None, None, None, every, None),
    )
    out_specs = P(None, None, None, every, None)
    return jax.shard_map(
        per_device, mesh=fine_mesh, in_specs=in_specs, out_specs=out_specs, check_vma=False
    )
```

profile of v0, /device:TPU:0, one launch (start us, length us, event | category | flops | bytes accessed | tf_op | source)
XLA Modules:
  0.0 183.5 jit_solution(9496349633297069249)
XLA Ops:
  0.7 3.9 %shard_map.127.refs_0_ = f32[32,136,128]{2,1,0:T(8,128)} custom-call(s32[1]{0:T(128)S(6)} %copy.21.count, s32[1]{0:T(128)} %bitcast.me, s32[1,512]{1,0:T(1,128)} %bitcast.9, s32[1,512]{1,0:T(1,128)} %bitcast.11, f32[2,3,512,128]{3,2,1,0:T(8,128)} %tiles.3), custom_call_target="tpu_custom_call" | custom-call | flops 1073741824 | bytes 4456448 | tf_op jit(solution)/shard_map/pallas_call | solution.py:186
  4.5 7.3 %all-to-all-start = ((f32[32,136,128]{2,1,0:T(8,128)}), f32[32,136,128]{2,1,0:T(8,128)S(1)}, u32[]{:S(2)}, u32[]{:S(2)}) async-start(f32[32,136,128]{2,1,0:T(8,128)} %shard_map.127.refs_0_), calls=%async_computation | async-start | bytes 4456448 | tf_op jit(solution)/shard_map/all_to_all | solution.py:568
  11.8 2.9 %shard_map.128.data = f32[32,64,128]{2,1,0:T(8,128)} custom-call(s32[1]{0:T(128)S(6)} %copy.21.count, s32[1]{0:T(128)} %bitcast.me, s32[1,512]{1,0:T(1,128)} %bitcast.10, s32[1,512]{1,0:T(1,128)} %bitcast.12, f32[2,3,512,128]{3,2,1,0:T(8,128)} %tiles.3, f32[32,136,128]{2,1,0:T(8,128)} %shard_map.127.refs_0_), custom_call_target="tpu_custom_call" | custom-call | flops 536870912 | bytes 2097152 | tf_op jit(solution)/shard_map/pallas_call | solution.py:186
  14.7 0.0 copy-start.2
  14.8 0.0 copy-start.3
  14.8 50.4 %all-to-all-done.after.data = f32[32,136,128]{2,1,0:T(8,128)S(1)} async-done(((f32[32,136,128]{2,1,0:T(8,128)}), f32[32,136,128]{2,1,0:T(8,128)S(1)}, u32[]{:S(2)}, u32[]{:S(2)}) %all-to-all-start) | async-done | bytes 2228256 | tf_op jit(solution)/shard_map/all_to_all | solution.py:568
  65.1 2.6 %all-to-all-start.1 = ((f32[32,64,128]{2,1,0:T(8,128)}), f32[32,64,128]{2,1,0:T(8,128)S(1)}, u32[]{:S(2)}, u32[]{:S(2)}) async-start(f32[32,64,128]{2,1,0:T(8,128)} %shard_map.129), calls=%async_computation.1 | async-start | bytes 2097152 | tf_op jit(solution)/shard_map/all_to_all | solution.py:568
  67.8 0.0 copy-done.2
  67.8 0.0 copy-done.3
  67.8 5.8 %shard_map.130 = (f32[32,2,64,128]{3,2,1,0:T(8,128)}, s32[1,1024]{1,0:T(1,128)S(1)}) custom-call(f32[256,256]{1,0:T(8,128)S(1)} %copy-done.2, f32[2,16,128]{2,1,0:T(8,128)S(1)} %copy-done.3, f32[32,136,128]{2,1,0:T(8,128)S(1)} %all-to-all-done.after.data), custom_call_target="tpu_custom_call" | custom-call | flops 3221225472 | bytes 4194304 | tf_op jit(solution)/shard_map/pallas_call | solution.py:301
  73.6 0.0 copy-start.4
  73.6 0.6 copy-done.4
  74.2 21.2 %all-to-all-done.1.data.after = f32[32,64,128]{2,1,0:T(8,128)S(1)} async-done(((f32[32,64,128]{2,1,0:T(8,128)}), f32[32,64,128]{2,1,0:T(8,128)S(1)}, u32[]{:S(2)}, u32[]{:S(2)}) %all-to-all-start.1) | async-done | bytes 1048608 | tf_op jit(solution)/shard_map/all_to_all | solution.py:568
  95.4 0.0 copy-start.5
  95.4 2.9 %all-to-all-start.2 = ((f32[32,2,64,128]{3,2,1,0:T(8,128)}), f32[32,2,64,128]{3,2,1,0:T(8,128)S(1)}, u32[]{:S(2)}, u32[]{:S(2)}) async-start(f32[32,2,64,128]{3,2,1,0:T(8,128)} %shard_map.132), calls=%async_computation.2 | async-start | bytes 4194304 | tf_op jit(solution)/shard_map/all_to_all | solution.py:568
  98.2 0.0 copy-done.5
  98.3 3.5 %shard_map.131.data = f32[32,1,64,128]{3,2,1,0:T(8,128)} custom-call(f32[256,256]{1,0:T(8,128)S(1)} %copy-done.2, f32[2,16,128]{2,1,0:T(8,128)S(1)} %copy-done.3, f32[32,64,128]{2,1,0:T(8,128)S(1)} %all-to-all-done.1.data.after, s32[1,1024]{1,0:T(1,128)S(1)} %copy-done.5), custom_call_target="tpu_custom_call" | custom-call | flops 1610612736 | bytes 2097152 | tf_op jit(solution)/shard_map/pallas_call | solution.py:301
  101.7 0.0 copy-start
  101.8 0.0 copy-start.1
  101.8 46.7 %all-to-all-done.2.after.data = f32[32,2,64,128]{3,2,1,0:T(8,128)S(1)} async-done(((f32[32,2,64,128]{3,2,1,0:T(8,128)}), f32[32,2,64,128]{3,2,1,0:T(8,128)S(1)}, u32[]{:S(2)}, u32[]{:S(2)}) %all-to-all-start.2) | async-done | bytes 2097184 | tf_op jit(solution)/shard_map/all_to_all | solution.py:568
  148.4 2.8 %all-to-all-start.3 = ((f32[32,1,64,128]{3,2,1,0:T(8,128)}), f32[32,1,64,128]{3,2,1,0:T(8,128)S(1)}, u32[]{:S(2)}, u32[]{:S(2)}) async-start(f32[32,1,64,128]{3,2,1,0:T(8,128)} %shard_map.133), calls=%async_computation.3 | async-start | bytes 2097152 | tf_op jit(solution)/shard_map/all_to_all | solution.py:568
  151.2 0.0 copy-done
  151.3 0.0 copy-done.1
  151.3 6.1 %shard_map.134.partial = f32[2,3,64,2048]{3,2,1,0:T(8,128)} custom-call(f32[2,32,128]{2,1,0:T(8,128)S(1)} %copy-done.1, f32[256,256]{1,0:T(8,128)S(1)} %copy-done, f32[32,2,64,128]{3,2,1,0:T(8,128)S(1)} %all-to-all-done.2.after.data, f32[2,6,64,2048]{3,2,1,0:T(8,128)} %bitcast.7), custom_call_target="tpu_custom_call" | custom-call | flops 408944640 | bytes 8388608 | tf_op jit(solution)/shard_map/pallas_call | solution.py:524
  157.4 21.3 %all-to-all-done.3.data = f32[32,1,64,128]{3,2,1,0:T(8,128)S(1)} async-done(((f32[32,1,64,128]{3,2,1,0:T(8,128)}), f32[32,1,64,128]{3,2,1,0:T(8,128)S(1)}, u32[]{:S(2)}, u32[]{:S(2)}) %all-to-all-start.3) | async-done | bytes 1048608 | tf_op jit(solution)/shard_map/all_to_all | solution.py:568
  178.7 4.7 %shard_map.135 = f32[2,3,64,2048]{3,2,1,0:T(8,128)} custom-call(f32[2,32,128]{2,1,0:T(8,128)S(1)} %copy-done.1, f32[256,256]{1,0:T(8,128)S(1)} %copy-done, f32[32,1,64,128]{3,2,1,0:T(8,128)S(1)} %all-to-all-done.3.data, f32[2,6,64,2048]{3,2,1,0:T(8,128)} %bitcast.8, f32[2,3,64,2048]{3,2,1,0:T(8,128)} %shard_map.134.partial), custom_call_target="tpu_custom_call" | custom-call | flops 204472320 | bytes 8388608 | tf_op jit(solution)/shard_map/pallas_call | solution.py:524
  (3 shorter events, 0.0 us)
Async XLA Ops:
  4.5 60.6 %all-to-all-start = ((f32[32,136,128]{2,1,0:T(8,128)}), f32[32,136,128]{2,1,0:T(8,128)S(1)}, u32[]{:S(2)}, u32[]{:S(2)}) async-start(f32[32,136,128]{2,1,0:T(8,128)} %shard_map.127.refs_0_), calls=%async_computation | async-start | bytes 4456448 | tf_op jit(solution)/shard_map/all_to_all | solution.py:568
  14.7 53.0 %copy-start.2 = (f32[256,256]{1,0:T(8,128)S(1)}, f32[256,256]{1,0:T(8,128)}, u32[]{:S(2)}) copy-start(f32[256,256]{1,0:T(8,128)} %constant.28.clone.table) | copy-start | bytes 786436
  14.8 53.0 %copy-start.3 = (f32[2,16,128]{2,1,0:T(8,128)S(1)}, f32[2,16,128]{2,1,0:T(8,128)}, u32[]{:S(2)}) copy-start(f32[2,16,128]{2,1,0:T(8,128)} %constant.29.clone.twist) | copy-start | bytes 49156
  65.1 30.2 %all-to-all-start.1 = ((f32[32,64,128]{2,1,0:T(8,128)}), f32[32,64,128]{2,1,0:T(8,128)S(1)}, u32[]{:S(2)}, u32[]{:S(2)}) async-start(f32[32,64,128]{2,1,0:T(8,128)} %shard_map.129), calls=%async_computation.1 | async-start | bytes 2097152 | tf_op jit(solution)/shard_map/all_to_all | solution.py:568
  73.6 0.6 copy-start.4
  95.4 2.9 %copy-start.5 = (s32[1,1024]{1,0:T(1,128)S(1)}, s32[1,1024]{1,0:T(1,128)}, u32[]{:S(2)}) copy-start(s32[1,1024]{1,0:T(1,128)} %copy-done.4) | copy-start | bytes 12292
  95.4 53.0 %all-to-all-start.2 = ((f32[32,2,64,128]{3,2,1,0:T(8,128)}), f32[32,2,64,128]{3,2,1,0:T(8,128)S(1)}, u32[]{:S(2)}, u32[]{:S(2)}) async-start(f32[32,2,64,128]{3,2,1,0:T(8,128)} %shard_map.132), calls=%async_computation.2 | async-start | bytes 4194304 | tf_op jit(solution)/shard_map/all_to_all | solution.py:568
  101.7 49.5 %copy-start = (f32[256,256]{1,0:T(8,128)S(1)}, f32[256,256]{1,0:T(8,128)}, u32[]{:S(2)}) copy-start(f32[256,256]{1,0:T(8,128)} %constant.31.clone.table) | copy-start | bytes 786436
  101.8 49.5 %copy-start.1 = (f32[2,32,128]{2,1,0:T(8,128)S(1)}, f32[2,32,128]{2,1,0:T(8,128)}, u32[]{:S(2)}) copy-start(f32[2,32,128]{2,1,0:T(8,128)} %constant.30.clone.twist) | copy-start | bytes 98308
  148.4 30.2 %all-to-all-start.3 = ((f32[32,1,64,128]{3,2,1,0:T(8,128)}), f32[32,1,64,128]{3,2,1,0:T(8,128)S(1)}, u32[]{:S(2)}, u32[]{:S(2)}) async-start(f32[32,1,64,128]{3,2,1,0:T(8,128)} %shard_map.133), calls=%async_computation.3 | async-start | bytes 2097152 | tf_op jit(solution)/shard_map/all_to_all | solution.py:568
where the time goes:
time: 184 us
  waiting for transfers between devices  139 us (76%)
  Pallas kernels  26.9 us (15%)
  starting transfers between devices  15.6 us (8%)
    all_to_all x4, waiting for transfers between devices, exchange(): return lax.all_to_all(data, places, split_axis=0, concat_axis=0, tiled=True)  139 us
    all_to_all x4, starting transfers between devices, exchange(): return lax.all_to_all(data, places, split_axis=0, concat_axis=0, tiled=True)  15.6 us
    pallas_call x2, Pallas kernels, mixed_waves(): pl.pallas_call(functools.partial(early_kernel if first else last_kernel,...  10.8 us
    pallas_call x2, Pallas kernels, slab_waves(): pl.pallas_call(functools.partial(slab_kernel, count, x_local, blocks, per...  9.25 us
    pallas_call x2, Pallas kernels, pack(): pl.pallas_call(functools.partial(pack_kernel, devices, count_gl, per_owne...  6.76 us
  transfers between devices with their start and end apart: 4, of which 4 were waited for; matrix products, arithmetic and copies ran while one was open for 0% of the time, Pallas kernels for 10%

commit v1 on v0

--- a/solution.py
+++ b/solution.py
@@ -102,7 +102,7 @@
 
 def place_of(owner, count_gl):
     shift = count_gl.bit_length() - 1
-    z = ((owner >> shift) & 1) * 2 + ((owner >> (shift + 1)) & 1)
+    z = (owner >> shift) & 3
     return (((owner >> (shift + 2)) << shift) + (owner & (count_gl - 1))) * 4 + z
 
 
@@ -114,9 +114,10 @@
 
 
 def pack_kernel(
-    devices, count_gl, per_owner, comps, with_slots, count, me, owner_row, slot_row, tiles, *refs
+    devices, count_gl, per_owner, count, me, owner_row, slot_row, tiles, out, *scratch
 ):
-    out, held, made, lists, sems, out_sems = refs[-6:]
+    held, made, lists, sems, out_sems = scratch
+    comps = range(tiles.shape[1])
     listed = owner_row.shape[1]
     fetches = [
         pltpu.make_async_copy(owner_row, lists.at[0], sems.at[0]),
@@ -152,17 +153,16 @@
         copy.start()
         sends.append(copy)
 
-    if with_slots:
-        stated = lists[1] + 1
-        lane = rank + (me[0] & (128 // per_owner - 1)) * per_owner
-        lane_at = lax.broadcasted_iota(jnp.int32, (128, listed), 0)
-        laned = jnp.where(lane_at == lane, 1.0, 0.0).astype(jnp.bfloat16)
-        coarse = (named * (stated >> 5).astype(jnp.float32)).astype(jnp.bfloat16)
-        fine = (named * (stated & 31).astype(jnp.float32)).astype(jnp.bfloat16)
-        slots = 32.0 * dot_rows(coarse, laned) + dot_rows(fine, laned)
-        start = 2 * len(comps) * per_owner
-        made[:, start:, :] = jnp.broadcast_to(slots[:, None, :], (devices, 8, 128))
-        send(start, 8)
+    stated = lists[1] + 1
+    lane = rank + (me[0] & (128 // per_owner - 1)) * per_owner
+    lane_at = lax.broadcasted_iota(jnp.int32, (128, listed), 0)
+    laned = jnp.where(lane_at == lane, 1.0, 0.0).astype(jnp.bfloat16)
+    coarse = (named * (stated >> 5).astype(jnp.float32)).astype(jnp.bfloat16)
+    fine = (named * (stated & 31).astype(jnp.float32)).astype(jnp.bfloat16)
+    slots = 32.0 * dot_rows(coarse, laned) + dot_rows(fine, laned)
+    start = 2 * len(comps) * per_owner
+    made[:, start:, :] = jnp.broadcast_to(slots[:, None, :], (devices, 8, 128))
+    send(start, 8)
     for i in range(len(comps)):
         fetches[2 + i].wait()
         parts = [part for r in range(2) for part in split_two(held[i, r])]
@@ -178,29 +178,27 @@
         copy.wait()
 
 
-def pack(tiles, comps, owner_row, slot_row, count, me, after, devices, count_gl, per_owner):
-    listed = tiles.shape[2]
-    with_slots = after is None
-    rows = 2 * len(comps) * per_owner + (8 if with_slots else 0)
-    extra = () if with_slots else (after,)
+def pack(tiles, owner_row, slot_row, count, me, devices, count_gl, per_owner):
+    comps, listed = tiles.shape[1:3]
+    rows = 2 * comps * per_owner + 8
     return pl.pallas_call(
-        functools.partial(pack_kernel, devices, count_gl, per_owner, comps, with_slots),
+        functools.partial(pack_kernel, devices, count_gl, per_owner),
         out_shape=pltpu.HBM((devices, rows, 128), jnp.float32),
         in_specs=[pl.BlockSpec(memory_space=pltpu.SMEM)] * 2
-        + [pl.BlockSpec(memory_space=pltpu.HBM)] * (3 + len(extra)),
+        + [pl.BlockSpec(memory_space=pltpu.HBM)] * 3,
         out_specs=pl.BlockSpec(memory_space=pltpu.HBM),
         scratch_shapes=[
-            pltpu.VMEM((len(comps), 2, listed, 128), jnp.float32),
+            pltpu.VMEM((comps, 2, listed, 128), jnp.float32),
             pltpu.VMEM((devices, rows, 128), jnp.float32),
             pltpu.VMEM((2, 1, listed), jnp.int32),
-            pltpu.SemaphoreType.DMA((2 + len(comps),)),
-            pltpu.SemaphoreType.DMA((1 + 2 * len(comps),)),
+            pltpu.SemaphoreType.DMA((2 + comps,)),
+            pltpu.SemaphoreType.DMA((1 + 2 * comps,)),
         ],
         compiler_params=params(24),
         cost_estimate=cost(
-            devices * per_owner * listed * 512 * 2 * len(comps), devices * rows * 1024
+            devices * per_owner * listed * 512 * 2 * comps, devices * rows * 1024
         ),
-    )(count, me, *[in_hbm(a) for a in (owner_row, slot_row, tiles, *extra)])
+    )(count, me, *[in_hbm(a) for a in (owner_row, slot_row, tiles)])
 
 
 def complex_table(cos_part, sin_part):
@@ -212,38 +210,32 @@
     ).astype(np.float32)
 
 
-def slab_kernel(count, x_local, blocks, per_owner, first, table, twist, data, *refs):
-    if first:
-        out, landings, made, slab, turned, out_sems = refs
-    else:
-        landings, out, made, slab, turned, out_sems = refs
+def slab_kernel(count, x_local, blocks, per_owner, table, twist, data, out, *scratch):
+    made, slab, turned, out_sems = scratch
     devices = data.shape[0]
     entries = devices * per_owner
     group = 128 // x_local
     pairs = blocks // group
     shift = blocks.bit_length() - 1
-    if first:
-        every = 128 // per_owner
-        stated = [
-            sum([data[o, data.shape[1] - 8 :][:1] for o in range(start, start + every)])
-            for start in range(0, devices, every)
-        ]
-        slot = jnp.concatenate(stated, axis=1).astype(jnp.int32) - 1
-        landing = jnp.where(slot >= 0, (slot & (blocks - 1)) * x_local + (slot >> shift), -1)
-        landings[...] = landing
-    else:
-        landing = landings[...]
+    every = 128 // per_owner
+    stated = [
+        sum([data[o, data.shape[1] - 8 :][:1] for o in range(start, start + every)])
+        for start in range(0, devices, every)
+    ]
+    slot = jnp.concatenate(stated, axis=1).astype(jnp.int32) - 1
+    landing = jnp.where(slot >= 0, (slot & (blocks - 1)) * x_local + (slot >> shift), -1)
     parts = []
     for i in range(2 * count):
         one = data[:, i * per_owner : (i + 1) * per_owner, :]
         parts.extend(split_two(one.reshape(entries, 128)))
     parts = jnp.concatenate(parts, axis=1)
-    for start in range(0, blocks * x_local, 256):
-        place = start + lax.broadcasted_iota(jnp.int32, (256, entries), 0)
+    step_rows = min(512, blocks * x_local)
+    for start in range(0, blocks * x_local, step_rows):
+        place = start + lax.broadcasted_iota(jnp.int32, (step_rows, entries), 0)
         chosen = jnp.where(place == landing, 1.0, 0.0).astype(jnp.bfloat16)
         got = jnp.dot(chosen, parts, preferred_element_type=jnp.float32)
         for i in range(2 * count):
-            slab[i // 2, i % 2, start : start + 256, :] = (
+            slab[i // 2, i % 2, start : start + step_rows, :] = (
                 got[:, 256 * i : 256 * i + 128] + got[:, 256 * i + 128 : 256 * i + 256]
             )
     sends = []
@@ -283,10 +275,9 @@
         send.wait()
 
 
-def slab_waves(data, landings, x_local, blocks, count_gl, per_owner):
+def slab_waves(data, x_local, blocks, count_gl, per_owner):
     devices = data.shape[0]
     count = data.shape[1] // (2 * per_owner)
-    first = landings is None
     fine = angles(128, 128, 128)
     order = owner_order(devices, count_gl)
     fine = fine.reshape(devices, 128 // devices, 128)[order].reshape(128, 128)
@@ -295,30 +286,23 @@
     twist = np.stack([np.cos(twist_angle), np.sin(twist_angle)]).astype(np.float32)
     entries = devices * per_owner
     rows = blocks * x_local * 2
-    out = pltpu.HBM((devices, count, rows // devices, 128), jnp.float32)
-    landing = jax.ShapeDtypeStruct((1, entries), jnp.int32)
-    in_place = pl.BlockSpec(memory_space=pltpu.VMEM)
     return pl.pallas_call(
-        functools.partial(slab_kernel, count, x_local, blocks, per_owner, first),
-        out_shape=(out, landing) if first else out,
-        in_specs=[in_place] * (3 if first else 4),
-        out_specs=(
-            (pl.BlockSpec(memory_space=pltpu.HBM), in_place)
-            if first
-            else pl.BlockSpec(memory_space=pltpu.HBM)
-        ),
+        functools.partial(slab_kernel, count, x_local, blocks, per_owner),
+        out_shape=pltpu.HBM((devices, count, rows // devices, 128), jnp.float32),
+        in_specs=[pl.BlockSpec(memory_space=pltpu.VMEM)] * 3,
+        out_specs=pl.BlockSpec(memory_space=pltpu.HBM),
         scratch_shapes=[
             pltpu.VMEM((count, rows, 128), jnp.float32),
             pltpu.VMEM((count, 2, blocks * x_local, 128), jnp.float32),
             pltpu.VMEM((blocks * x_local, 256), jnp.float32),
             pltpu.SemaphoreType.DMA((count,)),
         ],
-        compiler_params=params(24),
+        compiler_params=params(40),
         cost_estimate=cost(
             count * blocks * x_local * (entries * 1024 + 512 * 1024),
             count * (entries * 1024 + rows * 512),
         ),
-    )(jnp.asarray(table), jnp.asarray(twist), in_vmem(data), *(() if first else (landings,)))
+    )(jnp.asarray(table), jnp.asarray(twist), in_vmem(data))
 
 
 def choose(options, mask_of):
@@ -329,7 +313,7 @@
 
 
 def x_steps(
-    devices, x_local, y_local, blocks, order, index, twist, table, data, turned, columns, store
+    devices, x_local, y_local, blocks, order, index, twist, table, data, turned, columns, store, whole
 ):
     group = 128 // x_local
     pairs = blocks // group
@@ -391,99 +375,61 @@
             for step in range(kept):
                 row = step * blocks + (bank % group) * pairs
                 store(bank // group, row, start, one[step * pairs : (step + 1) * pairs])
-
-
-def mix_rows(rows, columns, tensor, waves, sums, terms):
-    for row, entry, wave in terms:
-        green_real, green_imag = tensor[entry, 0, rows, columns], tensor[entry, 1, rows, columns]
-        real, imag = waves[wave][0, rows, columns], waves[wave][1, rows, columns]
-        real_term = green_real * real - green_imag * imag
-        imag_term = green_real * imag + green_imag * real
-        old = sums[row]
-        sums[row] = (
-            (real_term, imag_term) if old is None else (old[0] + real_term, old[1] + imag_term)
-        )
+        whole(start)
+
+
+def mix_rows(rows, columns, tensor, waves):
+    sums = [None] * 3
+    for row in range(3):
+        for col in range(3):
+            entry = pair_index[row][col]
+            green_real, green_imag = tensor[0, entry, rows, columns], tensor[1, entry, rows, columns]
+            real, imag = waves[col, 0, rows, columns], waves[col, 1, rows, columns]
+            real_term = green_real * real - green_imag * imag
+            imag_term = green_real * imag + green_imag * real
+            old = sums[row]
+            sums[row] = (
+                (real_term, imag_term) if old is None else (old[0] + real_term, old[1] + imag_term)
+            )
     return sums
 
 
-def mix_pieces(y_local, width, made, out, out_sems, sums_of):
+def field_kernel(sizes, twist, table, data, green, out, *scratch):
+    y_local, x_cells = green.shape[2:]
+    turned, columns, tensor, kept, made, in_sem, out_sems = scratch
+    width = x_cells // made.shape[0]
+    fetch = pltpu.make_async_copy(green, tensor, in_sem)
+    fetch.start()
     sends = []
-    for piece in range(made.shape[0]):
-        columns = pl.ds(piece * width, width)
-
-        @pl.loop(0, y_local // 8)
-        def _(step):
-            rows = pl.ds(pl.multiple_of(step * 8, 8), 8)
-            for row, pair in enumerate(sums_of(rows, columns)):
-                for r in range(2):
-                    made[piece, r, row, rows, :] = pair[r]
-
-        send = pltpu.make_async_copy(
-            made.at[piece], out.at[:, :, :, columns], out_sems.at[piece]
-        )
-        send.start()
-        sends.append(send)
+    for comp in range(3):
+
+        def store(r, row, start, block):
+            kept[comp, r, row : row + block.shape[0], start : start + 128] = block
+
+        def whole(start):
+            if comp < 2 or (start + 128) % width:
+                return
+            piece = start // width
+            part = pl.ds(piece * width, width)
+
+            @pl.loop(0, y_local // 8)
+            def _(step):
+                rows = pl.ds(pl.multiple_of(step * 8, 8), 8)
+                for row, pair in enumerate(mix_rows(rows, part, tensor, kept)):
+                    for r in range(2):
+                        made[piece, r, row, rows, :] = pair[r]
+
+            send = pltpu.make_async_copy(
+                made.at[piece], out.at[:, :, :, part], out_sems.at[piece]
+            )
+            send.start()
+            sends.append(send)
+
+        if comp == 2:
+            fetch.wait()
+        x_steps(*sizes, comp, twist, table, data, turned, columns, store, whole)
     for send in sends:
         send.wait()
-
-
-def fetch_entries(green, tensor, entries, sems):
-    fetches = [
-        pltpu.make_async_copy(green.at[:, entry], tensor.at[i], sems.at[i])
-        for i, entry in enumerate(entries)
-    ]
-    for fetch in fetches:
-        fetch.start()
-    return fetches
-
-
-early_entries, late_entries = (0, 1, 3, 4, 5), (4, 5, 2)
-
-
-def early_kernel(sizes, twist, table, data, green, out, *scratch):
-    y_local, x_cells = green.shape[2:]
-    turned, columns, tensor, kept, made, in_sems, out_sems = scratch
-    fetches = fetch_entries(green, tensor, early_entries, in_sems)
-    for comp in range(2):
-
-        def store(r, row, start, block):
-            kept[comp, r, row : row + block.shape[0], start : start + 128] = block
-
-        x_steps(*sizes, comp, twist, table, data, turned, columns, store)
-    for fetch in fetches:
-        fetch.wait()
-    terms = [
-        (row, early_entries.index(pair_index[row][comp]), comp)
-        for row in range(3)
-        for comp in range(2)
-    ]
-    waves = [kept.at[0], kept.at[1]]
-
-    def sums_of(rows, columns):
-        return mix_rows(rows, columns, tensor, waves, [None] * 3, terms)
-
-    mix_pieces(y_local, x_cells // made.shape[0], made, out, out_sems, sums_of)
-
-
-def last_kernel(sizes, twist, table, data, green, partial, out, *scratch):
-    y_local, x_cells = green.shape[2:]
-    turned, columns, tensor, kept, held, made, in_sems, out_sems = scratch
-    fetches = fetch_entries(green, tensor, late_entries, in_sems)
-    fetches.append(pltpu.make_async_copy(partial, held, in_sems.at[len(late_entries)]))
-    fetches[-1].start()
-
-    def store(r, row, start, block):
-        kept[r, row : row + block.shape[0], start : start + 128] = block
-
-    x_steps(*sizes, 0, twist, table, data, turned, columns, store)
-    for fetch in fetches:
-        fetch.wait()
-
-    def sums_of(rows, columns):
-        sums = [(held[0, row, rows, columns], held[1, row, rows, columns]) for row in range(3)]
-        return mix_rows(rows, columns, tensor, [kept], sums, [(row, row, 0) for row in range(3)])
-
-    mix_pieces(y_local, x_cells // made.shape[0], made, out, out_sems, sums_of)
 
 
 def x_tables(devices, x_local, y_cells):
@@ -505,63 +451,31 @@
     ]
 
 
-def mixed_waves(data, green, partial, devices, x_local, y_local, y_cells, count_gl):
+def field(data, green, devices, x_local, y_local, y_cells, count_gl):
     x_cells = devices * x_local
     pieces = 8
     sizes = (devices, x_local, y_local, y_cells // 128, owner_order(devices, count_gl))
-    first = partial is None
-    comps, entries = (2, 5) if first else (1, 3)
     plane = (y_local, x_cells)
-    held = [pltpu.VMEM((entries, 2) + plane, jnp.float32)]
-    if first:
-        held += [pltpu.VMEM((2, 2) + plane, jnp.float32)]
-    else:
-        held += [
-            pltpu.VMEM((2,) + plane, jnp.float32),
-            pltpu.VMEM((2, 3) + plane, jnp.float32),
-        ]
-    operands = (green,) if first else (green, partial)
     return pl.pallas_call(
-        functools.partial(early_kernel if first else last_kernel, sizes),
+        functools.partial(field_kernel, sizes),
         out_shape=pltpu.HBM((2, 3) + plane, jnp.float32),
         in_specs=[pl.BlockSpec(memory_space=pltpu.VMEM)] * 3
-        + [pl.BlockSpec(memory_space=pltpu.HBM)] * len(operands),
+        + [pl.BlockSpec(memory_space=pltpu.HBM)],
         out_specs=pl.BlockSpec(memory_space=pltpu.HBM),
         scratch_shapes=x_scratch(devices, x_local, y_local)
-        + held
         + [
+            pltpu.VMEM((2, 6) + plane, jnp.float32),
+            pltpu.VMEM((3, 2) + plane, jnp.float32),
             pltpu.VMEM((pieces, 2, 3, y_local, x_cells // pieces), jnp.float32),
-            pltpu.SemaphoreType.DMA((5,)),
+            pltpu.SemaphoreType.DMA(()),
             pltpu.SemaphoreType.DMA((pieces,)),
         ],
         compiler_params=params(40),
-        cost_estimate=cost(
-            comps * x_cells * y_local * (x_local * 24 + 24), x_cells * y_local * 64
-        ),
-    )(
-        *x_tables(devices, x_local, y_cells),
-        in_vmem(data),
-        *[in_hbm(a) for a in operands],
-    )
-
-
-def gate_kernel(data, after, out):
-    del data, after, out
-
-
-def once_after(data, after):
-    return pl.pallas_call(
-        gate_kernel,
-        out_shape=pltpu.HBM(data.shape, data.dtype),
-        in_specs=[pl.BlockSpec(memory_space=pltpu.HBM), pl.BlockSpec(memory_space=pl.ANY)],
-        out_specs=pl.BlockSpec(memory_space=pltpu.HBM),
-        input_output_aliases={0: 0},
-        compiler_params=params(1),
-        cost_estimate=cost(0, 0),
-    )(in_hbm(data), after)
-
-
-places = ("gx", "gl", "zl", "zh")
+        cost_estimate=cost(3 * x_cells * y_local * (x_local * 24 + 24), x_cells * y_local * 96),
+    )(*x_tables(devices, x_local, y_cells), in_vmem(data), in_hbm(green))
+
+
+places = ("gx", "gl", "gz")
 
 
 def exchange(data):
@@ -582,27 +496,18 @@
     green = green.reshape(2, 6, y_local, x_cells)
     me = lax.axis_index(places).reshape(1).astype(jnp.int32)
     lists = (owner_row, slot_row, tile_count, me)
-    early = pack(tiles, (0, 1), *lists, None, devices, count_gl, per_owner)
-    late = pack(tiles, (2,), *lists, early, devices, count_gl, per_owner)
-    early = exchange(early)
-    late = exchange(once_after(late, early))
-    grid = (x_local, blocks, count_gl, per_owner)
-    early, landings = slab_waves(early, None, *grid)
-    early = exchange(once_after(early, late))
-    late = slab_waves(late, landings, *grid)
-    late = exchange(once_after(late, early))
-    sizes = (devices, x_local, y_local, y_cells, count_gl)
-    mixed = mixed_waves(early, green, None, *sizes)
-    mixed = mixed_waves(late, green, mixed, *sizes)
+    arrived = exchange(pack(tiles, *lists, devices, count_gl, per_owner))
+    moved = exchange(slab_waves(arrived, x_local, blocks, count_gl, per_owner))
+    mixed = field(moved, green, devices, x_local, y_local, y_cells, count_gl)
     return mixed.reshape(2, 3, planes, y_local, x_cells)
 
 
 def solution(mesh):
     count_gx, count_gy = mesh.devices.shape
     fine_mesh = jax.sharding.Mesh(
-        mesh.devices.reshape(count_gx, 2, 2, count_gy // 4), ("gx", "zh", "zl", "gl")
+        mesh.devices.reshape(count_gx, 4, count_gy // 4), ("gx", "gz", "gl")
     )
-    every = ("gx", "zh", "zl", "gl")
+    every = ("gx", "gz", "gl")
     in_specs = (
         P(None, None, every, None),
         P(every, None),

time: 184 us -> 180 us (0.978)
  blocking collectives: 0 us -> 158 us
  waiting for transfers between devices: 139 us -> 0 us
  starting transfers between devices: 15.6 us -> 0 us
  Pallas kernels: 26.9 us -> 21.7 us
    all_to_all x0 -> x2, blocking collectives: none -> 158 us  [exchange(): return lax.all_to_all(data, places, split_axis=0, concat_axis=0, tiled=True)]
    all_to_all x4 -> x0, waiting for transfers between devices: 139 us -> none  [exchange(): return lax.all_to_all(data, places, split_axis=0, concat_axis=0, tiled=True)]
    all_to_all x4 -> x0, starting transfers between devices: 15.6 us -> none  [exchange(): return lax.all_to_all(data, places, split_axis=0, concat_axis=0, tiled=True)]
    pallas_call x2 -> x1, Pallas kernels: 6.76 us -> 4.69 us  [pack(): pl.pallas_call(functools.partial(pack_kernel, devices, count_gl, per_owne...]
    pallas_call x5 -> x1, Pallas kernels: 10.8 us -> 8.91 us  [field(): pl.pallas_call(functools.partial(field_kernel, sizes), out_shape=pltpu.HB...]
    pallas_call x2 -> x1, Pallas kernels: 9.25 us -> 8.06 us  [slab_waves(): pl.pallas_call(functools.partial(slab_kernel, count, x_local, blocks, per...]
  transfers between devices with their start and end apart: 4 -> 0, of which waited for: 4 -> 0; matrix products, arithmetic and copies ran while one was open for 0% -> 0% of each run, Pallas kernels for 10% -> 0%
where the time goes in v1:
time: 180 us
  blocking collectives  158 us (88%)
  Pallas kernels  21.7 us (12%)
    all_to_all x2, blocking collectives, exchange(): return lax.all_to_all(data, places, split_axis=0, concat_axis=0, tiled=True)  158 us
    pallas_call x1, Pallas kernels, field(): pl.pallas_call(functools.partial(field_kernel, sizes), out_shape=pltpu.HB...  8.91 us
    pallas_call x1, Pallas kernels, slab_waves(): pl.pallas_call(functools.partial(slab_kernel, count, x_local, blocks, per...  8.06 us
    pallas_call x1, Pallas kernels, pack(): pl.pallas_call(functools.partial(pack_kernel, devices, count_gl, per_owne...  4.69 us

profile of v1, /device:TPU:0, one launch (start us, length us, event | category | flops | bytes accessed | tf_op | source)
XLA Modules:
  0.0 180.1 jit_solution(303469300575229060)
XLA Ops:
  0.7 4.7 %shard_map.91 = f32[32,200,128]{2,1,0:T(8,128)} custom-call(s32[1]{0:T(128)S(6)} %copy.11.count, s32[1]{0:T(128)} %bitcast.me, s32[1,512]{1,0:T(1,128)} %bitcast.8, s32[1,512]{1,0:T(1,128)} %bitcast.9, f32[2,3,512,128]{3,2,1,0:T(8,128)} %tiles.1), custom_call_target="tpu_custom_call" | custom-call | flops 1610612736 | bytes 6553600 | tf_op jit(solution)/shard_map/pallas_call | solution.py:184
  5.4 0.0 copy-start.2
  5.4 0.0 copy-start.3
  5.4 82.9 %all_to_all.10.data = f32[32,200,128]{2,1,0:T(8,128)S(1)} all-to-all(f32[32,200,128]{2,1,0:T(8,128)} %shard_map.91), channel_id=1, replica_groups=mesh['gx'=4,'gz'=4,'gl'=2] {'gx','gl','gz'}, dimensions={0} | all-to-all | bytes 6553600 | tf_op jit(solution)/shard_map/all_to_all | solution.py:482
  88.3 0.0 copy-done.2
  88.3 0.0 copy-done.3
  88.3 8.1 %shard_map.92 = f32[32,3,64,128]{3,2,1,0:T(8,128)} custom-call(f32[256,256]{1,0:T(8,128)S(1)} %copy-done.2, f32[2,16,128]{2,1,0:T(8,128)S(1)} %copy-done.3, f32[32,200,128]{2,1,0:T(8,128)S(1)} %all_to_all.10.data), custom_call_target="tpu_custom_call" | custom-call | flops 4831838208 | bytes 6291456 | tf_op jit(solution)/shard_map/pallas_call | solution.py:289
  96.4 0.0 copy-start
  96.4 0.0 copy-start.1
  96.4 74.7 %all_to_all.11.data = f32[32,3,64,128]{3,2,1,0:T(8,128)S(1)} all-to-all(f32[32,3,64,128]{3,2,1,0:T(8,128)} %shard_map.92), channel_id=1, replica_groups=mesh['gx'=4,'gz'=4,'gl'=2] {'gx','gl','gz'}, dimensions={0} | all-to-all | bytes 6291456 | tf_op jit(solution)/shard_map/all_to_all | solution.py:482
  171.0 0.0 copy-done
  171.0 0.0 copy-done.1
  171.0 8.9 %shard_map.93 = f32[2,3,64,2048]{3,2,1,0:T(8,128)} custom-call(f32[2,32,128]{2,1,0:T(8,128)S(1)} %copy-done.1, f32[256,256]{1,0:T(8,128)S(1)} %copy-done, f32[32,3,64,128]{3,2,1,0:T(8,128)S(1)} %all_to_all.11.data, f32[2,6,64,2048]{3,2,1,0:T(8,128)} %bitcast.7), custom_call_target="tpu_custom_call" | custom-call | flops 613416960 | bytes 12582912 | tf_op jit(solution)/shard_map/pallas_call | solution.py:459
Async XLA Ops:
  5.4 82.9 %copy-start.2 = (f32[256,256]{1,0:T(8,128)S(1)}, f32[256,256]{1,0:T(8,128)}, u32[]{:S(2)}) copy-start(f32[256,256]{1,0:T(8,128)} %constant.23.clone.table) | copy-start | bytes 786436
  5.4 82.9 %copy-start.3 = (f32[2,16,128]{2,1,0:T(8,128)S(1)}, f32[2,16,128]{2,1,0:T(8,128)}, u32[]{:S(2)}) copy-start(f32[2,16,128]{2,1,0:T(8,128)} %constant.24.clone.twist) | copy-start | bytes 49156
  96.4 74.7 %copy-start = (f32[256,256]{1,0:T(8,128)S(1)}, f32[256,256]{1,0:T(8,128)}, u32[]{:S(2)}) copy-start(f32[256,256]{1,0:T(8,128)} %constant.26.clone.table) | copy-start | bytes 786436
  96.4 74.7 %copy-start.1 = (f32[2,32,128]{2,1,0:T(8,128)S(1)}, f32[2,32,128]{2,1,0:T(8,128)}, u32[]{:S(2)}) copy-start(f32[2,32,128]{2,1,0:T(8,128)} %constant.25.clone.twist) | copy-start | bytes 98308

commit v2 on v1

--- a/solution.py
+++ b/solution.py
@@ -3,7 +3,6 @@
 
 import jax
 import jax.numpy as jnp
-import ml_dtypes
 import numpy as np
 from jax import lax
 from jax.experimental import pallas as pl
@@ -35,44 +34,24 @@
     return 2.0 * math.pi / length * products
 
 
-def halves(table):
-    wide = np.asarray(table, np.float32)
-    high = wide.astype(ml_dtypes.bfloat16)
-    low = (wide - high.astype(np.float32)).astype(ml_dtypes.bfloat16)
-    return jnp.asarray(high), jnp.asarray(low)
-
-
 def split_two(data):
     high = data.astype(jnp.bfloat16)
     return high, (data - high.astype(jnp.float32)).astype(jnp.bfloat16)
 
 
-def split_three(data):
-    high = data.astype(jnp.bfloat16)
-    rest = data - high.astype(jnp.float32)
-    middle = rest.astype(jnp.bfloat16)
-    return high, middle, (rest - middle.astype(jnp.float32)).astype(jnp.bfloat16)
-
-
 def dot_rows(left, right):
     return lax.dot_general(left, right, by_rows, preferred_element_type=jnp.float32)
 
 
-def dot_rows_split(table, data):
-    rows, depth = table.shape
-    table_high, table_low = split_two(table)
+def dot_rows_split(stacked, data):
+    rows = stacked.shape[0] // 2
     high, low = split_two(data)
-    if depth > 128:
-        both = dot_rows(jnp.concatenate([table_high, table_low]), high)
-        return both[:rows] + both[rows:] + dot_rows(table_high, low)
-    left = jnp.concatenate(
-        [
-            jnp.concatenate([table_high, table_high], axis=1),
-            jnp.concatenate([table_low, jnp.zeros_like(table_low)], axis=1),
-        ]
-    )
-    both = dot_rows(left, jnp.concatenate([high, low], axis=1))
-    return both[:rows] + both[rows:]
+    both = dot_rows(stacked, high)
+    return both[:rows] + both[rows:] + dot_rows(stacked[:rows], low)
+
+
+def stacked_halves(table):
+    return jnp.concatenate(split_two(table[...]))
 
 
 def flat_fft(values, times):
@@ -116,7 +95,7 @@
 def pack_kernel(
     devices, count_gl, per_owner, count, me, owner_row, slot_row, tiles, out, *scratch
 ):
-    held, made, lists, sems, out_sems = scratch
+    held, lists, sems = scratch
     comps = range(tiles.shape[1])
     listed = owner_row.shape[1]
     fetches = [
@@ -143,16 +122,6 @@
     target_at = lax.broadcasted_iota(jnp.int32, (devices * per_owner, listed), 0)
     chosen = jnp.where(target_at == target, 1.0, 0.0).astype(jnp.bfloat16)
     fetches[1].wait()
-    sends = []
-
-    def send(start, rows):
-        part = pl.ds(start, rows)
-        copy = pltpu.make_async_copy(
-            made.at[:, part], out.at[:, part], out_sems.at[len(sends)]
-        )
-        copy.start()
-        sends.append(copy)
-
     stated = lists[1] + 1
     lane = rank + (me[0] & (128 // per_owner - 1)) * per_owner
     lane_at = lax.broadcasted_iota(jnp.int32, (128, listed), 0)
@@ -161,8 +130,7 @@
     fine = (named * (stated & 31).astype(jnp.float32)).astype(jnp.bfloat16)
     slots = 32.0 * dot_rows(coarse, laned) + dot_rows(fine, laned)
     start = 2 * len(comps) * per_owner
-    made[:, start:, :] = jnp.broadcast_to(slots[:, None, :], (devices, 8, 128))
-    send(start, 8)
+    out[:, start:, :] = jnp.broadcast_to(slots[:, None, :], (devices, 8, 128))
     for i in range(len(comps)):
         fetches[2 + i].wait()
         parts = [part for r in range(2) for part in split_two(held[i, r])]
@@ -172,10 +140,7 @@
         for r in range(2):
             whole = got[:, 256 * r : 256 * r + 128] + got[:, 256 * r + 128 : 256 * r + 256]
             start = (2 * i + r) * per_owner
-            made[:, start : start + per_owner, :] = whole.reshape(devices, per_owner, 128)
-            send(start, per_owner)
-    for copy in sends:
-        copy.wait()
+            out[:, start : start + per_owner, :] = whole.reshape(devices, per_owner, 128)
 
 
 def pack(tiles, owner_row, slot_row, count, me, devices, count_gl, per_owner):
@@ -183,16 +148,14 @@
     rows = 2 * comps * per_owner + 8
     return pl.pallas_call(
         functools.partial(pack_kernel, devices, count_gl, per_owner),
-        out_shape=pltpu.HBM((devices, rows, 128), jnp.float32),
+        out_shape=pltpu.VMEM((devices, rows, 128), jnp.float32),
         in_specs=[pl.BlockSpec(memory_space=pltpu.SMEM)] * 2
         + [pl.BlockSpec(memory_space=pltpu.HBM)] * 3,
-        out_specs=pl.BlockSpec(memory_space=pltpu.HBM),
+        out_specs=pl.BlockSpec(memory_space=pltpu.VMEM),
         scratch_shapes=[
             pltpu.VMEM((comps, 2, listed, 128), jnp.float32),
-            pltpu.VMEM((devices, rows, 128), jnp.float32),
             pltpu.VMEM((2, 1, listed), jnp.int32),
             pltpu.SemaphoreType.DMA((2 + comps,)),
-            pltpu.SemaphoreType.DMA((1 + 2 * comps,)),
         ],
         compiler_params=params(24),
         cost_estimate=cost(
@@ -211,7 +174,7 @@
 
 
 def slab_kernel(count, x_local, blocks, per_owner, table, twist, data, out, *scratch):
-    made, slab, turned, out_sems = scratch
+    slab, turned = scratch
     devices = data.shape[0]
     entries = devices * per_owner
     group = 128 // x_local
@@ -238,10 +201,10 @@
             slab[i // 2, i % 2, start : start + step_rows, :] = (
                 got[:, 256 * i : 256 * i + 128] + got[:, 256 * i + 128 : 256 * i + 256]
             )
-    sends = []
+    stacked = stacked_halves(table)
     for index in range(count):
 
-        @pl.loop(0, x_local // 8)
+        @pl.loop(0, x_local // 8, unroll=2)
         def _(step):
             at = pl.multiple_of(step * 8, 8)
             values = [
@@ -257,22 +220,12 @@
                 turned[rows, 128:] = imag * cos_k - real * sin_k
 
         for start in range(0, pairs, 2):
-            moved = dot_rows_split(table[...], turned[start * 128 : (start + 2) * 128, :])
+            moved = dot_rows_split(stacked, turned[start * 128 : (start + 2) * 128, :])
             for k in range(2):
                 for r in range(2):
-                    rows = pl.ds(r * pairs + start + k, 128, stride=2 * pairs)
-                    made[index, rows, :] = moved[
-                        r * 128 : (r + 1) * 128, k * 128 : (k + 1) * 128
-                    ]
-        send = pltpu.make_async_copy(
-            made.at[index].reshape(devices, made.shape[1] // devices, 128),
-            out.at[:, index],
-            out_sems.at[index],
-        )
-        send.start()
-        sends.append(send)
-    for send in sends:
-        send.wait()
+                    one = moved[r * 128 : (r + 1) * 128, k * 128 : (k + 1) * 128]
+                    base = (index * 2 + r) * pairs + start + k
+                    out[pl.ds(base, 128, stride=count * 2 * pairs), :] = one
 
 
 def slab_waves(data, x_local, blocks, count_gl, per_owner):
@@ -286,16 +239,14 @@
     twist = np.stack([np.cos(twist_angle), np.sin(twist_angle)]).astype(np.float32)
     entries = devices * per_owner
     rows = blocks * x_local * 2
-    return pl.pallas_call(
+    made = pl.pallas_call(
         functools.partial(slab_kernel, count, x_local, blocks, per_owner),
-        out_shape=pltpu.HBM((devices, count, rows // devices, 128), jnp.float32),
+        out_shape=pltpu.VMEM((count * rows, 128), jnp.float32),
         in_specs=[pl.BlockSpec(memory_space=pltpu.VMEM)] * 3,
-        out_specs=pl.BlockSpec(memory_space=pltpu.HBM),
+        out_specs=pl.BlockSpec(memory_space=pltpu.VMEM),
         scratch_shapes=[
-            pltpu.VMEM((count, rows, 128), jnp.float32),
             pltpu.VMEM((count, 2, blocks * x_local, 128), jnp.float32),
             pltpu.VMEM((blocks * x_local, 256), jnp.float32),
-            pltpu.SemaphoreType.DMA((count,)),
         ],
         compiler_params=params(40),
         cost_estimate=cost(
@@ -303,6 +254,7 @@
             count * (entries * 1024 + rows * 512),
         ),
     )(jnp.asarray(table), jnp.asarray(twist), in_vmem(data))
+    return made.reshape(devices, count * rows // devices, 128)
 
 
 def choose(options, mask_of):
@@ -313,7 +265,7 @@
 
 
 def x_steps(
-    devices, x_local, y_local, blocks, order, index, twist, table, data, turned, columns, store, whole
+    devices, x_local, y_local, blocks, order, index, twist, stacked, data, turned, columns, store, whole
 ):
     group = 128 // x_local
     pairs = blocks // group
@@ -323,11 +275,10 @@
 
     @pl.loop(0, kept)
     def _(step):
-        at = pl.multiple_of(step * 2 * pairs, 2 * pairs)
+        stride = data.shape[1] // kept
+        at = pl.multiple_of(step * stride, 2 * pairs) + index * 2 * pairs
         values = [
-            tuple(
-                data[order.index(o), index, pl.ds(at + r * pairs, pairs), :] for r in range(2)
-            )
+            tuple(data[order.index(o), pl.ds(at + r * pairs, pairs), :] for r in range(2))
             for o in range(devices)
         ]
         waves = flat_fft(values, times_pair)
@@ -342,8 +293,8 @@
     square = banks * narrow == 128 and 128 // narrow == banks
     together = min(devices, 256 // narrow)
     for start in range(0, devices, together):
-        stacked = turned[start : start + together].reshape(together * narrow, 256)
-        moved = dot_rows_split(table[...], stacked)
+        rows = turned[start : start + together].reshape(together * narrow, 256)
+        moved = dot_rows_split(stacked, rows)
         if square:
             for base in range(0, together, banks):
                 rolled = []
@@ -400,6 +351,7 @@
     width = x_cells // made.shape[0]
     fetch = pltpu.make_async_copy(green, tensor, in_sem)
     fetch.start()
+    stacked = stacked_halves(table)
     sends = []
     for comp in range(3):
 
@@ -412,7 +364,7 @@
             piece = start // width
             part = pl.ds(piece * width, width)
 
-            @pl.loop(0, y_local // 8)
+            @pl.loop(0, y_local // 8, unroll=2)
             def _(step):
                 rows = pl.ds(pl.multiple_of(step * 8, 8), 8)
                 for row, pair in enumerate(mix_rows(rows, part, tensor, kept)):
@@ -427,7 +379,7 @@
 
         if comp == 2:
             fetch.wait()
-        x_steps(*sizes, comp, twist, table, data, turned, columns, store, whole)
+        x_steps(*sizes, comp, twist, stacked, data, turned, columns, store, whole)
     for send in sends:
         send.wait()
 

time: 180 us -> 177 us (0.983)
  Pallas kernels: 21.7 us -> 19.4 us
  blocking collectives: 158 us -> 156 us
where the time goes in v2:
time: 177 us
  blocking collectives  156 us (88%)
  Pallas kernels  19.4 us (11%)
    all_to_all x2, blocking collectives, exchange(): return lax.all_to_all(data, places, split_axis=0, concat_axis=0, tiled=True)  156 us
    pallas_call x1, Pallas kernels, field(): pl.pallas_call(functools.partial(field_kernel, sizes), out_shape=pltpu.HB...  8.9 us
    pallas_call x1, Pallas kernels, slab_waves(): pl.pallas_call(functools.partial(slab_kernel, count, x_local, blocks, per...  6.91 us
    pallas_call x1, Pallas kernels, pack(): pl.pallas_call(functools.partial(pack_kernel, devices, count_gl, per_owne...  3.56 us

profile of v2, /device:TPU:0, one launch (start us, length us, event | category | flops | bytes accessed | tf_op | source)
XLA Modules:
  0.0 176.6 jit_solution(4593195861267400946)
XLA Ops:
  0.7 3.6 %shard_map.91 = f32[32,200,128]{2,1,0:T(8,128)S(1)} custom-call(s32[1]{0:T(128)S(6)} %copy.11.count, s32[1]{0:T(128)} %bitcast.me, s32[1,512]{1,0:T(1,128)} %bitcast.10, s32[1,512]{1,0:T(1,128)} %bitcast.11, f32[2,3,512,128]{3,2,1,0:T(8,128)} %tiles.1), custom_call_target="tpu_custom_call" | custom-call | flops 1610612736 | bytes 6553600 | tf_op jit(solution)/shard_map/pallas_call | solution.py:149
  4.2 0.0 copy-start.2
  4.2 0.0 copy-start.3
  4.2 82.7 %all_to_all.10.data = f32[32,200,128]{2,1,0:T(8,128)S(1)} all-to-all(f32[32,200,128]{2,1,0:T(8,128)S(1)} %shard_map.91), channel_id=1, replica_groups=mesh['gx'=4,'gz'=4,'gl'=2] {'gx','gl','gz'}, dimensions={0} | all-to-all | bytes 6553600 | tf_op jit(solution)/shard_map/all_to_all | solution.py:434
  86.9 0.0 copy-done.2
  86.9 0.0 copy-done.3
  87.0 6.9 %shard_map.92 = f32[6144,128]{1,0:T(8,128)S(1)} custom-call(f32[256,256]{1,0:T(8,128)S(1)} %copy-done.2, f32[2,16,128]{2,1,0:T(8,128)S(1)} %copy-done.3, f32[32,200,128]{2,1,0:T(8,128)S(1)} %all_to_all.10.data), custom_call_target="tpu_custom_call" | custom-call | flops 4831838208 | bytes 6291456 | tf_op jit(solution)/shard_map/pallas_call | solution.py:242
  93.9 0.0 copy-start
  93.9 0.0 copy-start.1
  93.9 73.6 %all_to_all.11.data = f32[32,192,128]{2,1,0:T(8,128)S(1)} all-to-all(f32[32,192,128]{2,1,0:T(8,128)S(1)} %bitcast.8), channel_id=1, replica_groups=mesh['gx'=4,'gz'=4,'gl'=2] {'gx','gl','gz'}, dimensions={0} | all-to-all | bytes 6291456 | tf_op jit(solution)/shard_map/all_to_all | solution.py:434
  167.5 0.0 copy-done
  167.5 0.0 copy-done.1
  167.5 8.9 %shard_map.93 = f32[2,3,64,2048]{3,2,1,0:T(8,128)} custom-call(f32[2,32,128]{2,1,0:T(8,128)S(1)} %copy-done.1, f32[256,256]{1,0:T(8,128)S(1)} %copy-done, f32[32,192,128]{2,1,0:T(8,128)S(1)} %all_to_all.11.data, f32[2,6,64,2048]{3,2,1,0:T(8,128)} %bitcast.9), custom_call_target="tpu_custom_call" | custom-call | flops 613416960 | bytes 12582912 | tf_op jit(solution)/shard_map/pallas_call | solution.py:411
Async XLA Ops:
  4.2 82.7 %copy-start.2 = (f32[256,256]{1,0:T(8,128)S(1)}, f32[256,256]{1,0:T(8,128)}, u32[]{:S(2)}) copy-start(f32[256,256]{1,0:T(8,128)} %constant.23.clone.table) | copy-start | bytes 786436
  4.2 82.7 %copy-start.3 = (f32[2,16,128]{2,1,0:T(8,128)S(1)}, f32[2,16,128]{2,1,0:T(8,128)}, u32[]{:S(2)}) copy-start(f32[2,16,128]{2,1,0:T(8,128)} %constant.24.clone.twist) | copy-start | bytes 49156
  93.9 73.6 %copy-start = (f32[256,256]{1,0:T(8,128)S(1)}, f32[256,256]{1,0:T(8,128)}, u32[]{:S(2)}) copy-start(f32[256,256]{1,0:T(8,128)} %constant.26.clone.table) | copy-start | bytes 786436
  93.9 73.6 %copy-start.1 = (f32[2,32,128]{2,1,0:T(8,128)S(1)}, f32[2,32,128]{2,1,0:T(8,128)}, u32[]{:S(2)}) copy-start(f32[2,32,128]{2,1,0:T(8,128)} %constant.25.clone.twist) | copy-start | bytes 98308

commit v3 on v2

--- a/solution.py
+++ b/solution.py
@@ -174,7 +174,7 @@
 
 
 def slab_kernel(count, x_local, blocks, per_owner, table, twist, data, out, *scratch):
-    slab, turned = scratch
+    chosen, slab, turned = scratch
     devices = data.shape[0]
     entries = devices * per_owner
     group = 128 // x_local
@@ -187,45 +187,59 @@
     ]
     slot = jnp.concatenate(stated, axis=1).astype(jnp.int32) - 1
     landing = jnp.where(slot >= 0, (slot & (blocks - 1)) * x_local + (slot >> shift), -1)
-    parts = []
-    for i in range(2 * count):
-        one = data[:, i * per_owner : (i + 1) * per_owner, :]
-        parts.extend(split_two(one.reshape(entries, 128)))
-    parts = jnp.concatenate(parts, axis=1)
-    step_rows = min(512, blocks * x_local)
-    for start in range(0, blocks * x_local, step_rows):
-        place = start + lax.broadcasted_iota(jnp.int32, (step_rows, entries), 0)
-        chosen = jnp.where(place == landing, 1.0, 0.0).astype(jnp.bfloat16)
-        got = jnp.dot(chosen, parts, preferred_element_type=jnp.float32)
-        for i in range(2 * count):
-            slab[i // 2, i % 2, start : start + step_rows, :] = (
-                got[:, 256 * i : 256 * i + 128] + got[:, 256 * i + 128 : 256 * i + 256]
+    slab_rows = blocks * x_local
+    place = lax.broadcasted_iota(jnp.int32, (slab_rows, entries), 0)
+    chosen[...] = jnp.where(place == landing, 1.0, 0.0).astype(jnp.bfloat16)
+    stacked = stacked_halves(table)
+    step_rows = slab_rows // 2
+
+    def scatter(index, half):
+        parts = []
+        for r in range(2):
+            start = (2 * index + r) * per_owner
+            parts.extend(split_two(data[:, start : start + per_owner, :].reshape(entries, 128)))
+        rows = pl.ds(half * step_rows, step_rows)
+        got = jnp.dot(
+            chosen[rows, :], jnp.concatenate(parts, axis=1), preferred_element_type=jnp.float32
+        )
+        for r in range(2):
+            slab[index, r, rows, :] = (
+                got[:, 256 * r : 256 * r + 128] + got[:, 256 * r + 128 : 256 * r + 256]
             )
-    stacked = stacked_halves(table)
+
+    def transform(index, step):
+        at = step * 8
+        values = [
+            tuple(slab[index, r, pl.ds(t * x_local + at, 8), :] for r in range(2))
+            for t in range(blocks)
+        ]
+        waves = flat_fft(values, times_pair)
+        for k in range(blocks):
+            real, imag = waves[k]
+            cos_k, sin_k = twist[0, k : k + 1, :], twist[1, k : k + 1, :]
+            rows = pl.ds(((k % pairs) * group + k // pairs) * x_local + at, 8)
+            turned[index % 2, rows, :128] = real * cos_k + imag * sin_k
+            turned[index % 2, rows, 128:] = imag * cos_k - real * sin_k
+
+    def along_y(index, start):
+        moved = dot_rows_split(stacked, turned[index % 2, start * 128 : (start + 2) * 128, :])
+        for k in range(2):
+            for r in range(2):
+                one = moved[r * 128 : (r + 1) * 128, k * 128 : (k + 1) * 128]
+                base = (index * 2 + r) * pairs + start + k
+                out[pl.ds(base, 128, stride=count * 2 * pairs), :] = one
+
+    steps = x_local // 8
+    scatter(0, 0)
+    scatter(0, 1)
     for index in range(count):
-
-        @pl.loop(0, x_local // 8, unroll=2)
-        def _(step):
-            at = pl.multiple_of(step * 8, 8)
-            values = [
-                tuple(slab[index, r, pl.ds(t * x_local + at, 8), :] for r in range(2))
-                for t in range(blocks)
-            ]
-            waves = flat_fft(values, times_pair)
-            for k in range(blocks):
-                real, imag = waves[k]
-                cos_k, sin_k = twist[0, k : k + 1, :], twist[1, k : k + 1, :]
-                rows = pl.ds(((k % pairs) * group + k // pairs) * x_local + at, 8)
-                turned[rows, :128] = real * cos_k + imag * sin_k
-                turned[rows, 128:] = imag * cos_k - real * sin_k
-
+        for half in range(2):
+            if index + 1 < count:
+                scatter(index + 1, half)
+            for step in range(half * steps // 2, (half + 1) * steps // 2):
+                transform(index, step)
         for start in range(0, pairs, 2):
-            moved = dot_rows_split(stacked, turned[start * 128 : (start + 2) * 128, :])
-            for k in range(2):
-                for r in range(2):
-                    one = moved[r * 128 : (r + 1) * 128, k * 128 : (k + 1) * 128]
-                    base = (index * 2 + r) * pairs + start + k
-                    out[pl.ds(base, 128, stride=count * 2 * pairs), :] = one
+            along_y(index, start)
 
 
 def slab_waves(data, x_local, blocks, count_gl, per_owner):
@@ -245,8 +259,9 @@
         in_specs=[pl.BlockSpec(memory_space=pltpu.VMEM)] * 3,
         out_specs=pl.BlockSpec(memory_space=pltpu.VMEM),
         scratch_shapes=[
+            pltpu.VMEM((blocks * x_local, entries), jnp.bfloat16),
             pltpu.VMEM((count, 2, blocks * x_local, 128), jnp.float32),
-            pltpu.VMEM((blocks * x_local, 256), jnp.float32),
+            pltpu.VMEM((2, blocks * x_local, 256), jnp.float32),
         ],
         compiler_params=params(40),
         cost_estimate=cost(
@@ -264,69 +279,81 @@
     return made
 
 
-def x_steps(
-    devices, x_local, y_local, blocks, order, index, twist, stacked, data, turned, columns, store, whole
-):
+def x_first(sizes, comp, step, twist, data, turned):
+    devices, x_local, y_local, blocks, order = sizes
+    pairs = blocks * x_local // 128
+    kept = y_local // blocks
+    at = step * (data.shape[1] // kept) + comp * 2 * pairs
+    values = [
+        tuple(data[order.index(o), pl.ds(at + r * pairs, pairs), :] for r in range(2))
+        for o in range(devices)
+    ]
+    waves = flat_fft(values, times_pair)
+    rows = pl.ds(step * pairs, pairs)
+    for k in range(devices):
+        real, imag = waves[k]
+        cos_k, sin_k = twist[0, k : k + 1, :], twist[1, k : k + 1, :]
+        turned[comp % 2, k, rows, :128] = real * cos_k + imag * sin_k
+        turned[comp % 2, k, rows, 128:] = imag * cos_k - real * sin_k
+
+
+def x_second(sizes, comp, start, together, stacked, turned, columns):
+    devices, x_local, y_local, blocks, _ = sizes
+    group = 128 // x_local
+    narrow = (y_local // blocks) * (blocks // group)
+    banks = 2 * group
+    lane = lax.broadcasted_iota(jnp.int32, (1, 128), 1)
+    rows = turned[comp % 2, start : start + together].reshape(together * narrow, 256)
+    moved = dot_rows_split(stacked, rows)
+    if square(sizes):
+        for base in range(0, together, banks):
+            rolled = []
+            for bank in range(banks):
+                one = moved[bank * x_local : (bank + 1) * x_local, base * narrow :][:, :128]
+                rolled.append(pltpu.roll(one, bank * narrow, 1) if bank else one)
+            for k in range(banks):
+                options = [rolled[(place - k) % banks] for place in range(banks)]
+                rows = pl.ds(start + base + k, x_local, stride=devices)
+                columns[rows, :] = choose(options, lambda i: lane // narrow == i)
+        return
+    for k in range(together):
+        one = jnp.concatenate(
+            [
+                moved[bank * x_local : (bank + 1) * x_local, k * narrow : (k + 1) * narrow]
+                for bank in range(banks)
+            ],
+            axis=1,
+        )
+        columns[pl.ds(start + k, x_local, stride=devices), :] = one
+
+
+def square(sizes):
+    _, x_local, y_local, blocks, _ = sizes
+    group = 128 // x_local
+    narrow = (y_local // blocks) * (blocks // group)
+    return 2 * group * narrow == 128 and 128 // narrow == 2 * group
+
+
+def x_third(sizes, comp, start, columns, kept):
+    _, x_local, y_local, blocks, _ = sizes
     group = 128 // x_local
     pairs = blocks // group
-    kept = y_local // blocks
-    narrow = kept * pairs
+    steps = y_local // blocks
+    narrow = steps * pairs
     banks = 2 * group
-
-    @pl.loop(0, kept)
-    def _(step):
-        stride = data.shape[1] // kept
-        at = pl.multiple_of(step * stride, 2 * pairs) + index * 2 * pairs
-        values = [
-            tuple(data[order.index(o), pl.ds(at + r * pairs, pairs), :] for r in range(2))
-            for o in range(devices)
-        ]
-        waves = flat_fft(values, times_pair)
-        rows = pl.ds(pl.multiple_of(step * pairs, pairs), pairs)
-        for k in range(devices):
-            real, imag = waves[k]
-            cos_k, sin_k = twist[0, k : k + 1, :], twist[1, k : k + 1, :]
-            turned[k, rows, :128] = real * cos_k + imag * sin_k
-            turned[k, rows, 128:] = imag * cos_k - real * sin_k
-
     lane = lax.broadcasted_iota(jnp.int32, (1, 128), 1)
-    square = banks * narrow == 128 and 128 // narrow == banks
-    together = min(devices, 256 // narrow)
-    for start in range(0, devices, together):
-        rows = turned[start : start + together].reshape(together * narrow, 256)
-        moved = dot_rows_split(stacked, rows)
-        if square:
-            for base in range(0, together, banks):
-                rolled = []
-                for bank in range(banks):
-                    one = moved[bank * x_local : (bank + 1) * x_local, base * narrow :][:, :128]
-                    rolled.append(pltpu.roll(one, bank * narrow, 1) if bank else one)
-                for k in range(banks):
-                    options = [rolled[(place - k) % banks] for place in range(banks)]
-                    rows = pl.ds(start + base + k, x_local, stride=devices)
-                    columns[rows, :] = choose(options, lambda i: lane // narrow == i)
-        else:
-            for k in range(together):
-                one = jnp.concatenate(
-                    [
-                        moved[bank * x_local : (bank + 1) * x_local, k * narrow : (k + 1) * narrow]
-                        for bank in range(banks)
-                    ],
-                    axis=1,
-                )
-                columns[pl.ds(start + k, x_local, stride=devices), :] = one
-    for start in range(0, devices * x_local, 128):
-        block = columns[start : start + 128, :].T
-        pieces = [block[bank * narrow : (bank + 1) * narrow] for bank in range(banks)]
-        for bank in range(banks):
-            one = pieces[bank]
-            if square:
-                options = [pieces[(bank + k) % banks] for k in range(banks)]
-                one = choose(options, lambda i: lane % banks == i)
-            for step in range(kept):
-                row = step * blocks + (bank % group) * pairs
-                store(bank // group, row, start, one[step * pairs : (step + 1) * pairs])
-        whole(start)
+    block = columns[start : start + 128, :].T
+    pieces = [block[bank * narrow : (bank + 1) * narrow] for bank in range(banks)]
+    for bank in range(banks):
+        one = pieces[bank]
+        if square(sizes):
+            options = [pieces[(bank + k) % banks] for k in range(banks)]
+            one = choose(options, lambda i: lane % banks == i)
+        for step in range(steps):
+            row = step * blocks + (bank % group) * pairs
+            kept[comp, bank // group, row : row + pairs, start : start + 128] = one[
+                step * pairs : (step + 1) * pairs
+            ]
 
 
 def mix_rows(rows, columns, tensor, waves):
@@ -352,34 +379,39 @@
     fetch = pltpu.make_async_copy(green, tensor, in_sem)
     fetch.start()
     stacked = stacked_halves(table)
+    devices, x_local, _, blocks, _ = sizes
+    steps = y_local // blocks
+    narrow = y_local * x_local // 128
+    together = min(devices, 256 // narrow)
+    groups = devices // together
+    for step in range(steps):
+        x_first(sizes, 0, step, twist, data, turned)
+    for comp in range(3):
+        for i in range(max(steps, groups)):
+            if comp < 2 and i < steps:
+                x_first(sizes, comp + 1, i, twist, data, turned)
+            if i < groups:
+                x_second(sizes, comp, i * together, together, stacked, turned, columns)
+        if comp < 2:
+            for start in range(0, x_cells, 128):
+                x_third(sizes, comp, start, columns, kept)
+    fetch.wait()
     sends = []
-    for comp in range(3):
-
-        def store(r, row, start, block):
-            kept[comp, r, row : row + block.shape[0], start : start + 128] = block
-
-        def whole(start):
-            if comp < 2 or (start + 128) % width:
-                return
-            piece = start // width
-            part = pl.ds(piece * width, width)
-
-            @pl.loop(0, y_local // 8, unroll=2)
-            def _(step):
-                rows = pl.ds(pl.multiple_of(step * 8, 8), 8)
-                for row, pair in enumerate(mix_rows(rows, part, tensor, kept)):
-                    for r in range(2):
-                        made[piece, r, row, rows, :] = pair[r]
-
-            send = pltpu.make_async_copy(
-                made.at[piece], out.at[:, :, :, part], out_sems.at[piece]
-            )
-            send.start()
-            sends.append(send)
-
-        if comp == 2:
-            fetch.wait()
-        x_steps(*sizes, comp, twist, stacked, data, turned, columns, store, whole)
+    for piece in range(made.shape[0]):
+        for start in range(piece * width, (piece + 1) * width, 128):
+            x_third(sizes, 2, start, columns, kept)
+        part = pl.ds(piece * width, width)
+
+        @pl.loop(0, y_local // 8, unroll=2)
+        def _(step):
+            rows = pl.ds(pl.multiple_of(step * 8, 8), 8)
+            for row, pair in enumerate(mix_rows(rows, part, tensor, kept)):
+                for r in range(2):
+                    made[piece, r, row, rows, :] = pair[r]
+
+        send = pltpu.make_async_copy(made.at[piece], out.at[:, :, :, part], out_sems.at[piece])
+        send.start()
+        sends.append(send)
     for send in sends:
         send.wait()
 
@@ -398,7 +430,7 @@
 
 def x_scratch(devices, x_local, y_local):
     return [
-        pltpu.VMEM((devices, y_local * x_local // 128, 256), jnp.float32),
+        pltpu.VMEM((2, devices, y_local * x_local // 128, 256), jnp.float32),
         pltpu.VMEM((devices * x_local, 2 * y_local), jnp.float32),
     ]
 

time: 177 us -> 176 us (level)
  no operation moved by 1% of the time
where the time goes in v3:
time: 176 us
  blocking collectives  156 us (89%)
  Pallas kernels  18.8 us (11%)
    all_to_all x2, blocking collectives, exchange(): return lax.all_to_all(data, places, split_axis=0, concat_axis=0, tiled=True)  156 us
    pallas_call x1, Pallas kernels, field(): pl.pallas_call(functools.partial(field_kernel, sizes), out_shape=pltpu.HB...  9.91 us
    pallas_call x1, Pallas kernels, slab_waves(): pl.pallas_call(functools.partial(slab_kernel, count, x_local, blocks, per...  5.36 us
    pallas_call x1, Pallas kernels, pack(): pl.pallas_call(functools.partial(pack_kernel, devices, count_gl, per_owne...  3.56 us

profile of v3, /device:TPU:0, one launch (start us, length us, event | category | flops | bytes accessed | tf_op | source)
XLA Modules:
  0.0 176.0 jit_solution(2335191503182856806)
XLA Ops:
  0.7 3.6 %shard_map.91 = f32[32,200,128]{2,1,0:T(8,128)S(1)} custom-call(s32[1]{0:T(128)S(6)} %copy.11.count, s32[1]{0:T(128)} %bitcast.me, s32[1,512]{1,0:T(1,128)} %bitcast.10, s32[1,512]{1,0:T(1,128)} %bitcast.11, f32[2,3,512,128]{3,2,1,0:T(8,128)} %tiles.1), custom_call_target="tpu_custom_call" | custom-call | flops 1610612736 | bytes 6553600 | tf_op jit(solution)/shard_map/pallas_call | solution.py:149
  4.2 0.0 copy-start.2
  4.2 0.0 copy-start.3
  4.2 82.7 %all_to_all.10.data = f32[32,200,128]{2,1,0:T(8,128)S(1)} all-to-all(f32[32,200,128]{2,1,0:T(8,128)S(1)} %shard_map.91), channel_id=1, replica_groups=mesh['gx'=4,'gz'=4,'gl'=2] {'gx','gl','gz'}, dimensions={0} | all-to-all | bytes 6553600 | tf_op jit(solution)/shard_map/all_to_all | solution.py:466
  86.9 0.0 copy-done.2
  86.9 0.0 copy-done.3
  87.0 5.4 %shard_map.92 = f32[6144,128]{1,0:T(8,128)S(1)} custom-call(f32[256,256]{1,0:T(8,128)S(1)} %copy-done.2, f32[2,16,128]{2,1,0:T(8,128)S(1)} %copy-done.3, f32[32,200,128]{2,1,0:T(8,128)S(1)} %all_to_all.10.data), custom_call_target="tpu_custom_call" | custom-call | flops 4831838208 | bytes 6291456 | tf_op jit(solution)/shard_map/pallas_call | solution.py:256
  92.3 0.0 copy-start
  92.3 0.0 copy-start.1
  92.3 73.6 %all_to_all.11.data = f32[32,192,128]{2,1,0:T(8,128)S(1)} all-to-all(f32[32,192,128]{2,1,0:T(8,128)S(1)} %bitcast.8), channel_id=1, replica_groups=mesh['gx'=4,'gz'=4,'gl'=2] {'gx','gl','gz'}, dimensions={0} | all-to-all | bytes 6291456 | tf_op jit(solution)/shard_map/all_to_all | solution.py:466
  166.0 0.0 copy-done
  166.0 0.0 copy-done.1
  166.0 9.9 %shard_map.93 = f32[2,3,64,2048]{3,2,1,0:T(8,128)} custom-call(f32[2,32,128]{2,1,0:T(8,128)S(1)} %copy-done.1, f32[256,256]{1,0:T(8,128)S(1)} %copy-done, f32[32,192,128]{2,1,0:T(8,128)S(1)} %all_to_all.11.data, f32[2,6,64,2048]{3,2,1,0:T(8,128)} %bitcast.9), custom_call_target="tpu_custom_call" | custom-call | flops 613416960 | bytes 12582912 | tf_op jit(solution)/shard_map/pallas_call | solution.py:443
Async XLA Ops:
  4.2 82.7 %copy-start.2 = (f32[256,256]{1,0:T(8,128)S(1)}, f32[256,256]{1,0:T(8,128)}, u32[]{:S(2)}) copy-start(f32[256,256]{1,0:T(8,128)} %constant.23.clone.table) | copy-start | bytes 786436
  4.2 82.7 %copy-start.3 = (f32[2,16,128]{2,1,0:T(8,128)S(1)}, f32[2,16,128]{2,1,0:T(8,128)}, u32[]{:S(2)}) copy-start(f32[2,16,128]{2,1,0:T(8,128)} %constant.24.clone.twist) | copy-start | bytes 49156
  92.3 73.6 %copy-start = (f32[256,256]{1,0:T(8,128)S(1)}, f32[256,256]{1,0:T(8,128)}, u32[]{:S(2)}) copy-start(f32[256,256]{1,0:T(8,128)} %constant.26.clone.table) | copy-start | bytes 786436
  92.3 73.6 %copy-start.1 = (f32[2,32,128]{2,1,0:T(8,128)S(1)}, f32[2,32,128]{2,1,0:T(8,128)}, u32[]{:S(2)}) copy-start(f32[2,32,128]{2,1,0:T(8,128)} %constant.25.clone.twist) | copy-start | bytes 98308

commit v4 on v3

--- a/solution.py
+++ b/solution.py
@@ -283,13 +283,13 @@
     devices, x_local, y_local, blocks, order = sizes
     pairs = blocks * x_local // 128
     kept = y_local // blocks
-    at = step * (data.shape[1] // kept) + comp * 2 * pairs
+    at = pl.multiple_of(step * (data.shape[1] // kept), 2 * pairs) + comp * 2 * pairs
     values = [
         tuple(data[order.index(o), pl.ds(at + r * pairs, pairs), :] for r in range(2))
         for o in range(devices)
     ]
     waves = flat_fft(values, times_pair)
-    rows = pl.ds(step * pairs, pairs)
+    rows = pl.ds(pl.multiple_of(step * pairs, pairs), pairs)
     for k in range(devices):
         real, imag = waves[k]
         cos_k, sin_k = twist[0, k : k + 1, :], twist[1, k : k + 1, :]
@@ -297,13 +297,14 @@
         turned[comp % 2, k, rows, 128:] = imag * cos_k - real * sin_k
 
 
-def x_second(sizes, comp, start, together, stacked, turned, columns):
+def x_second(sizes, comp, step, together, stacked, turned, columns):
     devices, x_local, y_local, blocks, _ = sizes
     group = 128 // x_local
     narrow = (y_local // blocks) * (blocks // group)
     banks = 2 * group
     lane = lax.broadcasted_iota(jnp.int32, (1, 128), 1)
-    rows = turned[comp % 2, start : start + together].reshape(together * narrow, 256)
+    start = step * together
+    rows = turned[comp % 2, pl.ds(start, together)].reshape(together * narrow, 256)
     moved = dot_rows_split(stacked, rows)
     if square(sizes):
         for base in range(0, together, banks):
@@ -314,7 +315,7 @@
             for k in range(banks):
                 options = [rolled[(place - k) % banks] for place in range(banks)]
                 rows = pl.ds(start + base + k, x_local, stride=devices)
-                columns[rows, :] = choose(options, lambda i: lane // narrow == i)
+                columns[comp, rows, :] = choose(options, lambda i: lane // narrow == i)
         return
     for k in range(together):
         one = jnp.concatenate(
@@ -324,7 +325,7 @@
             ],
             axis=1,
         )
-        columns[pl.ds(start + k, x_local, stride=devices), :] = one
+        columns[comp, pl.ds(start + k, x_local, stride=devices), :] = one
 
 
 def square(sizes):
@@ -342,7 +343,7 @@
     narrow = steps * pairs
     banks = 2 * group
     lane = lax.broadcasted_iota(jnp.int32, (1, 128), 1)
-    block = columns[start : start + 128, :].T
+    block = columns[comp, start : start + 128, :].T
     pieces = [block[bank * narrow : (bank + 1) * narrow] for bank in range(banks)]
     for bank in range(banks):
         one = pieces[bank]
@@ -384,31 +385,36 @@
     narrow = y_local * x_local // 128
     together = min(devices, 256 // narrow)
     groups = devices // together
-    for step in range(steps):
-        x_first(sizes, 0, step, twist, data, turned)
+    pl.loop(0, steps)(lambda i: x_first(sizes, 0, i, twist, data, turned))
     for comp in range(3):
-        for i in range(max(steps, groups)):
-            if comp < 2 and i < steps:
+
+        @pl.loop(0, groups)
+        def _(i):
+            if comp < 2 and steps == groups:
                 x_first(sizes, comp + 1, i, twist, data, turned)
-            if i < groups:
-                x_second(sizes, comp, i * together, together, stacked, turned, columns)
-        if comp < 2:
-            for start in range(0, x_cells, 128):
+            x_second(sizes, comp, i, together, stacked, turned, columns)
+
+        if comp < 2 and steps != groups:
+            pl.loop(0, steps)(lambda i: x_first(sizes, comp + 1, i, twist, data, turned))
+    fetch.wait()
+    pieces = made.shape[0]
+
+    def turn(piece):
+        for start in range(piece * width, (piece + 1) * width, 128):
+            for comp in range(3):
                 x_third(sizes, comp, start, columns, kept)
-    fetch.wait()
+
     sends = []
-    for piece in range(made.shape[0]):
-        for start in range(piece * width, (piece + 1) * width, 128):
-            x_third(sizes, 2, start, columns, kept)
+    turn(0)
+    for piece in range(pieces):
+        if piece + 1 < pieces:
+            turn(piece + 1)
         part = pl.ds(piece * width, width)
-
-        @pl.loop(0, y_local // 8, unroll=2)
-        def _(step):
-            rows = pl.ds(pl.multiple_of(step * 8, 8), 8)
+        for step in range(y_local // 8):
+            rows = pl.ds(step * 8, 8)
             for row, pair in enumerate(mix_rows(rows, part, tensor, kept)):
                 for r in range(2):
                     made[piece, r, row, rows, :] = pair[r]
-
         send = pltpu.make_async_copy(made.at[piece], out.at[:, :, :, part], out_sems.at[piece])
         send.start()
         sends.append(send)
@@ -431,7 +437,7 @@
 def x_scratch(devices, x_local, y_local):
     return [
         pltpu.VMEM((2, devices, y_local * x_local // 128, 256), jnp.float32),
-        pltpu.VMEM((devices * x_local, 2 * y_local), jnp.float32),
+        pltpu.VMEM((3, devices * x_local, 2 * y_local), jnp.float32),
     ]
 
 

time: 176 us -> 176 us (level)
  no operation moved by 1% of the time
where the time goes in v4:
time: 176 us
  blocking collectives  156 us (89%)
  Pallas kernels  19.1 us (11%)
    all_to_all x2, blocking collectives, exchange(): return lax.all_to_all(data, places, split_axis=0, concat_axis=0, tiled=True)  156 us
    pallas_call x1, Pallas kernels, field(): pl.pallas_call(functools.partial(field_kernel, sizes), out_shape=pltpu.HB...  10.2 us
    pallas_call x1, Pallas kernels, slab_waves(): pl.pallas_call(functools.partial(slab_kernel, count, x_local, blocks, per...  5.36 us
    pallas_call x1, Pallas kernels, pack(): pl.pallas_call(functools.partial(pack_kernel, devices, count_gl, per_owne...  3.56 us

profile of v4, /device:TPU:0, one launch (start us, length us, event | category | flops | bytes accessed | tf_op | source)
XLA Modules:
  0.0 176.2 jit_solution(16020549438868211607)
XLA Ops:
  0.7 3.6 %shard_map.91 = f32[32,200,128]{2,1,0:T(8,128)S(1)} custom-call(s32[1]{0:T(128)S(6)} %copy.11.count, s32[1]{0:T(128)} %bitcast.me, s32[1,512]{1,0:T(1,128)} %bitcast.10, s32[1,512]{1,0:T(1,128)} %bitcast.11, f32[2,3,512,128]{3,2,1,0:T(8,128)} %tiles.1), custom_call_target="tpu_custom_call" | custom-call | flops 1610612736 | bytes 6553600 | tf_op jit(solution)/shard_map/pallas_call | solution.py:149
  4.2 0.0 copy-start.2
  4.2 0.0 copy-start.3
  4.2 82.7 %all_to_all.10.data = f32[32,200,128]{2,1,0:T(8,128)S(1)} all-to-all(f32[32,200,128]{2,1,0:T(8,128)S(1)} %shard_map.91), channel_id=1, replica_groups=mesh['gx'=4,'gz'=4,'gl'=2] {'gx','gl','gz'}, dimensions={0} | all-to-all | bytes 6553600 | tf_op jit(solution)/shard_map/all_to_all | solution.py:472
  86.9 0.0 copy-done.2
  87.0 0.0 copy-done.3
  87.0 5.4 %shard_map.92 = f32[6144,128]{1,0:T(8,128)S(1)} custom-call(f32[256,256]{1,0:T(8,128)S(1)} %copy-done.2, f32[2,16,128]{2,1,0:T(8,128)S(1)} %copy-done.3, f32[32,200,128]{2,1,0:T(8,128)S(1)} %all_to_all.10.data), custom_call_target="tpu_custom_call" | custom-call | flops 4831838208 | bytes 6291456 | tf_op jit(solution)/shard_map/pallas_call | solution.py:256
  92.3 0.0 copy-start
  92.3 0.0 copy-start.1
  92.3 73.6 %all_to_all.11.data = f32[32,192,128]{2,1,0:T(8,128)S(1)} all-to-all(f32[32,192,128]{2,1,0:T(8,128)S(1)} %bitcast.8), channel_id=1, replica_groups=mesh['gx'=4,'gz'=4,'gl'=2] {'gx','gl','gz'}, dimensions={0} | all-to-all | bytes 6291456 | tf_op jit(solution)/shard_map/all_to_all | solution.py:472
  166.0 0.0 copy-done
  166.0 0.0 copy-done.1
  166.0 10.2 %shard_map.93 = f32[2,3,64,2048]{3,2,1,0:T(8,128)} custom-call(f32[2,32,128]{2,1,0:T(8,128)S(1)} %copy-done.1, f32[256,256]{1,0:T(8,128)S(1)} %copy-done, f32[32,192,128]{2,1,0:T(8,128)S(1)} %all_to_all.11.data, f32[2,6,64,2048]{3,2,1,0:T(8,128)} %bitcast.9), custom_call_target="tpu_custom_call" | custom-call | flops 613416960 | bytes 12582912 | tf_op jit(solution)/shard_map/pallas_call | solution.py:449
Async XLA Ops:
  4.2 82.7 %copy-start.2 = (f32[256,256]{1,0:T(8,128)S(1)}, f32[256,256]{1,0:T(8,128)}, u32[]{:S(2)}) copy-start(f32[256,256]{1,0:T(8,128)} %constant.23.clone.table) | copy-start | bytes 786436
  4.2 82.7 %copy-start.3 = (f32[2,16,128]{2,1,0:T(8,128)S(1)}, f32[2,16,128]{2,1,0:T(8,128)}, u32[]{:S(2)}) copy-start(f32[2,16,128]{2,1,0:T(8,128)} %constant.24.clone.twist) | copy-start | bytes 49156
  92.3 73.6 %copy-start = (f32[256,256]{1,0:T(8,128)S(1)}, f32[256,256]{1,0:T(8,128)}, u32[]{:S(2)}) copy-start(f32[256,256]{1,0:T(8,128)} %constant.26.clone.table) | copy-start | bytes 786436
  92.3 73.6 %copy-start.1 = (f32[2,32,128]{2,1,0:T(8,128)S(1)}, f32[2,32,128]{2,1,0:T(8,128)}, u32[]{:S(2)}) copy-start(f32[2,32,128]{2,1,0:T(8,128)} %constant.25.clone.twist) | copy-start | bytes 98308

commit v5 on v3

--- a/solution.py
+++ b/solution.py
@@ -283,13 +283,13 @@
     devices, x_local, y_local, blocks, order = sizes
     pairs = blocks * x_local // 128
     kept = y_local // blocks
-    at = step * (data.shape[1] // kept) + comp * 2 * pairs
+    at = pl.multiple_of(step * (data.shape[1] // kept), 2 * pairs) + comp * 2 * pairs
     values = [
         tuple(data[order.index(o), pl.ds(at + r * pairs, pairs), :] for r in range(2))
         for o in range(devices)
     ]
     waves = flat_fft(values, times_pair)
-    rows = pl.ds(step * pairs, pairs)
+    rows = pl.ds(pl.multiple_of(step * pairs, pairs), pairs)
     for k in range(devices):
         real, imag = waves[k]
         cos_k, sin_k = twist[0, k : k + 1, :], twist[1, k : k + 1, :]
@@ -297,13 +297,14 @@
         turned[comp % 2, k, rows, 128:] = imag * cos_k - real * sin_k
 
 
-def x_second(sizes, comp, start, together, stacked, turned, columns):
+def x_second(sizes, comp, step, together, stacked, turned, columns):
     devices, x_local, y_local, blocks, _ = sizes
     group = 128 // x_local
     narrow = (y_local // blocks) * (blocks // group)
     banks = 2 * group
     lane = lax.broadcasted_iota(jnp.int32, (1, 128), 1)
-    rows = turned[comp % 2, start : start + together].reshape(together * narrow, 256)
+    start = step * together
+    rows = turned[comp % 2, pl.ds(start, together)].reshape(together * narrow, 256)
     moved = dot_rows_split(stacked, rows)
     if square(sizes):
         for base in range(0, together, banks):
@@ -314,7 +315,7 @@
             for k in range(banks):
                 options = [rolled[(place - k) % banks] for place in range(banks)]
                 rows = pl.ds(start + base + k, x_local, stride=devices)
-                columns[rows, :] = choose(options, lambda i: lane // narrow == i)
+                columns[comp, rows, :] = choose(options, lambda i: lane // narrow == i)
         return
     for k in range(together):
         one = jnp.concatenate(
@@ -324,7 +325,7 @@
             ],
             axis=1,
         )
-        columns[pl.ds(start + k, x_local, stride=devices), :] = one
+        columns[comp, pl.ds(start + k, x_local, stride=devices), :] = one
 
 
 def square(sizes):
@@ -342,7 +343,7 @@
     narrow = steps * pairs
     banks = 2 * group
     lane = lax.broadcasted_iota(jnp.int32, (1, 128), 1)
-    block = columns[start : start + 128, :].T
+    block = columns[comp, start : start + 128, :].T
     pieces = [block[bank * narrow : (bank + 1) * narrow] for bank in range(banks)]
     for bank in range(banks):
         one = pieces[bank]
@@ -384,17 +385,14 @@
     narrow = y_local * x_local // 128
     together = min(devices, 256 // narrow)
     groups = devices // together
-    for step in range(steps):
-        x_first(sizes, 0, step, twist, data, turned)
+    blocks_each = x_cells // 128 // groups
     for comp in range(3):
-        for i in range(max(steps, groups)):
-            if comp < 2 and i < steps:
-                x_first(sizes, comp + 1, i, twist, data, turned)
-            if i < groups:
-                x_second(sizes, comp, i * together, together, stacked, turned, columns)
-        if comp < 2:
-            for start in range(0, x_cells, 128):
-                x_third(sizes, comp, start, columns, kept)
+        pl.loop(0, steps)(lambda i: x_first(sizes, comp, i, twist, data, turned))
+        for i in range(groups):
+            x_second(sizes, comp, i, together, stacked, turned, columns)
+            for block in range(i * blocks_each, (i + 1) * blocks_each):
+                if comp > 0:
+                    x_third(sizes, comp - 1, block * 128, columns, kept)
     fetch.wait()
     sends = []
     for piece in range(made.shape[0]):
@@ -431,7 +429,7 @@
 def x_scratch(devices, x_local, y_local):
     return [
         pltpu.VMEM((2, devices, y_local * x_local // 128, 256), jnp.float32),
-        pltpu.VMEM((devices * x_local, 2 * y_local), jnp.float32),
+        pltpu.VMEM((3, devices * x_local, 2 * y_local), jnp.float32),
     ]
 
 

time: 176 us -> 175 us (level)
  no operation moved by 1% of the time
where the time goes in v5:
time: 175 us; the launch traced here: 174 us
  blocking collectives  156 us (89%)
  Pallas kernels  17.2 us (10%)
    all_to_all x2, blocking collectives, exchange(): return lax.all_to_all(data, places, split_axis=0, concat_axis=0, tiled=True)  156 us
    pallas_call x1, Pallas kernels, field(): pl.pallas_call(functools.partial(field_kernel, sizes), out_shape=pltpu.HB...  8.31 us
    pallas_call x1, Pallas kernels, slab_waves(): pl.pallas_call(functools.partial(slab_kernel, count, x_local, blocks, per...  5.36 us
    pallas_call x1, Pallas kernels, pack(): pl.pallas_call(functools.partial(pack_kernel, devices, count_gl, per_owne...  3.56 us

profile of v5, /device:TPU:0, one launch (start us, length us, event | category | flops | bytes accessed | tf_op | source)
XLA Modules:
  0.0 174.4 jit_solution(7939773784853757727)
XLA Ops:
  0.7 3.6 %shard_map.91 = f32[32,200,128]{2,1,0:T(8,128)S(1)} custom-call(s32[1]{0:T(128)S(6)} %copy.11.count, s32[1]{0:T(128)} %bitcast.me, s32[1,512]{1,0:T(1,128)} %bitcast.10, s32[1,512]{1,0:T(1,128)} %bitcast.11, f32[2,3,512,128]{3,2,1,0:T(8,128)} %tiles.1), custom_call_target="tpu_custom_call" | custom-call | flops 1610612736 | bytes 6553600 | tf_op jit(solution)/shard_map/pallas_call | solution.py:149
  4.2 0.0 copy-start.2
  4.2 0.0 copy-start.3
  4.2 82.7 %all_to_all.10.data = f32[32,200,128]{2,1,0:T(8,128)S(1)} all-to-all(f32[32,200,128]{2,1,0:T(8,128)S(1)} %shard_map.91), channel_id=1, replica_groups=mesh['gx'=4,'gz'=4,'gl'=2] {'gx','gl','gz'}, dimensions={0} | all-to-all | bytes 6553600 | tf_op jit(solution)/shard_map/all_to_all | solution.py:464
  86.9 0.0 copy-done.2
  86.9 0.0 copy-done.3
  87.0 5.4 %shard_map.92 = f32[6144,128]{1,0:T(8,128)S(1)} custom-call(f32[256,256]{1,0:T(8,128)S(1)} %copy-done.2, f32[2,16,128]{2,1,0:T(8,128)S(1)} %copy-done.3, f32[32,200,128]{2,1,0:T(8,128)S(1)} %all_to_all.10.data), custom_call_target="tpu_custom_call" | custom-call | flops 4831838208 | bytes 6291456 | tf_op jit(solution)/shard_map/pallas_call | solution.py:256
  92.3 0.0 copy-start
  92.3 0.0 copy-start.1
  92.3 73.6 %all_to_all.11.data = f32[32,192,128]{2,1,0:T(8,128)S(1)} all-to-all(f32[32,192,128]{2,1,0:T(8,128)S(1)} %bitcast.8), channel_id=1, replica_groups=mesh['gx'=4,'gz'=4,'gl'=2] {'gx','gl','gz'}, dimensions={0} | all-to-all | bytes 6291456 | tf_op jit(solution)/shard_map/all_to_all | solution.py:464
  166.0 0.0 copy-done
  166.0 0.0 copy-done.1
  166.0 8.3 %shard_map.93 = f32[2,3,64,2048]{3,2,1,0:T(8,128)} custom-call(f32[2,32,128]{2,1,0:T(8,128)S(1)} %copy-done.1, f32[256,256]{1,0:T(8,128)S(1)} %copy-done, f32[32,192,128]{2,1,0:T(8,128)S(1)} %all_to_all.11.data, f32[2,6,64,2048]{3,2,1,0:T(8,128)} %bitcast.9), custom_call_target="tpu_custom_call" | custom-call | flops 613416960 | bytes 12582912 | tf_op jit(solution)/shard_map/pallas_call | solution.py:441
Async XLA Ops:
  4.2 82.7 %copy-start.2 = (f32[256,256]{1,0:T(8,128)S(1)}, f32[256,256]{1,0:T(8,128)}, u32[]{:S(2)}) copy-start(f32[256,256]{1,0:T(8,128)} %constant.23.clone.table) | copy-start | bytes 786436
  4.2 82.7 %copy-start.3 = (f32[2,16,128]{2,1,0:T(8,128)S(1)}, f32[2,16,128]{2,1,0:T(8,128)}, u32[]{:S(2)}) copy-start(f32[2,16,128]{2,1,0:T(8,128)} %constant.24.clone.twist) | copy-start | bytes 49156
  92.3 73.6 %copy-start = (f32[256,256]{1,0:T(8,128)S(1)}, f32[256,256]{1,0:T(8,128)}, u32[]{:S(2)}) copy-start(f32[256,256]{1,0:T(8,128)} %constant.26.clone.table) | copy-start | bytes 786436
  92.3 73.6 %copy-start.1 = (f32[2,32,128]{2,1,0:T(8,128)S(1)}, f32[2,32,128]{2,1,0:T(8,128)}, u32[]{:S(2)}) copy-start(f32[2,32,128]{2,1,0:T(8,128)} %constant.25.clone.twist) | copy-start | bytes 98308

commit v6 on v5

--- a/solution.py
+++ b/solution.py
@@ -79,21 +79,23 @@
     return (real * cos_k + imag * sin_k, imag * cos_k - real * sin_k)
 
 
-def place_of(owner, count_gl):
+def place_of(owner, sizes):
+    count_gx, count_gl = sizes
     shift = count_gl.bit_length() - 1
     z = (owner >> shift) & 3
-    return (((owner >> (shift + 2)) << shift) + (owner & (count_gl - 1))) * 4 + z
-
-
-def owner_order(devices, count_gl):
+    return ((owner & (count_gl - 1)) * count_gx + (owner >> (shift + 2))) * 4 + z
+
+
+def owner_order(sizes):
+    devices = 4 * sizes[0] * sizes[1]
     order = [0] * devices
     for owner in range(devices):
-        order[place_of(owner, count_gl)] = owner
+        order[place_of(owner, sizes)] = owner
     return order
 
 
 def pack_kernel(
-    devices, count_gl, per_owner, count, me, owner_row, slot_row, tiles, out, *scratch
+    devices, mesh_sizes, per_owner, count, me, owner_row, slot_row, tiles, out, *scratch
 ):
     held, lists, sems = scratch
     comps = range(tiles.shape[1])
@@ -113,7 +115,7 @@
     before = jnp.where(sender < reader, 1.0, 0.0).astype(jnp.bfloat16)
     live = lax.broadcasted_iota(jnp.int32, (1, listed), 1) < count[0]
     fetches[0].wait()
-    place = jnp.where(live, place_of(lists[0], count_gl), -1)
+    place = jnp.where(live, place_of(lists[0], mesh_sizes), -1)
     place_at = lax.broadcasted_iota(jnp.int32, (devices, listed), 0)
     named = jnp.where(place_at == place, 1.0, 0.0)
     counted = jnp.dot(named.astype(jnp.bfloat16), before, preferred_element_type=jnp.float32)
@@ -143,11 +145,11 @@
             out[:, start : start + per_owner, :] = whole.reshape(devices, per_owner, 128)
 
 
-def pack(tiles, owner_row, slot_row, count, me, devices, count_gl, per_owner):
+def pack(tiles, owner_row, slot_row, count, me, devices, mesh_sizes, per_owner):
     comps, listed = tiles.shape[1:3]
     rows = 2 * comps * per_owner + 8
     return pl.pallas_call(
-        functools.partial(pack_kernel, devices, count_gl, per_owner),
+        functools.partial(pack_kernel, devices, mesh_sizes, per_owner),
         out_shape=pltpu.VMEM((devices, rows, 128), jnp.float32),
         in_specs=[pl.BlockSpec(memory_space=pltpu.SMEM)] * 2
         + [pl.BlockSpec(memory_space=pltpu.HBM)] * 3,
@@ -242,11 +244,11 @@
             along_y(index, start)
 
 
-def slab_waves(data, x_local, blocks, count_gl, per_owner):
+def slab_waves(data, x_local, blocks, mesh_sizes, per_owner):
     devices = data.shape[0]
     count = data.shape[1] // (2 * per_owner)
     fine = angles(128, 128, 128)
-    order = owner_order(devices, count_gl)
+    order = owner_order(mesh_sizes)
     fine = fine.reshape(devices, 128 // devices, 128)[order].reshape(128, 128)
     table = complex_table(np.cos(fine), np.sin(fine))
     twist_angle = angles(blocks, 128, blocks * 128)
@@ -394,19 +396,23 @@
                 if comp > 0:
                     x_third(sizes, comp - 1, block * 128, columns, kept)
     fetch.wait()
-    sends = []
-    for piece in range(made.shape[0]):
+    pieces = made.shape[0]
+
+    def turn(piece):
         for start in range(piece * width, (piece + 1) * width, 128):
             x_third(sizes, 2, start, columns, kept)
+
+    sends = []
+    turn(0)
+    for piece in range(pieces):
+        if piece + 1 < pieces:
+            turn(piece + 1)
         part = pl.ds(piece * width, width)
-
-        @pl.loop(0, y_local // 8, unroll=2)
-        def _(step):
-            rows = pl.ds(pl.multiple_of(step * 8, 8), 8)
+        for step in range(y_local // 8):
+            rows = pl.ds(step * 8, 8)
             for row, pair in enumerate(mix_rows(rows, part, tensor, kept)):
                 for r in range(2):
                     made[piece, r, row, rows, :] = pair[r]
-
         send = pltpu.make_async_copy(made.at[piece], out.at[:, :, :, part], out_sems.at[piece])
         send.start()
         sends.append(send)
@@ -433,10 +439,10 @@
     ]
 
 
-def field(data, green, devices, x_local, y_local, y_cells, count_gl):
+def field(data, green, devices, x_local, y_local, y_cells, mesh_sizes):
     x_cells = devices * x_local
     pieces = 8
-    sizes = (devices, x_local, y_local, y_cells // 128, owner_order(devices, count_gl))
+    sizes = (devices, x_local, y_local, y_cells // 128, owner_order(mesh_sizes))
     plane = (y_local, x_cells)
     return pl.pallas_call(
         functools.partial(field_kernel, sizes),
@@ -457,7 +463,7 @@
     )(*x_tables(devices, x_local, y_cells), in_vmem(data), in_hbm(green))
 
 
-places = ("gx", "gl", "gz")
+places = ("gl", "gx", "gz")
 
 
 def exchange(data):
@@ -466,7 +472,8 @@
 
 def per_device(tiles, tile_owner, tile_slot, tile_count, green):
     count_gl = lax.axis_size("gl")
-    devices = lax.axis_size("gx") * 4 * count_gl
+    mesh_sizes = (lax.axis_size("gx"), count_gl)
+    devices = 4 * mesh_sizes[0] * count_gl
     tile_total, tile_len = tiles.shape[2], tiles.shape[3]
     planes, y_local, x_cells = green.shape[2:]
     y_cells = y_local * devices
@@ -478,9 +485,9 @@
     green = green.reshape(2, 6, y_local, x_cells)
     me = lax.axis_index(places).reshape(1).astype(jnp.int32)
     lists = (owner_row, slot_row, tile_count, me)
-    arrived = exchange(pack(tiles, *lists, devices, count_gl, per_owner))
-    moved = exchange(slab_waves(arrived, x_local, blocks, count_gl, per_owner))
-    mixed = field(moved, green, devices, x_local, y_local, y_cells, count_gl)
+    arrived = exchange(pack(tiles, *lists, devices, mesh_sizes, per_owner))
+    moved = exchange(slab_waves(arrived, x_local, blocks, mesh_sizes, per_owner))
+    mixed = field(moved, green, devices, x_local, y_local, y_cells, mesh_sizes)
     return mixed.reshape(2, 3, planes, y_local, x_cells)
 
 

time: 175 us -> 173 us (0.989)
  blocking collectives: 156 us -> 154 us
    all_to_all x2, blocking collectives: 156 us -> 154 us  [exchange(): return lax.all_to_all(data, places, split_axis=0, concat_axis=0, tiled=True)]
where the time goes in v6:
time: 173 us; the launch traced here: 172 us
  blocking collectives  154 us (89%)
  Pallas kernels  16.3 us (9%)
    all_to_all x2, blocking collectives, exchange(): return lax.all_to_all(data, places, split_axis=0, concat_axis=0, tiled=True)  154 us
    pallas_call x1, Pallas kernels, field(): pl.pallas_call(functools.partial(field_kernel, sizes), out_shape=pltpu.HB...  7.36 us
    pallas_call x1, Pallas kernels, slab_waves(): pl.pallas_call(functools.partial(slab_kernel, count, x_local, blocks, per...  5.36 us
    pallas_call x1, Pallas kernels, pack(): pl.pallas_call(functools.partial(pack_kernel, devices, mesh_sizes, per_ow...  3.56 us

profile of v6, /device:TPU:0, one launch (start us, length us, event | category | flops | bytes accessed | tf_op | source)
XLA Modules:
  0.0 171.6 jit_solution(11991058754630153829)
XLA Ops:
  0.7 3.6 %shard_map.91 = f32[32,200,128]{2,1,0:T(8,128)S(1)} custom-call(s32[1]{0:T(128)S(6)} %copy.11.count, s32[1]{0:T(128)} %bitcast.me, s32[1,512]{1,0:T(1,128)} %bitcast.10, s32[1,512]{1,0:T(1,128)} %bitcast.11, f32[2,3,512,128]{3,2,1,0:T(8,128)} %tiles.1), custom_call_target="tpu_custom_call" | custom-call | flops 1610612736 | bytes 6553600 | tf_op jit(solution)/shard_map/pallas_call | solution.py:151
  4.2 0.0 copy-start.2
  4.2 0.0 copy-start.3
  4.2 82.2 %all_to_all.10.data = f32[32,200,128]{2,1,0:T(8,128)S(1)} all-to-all(f32[32,200,128]{2,1,0:T(8,128)S(1)} %shard_map.91), channel_id=1, replica_groups=mesh['gx'=4,'gz'=4,'gl'=2] {'gl','gx','gz'}, dimensions={0} | all-to-all | bytes 6553600 | tf_op jit(solution)/shard_map/all_to_all | solution.py:470
  86.4 0.0 copy-done.2
  86.4 0.0 copy-done.3
  86.4 5.4 %shard_map.92 = f32[6144,128]{1,0:T(8,128)S(1)} custom-call(f32[256,256]{1,0:T(8,128)S(1)} %copy-done.2, f32[2,16,128]{2,1,0:T(8,128)S(1)} %copy-done.3, f32[32,200,128]{2,1,0:T(8,128)S(1)} %all_to_all.10.data), custom_call_target="tpu_custom_call" | custom-call | flops 4831838208 | bytes 6291456 | tf_op jit(solution)/shard_map/pallas_call | solution.py:258
  91.8 0.0 copy-start
  91.8 0.0 copy-start.1
  91.8 72.3 %all_to_all.11.data = f32[32,192,128]{2,1,0:T(8,128)S(1)} all-to-all(f32[32,192,128]{2,1,0:T(8,128)S(1)} %bitcast.8), channel_id=1, replica_groups=mesh['gx'=4,'gz'=4,'gl'=2] {'gl','gx','gz'}, dimensions={0} | all-to-all | bytes 6291456 | tf_op jit(solution)/shard_map/all_to_all | solution.py:470
  164.1 0.0 copy-done
  164.1 0.0 copy-done.1
  164.1 7.4 %shard_map.93 = f32[2,3,64,2048]{3,2,1,0:T(8,128)} custom-call(f32[2,32,128]{2,1,0:T(8,128)S(1)} %copy-done.1, f32[256,256]{1,0:T(8,128)S(1)} %copy-done, f32[32,192,128]{2,1,0:T(8,128)S(1)} %all_to_all.11.data, f32[2,6,64,2048]{3,2,1,0:T(8,128)} %bitcast.9), custom_call_target="tpu_custom_call" | custom-call | flops 613416960 | bytes 12582912 | tf_op jit(solution)/shard_map/pallas_call | solution.py:447
Async XLA Ops:
  4.2 82.2 %copy-start.2 = (f32[256,256]{1,0:T(8,128)S(1)}, f32[256,256]{1,0:T(8,128)}, u32[]{:S(2)}) copy-start(f32[256,256]{1,0:T(8,128)} %constant.23.clone.table) | copy-start | bytes 786436
  4.2 82.2 %copy-start.3 = (f32[2,16,128]{2,1,0:T(8,128)S(1)}, f32[2,16,128]{2,1,0:T(8,128)}, u32[]{:S(2)}) copy-start(f32[2,16,128]{2,1,0:T(8,128)} %constant.24.clone.twist) | copy-start | bytes 49156
  91.8 72.3 %copy-start = (f32[256,256]{1,0:T(8,128)S(1)}, f32[256,256]{1,0:T(8,128)}, u32[]{:S(2)}) copy-start(f32[256,256]{1,0:T(8,128)} %constant.26.clone.table) | copy-start | bytes 786436
  91.8 72.3 %copy-start.1 = (f32[2,32,128]{2,1,0:T(8,128)S(1)}, f32[2,32,128]{2,1,0:T(8,128)}, u32[]{:S(2)}) copy-start(f32[2,32,128]{2,1,0:T(8,128)} %constant.25.clone.twist) | copy-start | bytes 98308

commit v7 on v6

--- a/solution.py
+++ b/solution.py
@@ -82,8 +82,8 @@
 def place_of(owner, sizes):
     count_gx, count_gl = sizes
     shift = count_gl.bit_length() - 1
-    z = (owner >> shift) & 3
-    return ((owner & (count_gl - 1)) * count_gx + (owner >> (shift + 2))) * 4 + z
+    z, gx = (owner >> shift) & 3, owner >> (shift + 2)
+    return ((owner & (count_gl - 1)) * (count_gx // 2) + (gx >> 1)) * 8 + z * 2 + (gx & 1)
 
 
 def owner_order(sizes):
@@ -274,11 +274,16 @@
     return made.reshape(devices, count * rows // devices, 128)
 
 
-def choose(options, mask_of):
-    made = options[0]
-    for i in range(1, len(options)):
-        made = jnp.where(mask_of(i), options[i], made)
-    return made
+def rotated(pieces, selector):
+    count = len(pieces)
+    step = 1
+    while step < count:
+        taken = (selector & step) != 0
+        pieces = [
+            jnp.where(taken, pieces[(j + step) % count], pieces[j]) for j in range(count)
+        ]
+        step *= 2
+    return pieces
 
 
 def x_first(sizes, comp, step, twist, data, turned):
@@ -314,10 +319,10 @@
             for bank in range(banks):
                 one = moved[bank * x_local : (bank + 1) * x_local, base * narrow :][:, :128]
                 rolled.append(pltpu.roll(one, bank * narrow, 1) if bank else one)
+            made = rotated(rolled, lane >> (narrow.bit_length() - 1))
             for k in range(banks):
-                options = [rolled[(place - k) % banks] for place in range(banks)]
                 rows = pl.ds(start + base + k, x_local, stride=devices)
-                columns[comp, rows, :] = choose(options, lambda i: lane // narrow == i)
+                columns[comp, rows, :] = made[-k % banks]
         return
     for k in range(together):
         one = jnp.concatenate(
@@ -347,11 +352,9 @@
     lane = lax.broadcasted_iota(jnp.int32, (1, 128), 1)
     block = columns[comp, start : start + 128, :].T
     pieces = [block[bank * narrow : (bank + 1) * narrow] for bank in range(banks)]
-    for bank in range(banks):
-        one = pieces[bank]
-        if square(sizes):
-            options = [pieces[(bank + k) % banks] for k in range(banks)]
-            one = choose(options, lambda i: lane % banks == i)
+    if square(sizes):
+        pieces = rotated(pieces, lane & (banks - 1))
+    for bank, one in enumerate(pieces):
         for step in range(steps):
             row = step * blocks + (bank % group) * pairs
             kept[comp, bank // group, row : row + pairs, start : start + 128] = one[
@@ -441,7 +444,7 @@
 
 def field(data, green, devices, x_local, y_local, y_cells, mesh_sizes):
     x_cells = devices * x_local
-    pieces = 8
+    pieces = 16
     sizes = (devices, x_local, y_local, y_cells // 128, owner_order(mesh_sizes))
     plane = (y_local, x_cells)
     return pl.pallas_call(
@@ -463,7 +466,7 @@
     )(*x_tables(devices, x_local, y_cells), in_vmem(data), in_hbm(green))
 
 
-places = ("gl", "gx", "gz")
+places = ("gl", "gy", "gz", "core")
 
 
 def exchange(data):
@@ -472,7 +475,7 @@
 
 def per_device(tiles, tile_owner, tile_slot, tile_count, green):
     count_gl = lax.axis_size("gl")
-    mesh_sizes = (lax.axis_size("gx"), count_gl)
+    mesh_sizes = (lax.axis_size("gy") * 2, count_gl)
     devices = 4 * mesh_sizes[0] * count_gl
     tile_total, tile_len = tiles.shape[2], tiles.shape[3]
     planes, y_local, x_cells = green.shape[2:]
@@ -494,9 +497,9 @@
 def solution(mesh):
     count_gx, count_gy = mesh.devices.shape
     fine_mesh = jax.sharding.Mesh(
-        mesh.devices.reshape(count_gx, 4, count_gy // 4), ("gx", "gz", "gl")
+        mesh.devices.reshape(count_gx // 2, 2, 4, count_gy // 4), ("gy", "core", "gz", "gl")
     )
-    every = ("gx", "gz", "gl")
+    every = ("gy", "core", "gz", "gl")
     in_specs = (
         P(None, None, every, None),
         P(every, None),

time: 173 us -> 175 us (1.012)
  blocking collectives: 154 us -> 157 us
    all_to_all x2, blocking collectives: 154 us -> 157 us  [exchange(): return lax.all_to_all(data, places, split_axis=0, concat_axis=0, tiled=True)]
where the time goes in v7:
time: 175 us; the launch traced here: 174 us
  blocking collectives  157 us (90%)
  Pallas kernels  16.5 us (9%)
    all_to_all x2, blocking collectives, exchange(): return lax.all_to_all(data, places, split_axis=0, concat_axis=0, tiled=True)  157 us
    pallas_call x1, Pallas kernels, field(): pl.pallas_call(functools.partial(field_kernel, sizes), out_shape=pltpu.HB...  7.55 us
    pallas_call x1, Pallas kernels, slab_waves(): pl.pallas_call(functools.partial(slab_kernel, count, x_local, blocks, per...  5.36 us
    pallas_call x1, Pallas kernels, pack(): pl.pallas_call(functools.partial(pack_kernel, devices, mesh_sizes, per_ow...  3.56 us

profile of v7, /device:TPU:0, one launch (start us, length us, event | category | flops | bytes accessed | tf_op | source)
XLA Modules:
  0.0 174.4 jit_solution(13690023053322404268)
XLA Ops:
  0.7 3.6 %shard_map.91 = f32[32,200,128]{2,1,0:T(8,128)S(1)} custom-call(s32[1]{0:T(128)S(6)} %copy.11.count, s32[1]{0:T(128)} %bitcast.me, s32[1,512]{1,0:T(1,128)} %bitcast.10, s32[1,512]{1,0:T(1,128)} %bitcast.11, f32[2,3,512,128]{3,2,1,0:T(8,128)} %tiles.1), custom_call_target="tpu_custom_call" | custom-call | flops 1610612736 | bytes 6553600 | tf_op jit(solution)/shard_map/pallas_call | solution.py:151
  4.2 0.0 copy-start.2
  4.2 0.0 copy-start.3
  4.2 82.4 %all_to_all.10.data = f32[32,200,128]{2,1,0:T(8,128)S(1)} all-to-all(f32[32,200,128]{2,1,0:T(8,128)S(1)} %shard_map.91), channel_id=1, replica_groups=mesh['gy'=2,'core'=2,'gz'=4,'gl'=2] {'gl','gy','gz','core'}, dimensions={0} | all-to-all | bytes 6553600 | tf_op jit(solution)/shard_map/all_to_all | solution.py:473
  86.7 0.0 copy-done.2
  86.7 0.0 copy-done.3
  86.7 5.4 %shard_map.92 = f32[6144,128]{1,0:T(8,128)S(1)} custom-call(f32[256,256]{1,0:T(8,128)S(1)} %copy-done.2, f32[2,16,128]{2,1,0:T(8,128)S(1)} %copy-done.3, f32[32,200,128]{2,1,0:T(8,128)S(1)} %all_to_all.10.data), custom_call_target="tpu_custom_call" | custom-call | flops 4831838208 | bytes 6291456 | tf_op jit(solution)/shard_map/pallas_call | solution.py:258
  92.1 0.0 copy-start
  92.1 0.0 copy-start.1
  92.1 74.6 %all_to_all.11.data = f32[32,192,128]{2,1,0:T(8,128)S(1)} all-to-all(f32[32,192,128]{2,1,0:T(8,128)S(1)} %bitcast.8), channel_id=1, replica_groups=mesh['gy'=2,'core'=2,'gz'=4,'gl'=2] {'gl','gy','gz','core'}, dimensions={0} | all-to-all | bytes 6291456 | tf_op jit(solution)/shard_map/all_to_all | solution.py:473
  166.6 0.0 copy-done
  166.7 0.0 copy-done.1
  166.7 7.5 %shard_map.93 = f32[2,3,64,2048]{3,2,1,0:T(8,128)} custom-call(f32[2,32,128]{2,1,0:T(8,128)S(1)} %copy-done.1, f32[256,256]{1,0:T(8,128)S(1)} %copy-done, f32[32,192,128]{2,1,0:T(8,128)S(1)} %all_to_all.11.data, f32[2,6,64,2048]{3,2,1,0:T(8,128)} %bitcast.9), custom_call_target="tpu_custom_call" | custom-call | flops 613416960 | bytes 12582912 | tf_op jit(solution)/shard_map/pallas_call | solution.py:450
Async XLA Ops:
  4.2 82.5 %copy-start.2 = (f32[256,256]{1,0:T(8,128)S(1)}, f32[256,256]{1,0:T(8,128)}, u32[]{:S(2)}) copy-start(f32[256,256]{1,0:T(8,128)} %constant.29.clone.table) | copy-start | bytes 786436
  4.2 82.5 %copy-start.3 = (f32[2,16,128]{2,1,0:T(8,128)S(1)}, f32[2,16,128]{2,1,0:T(8,128)}, u32[]{:S(2)}) copy-start(f32[2,16,128]{2,1,0:T(8,128)} %constant.30.clone.twist) | copy-start | bytes 49156
  92.1 74.6 %copy-start = (f32[256,256]{1,0:T(8,128)S(1)}, f32[256,256]{1,0:T(8,128)}, u32[]{:S(2)}) copy-start(f32[256,256]{1,0:T(8,128)} %constant.32.clone.table) | copy-start | bytes 786436
  92.1 74.6 %copy-start.1 = (f32[2,32,128]{2,1,0:T(8,128)S(1)}, f32[2,32,128]{2,1,0:T(8,128)}, u32[]{:S(2)}) copy-start(f32[2,32,128]{2,1,0:T(8,128)} %constant.31.clone.twist) | copy-start | bytes 98308

commit v8 on v7

--- a/solution.py
+++ b/solution.py
@@ -82,8 +82,8 @@
 def place_of(owner, sizes):
     count_gx, count_gl = sizes
     shift = count_gl.bit_length() - 1
-    z, gx = (owner >> shift) & 3, owner >> (shift + 2)
-    return ((owner & (count_gl - 1)) * (count_gx // 2) + (gx >> 1)) * 8 + z * 2 + (gx & 1)
+    z = (owner >> shift) & 3
+    return ((owner & (count_gl - 1)) * count_gx + (owner >> (shift + 2))) * 4 + z
 
 
 def owner_order(sizes):
@@ -95,7 +95,7 @@
 
 
 def pack_kernel(
-    devices, mesh_sizes, per_owner, count, me, owner_row, slot_row, tiles, out, *scratch
+    devices, mesh_sizes, per_owner, count, owner_row, slot_row, tiles, out, table, *scratch
 ):
     held, lists, sems = scratch
     comps = range(tiles.shape[1])
@@ -125,14 +125,15 @@
     chosen = jnp.where(target_at == target, 1.0, 0.0).astype(jnp.bfloat16)
     fetches[1].wait()
     stated = lists[1] + 1
-    lane = rank + (me[0] & (128 // per_owner - 1)) * per_owner
+    every = 128 // per_owner
+    lane = jnp.where(live, rank + (place & (every - 1)) * per_owner, -1)
     lane_at = lax.broadcasted_iota(jnp.int32, (128, listed), 0)
     laned = jnp.where(lane_at == lane, 1.0, 0.0).astype(jnp.bfloat16)
-    coarse = (named * (stated >> 5).astype(jnp.float32)).astype(jnp.bfloat16)
-    fine = (named * (stated & 31).astype(jnp.float32)).astype(jnp.bfloat16)
-    slots = 32.0 * dot_rows(coarse, laned) + dot_rows(fine, laned)
-    start = 2 * len(comps) * per_owner
-    out[:, start:, :] = jnp.broadcast_to(slots[:, None, :], (devices, 8, 128))
+    row_at = lax.broadcasted_iota(jnp.int32, (8, listed), 0)
+    rowed = jnp.where(row_at == place >> (every.bit_length() - 1), 1.0, 0.0)
+    coarse = (rowed * (stated >> 5).astype(jnp.float32)).astype(jnp.bfloat16)
+    fine = (rowed * (stated & 31).astype(jnp.float32)).astype(jnp.bfloat16)
+    table[...] = 32.0 * dot_rows(coarse, laned) + dot_rows(fine, laned)
     for i in range(len(comps)):
         fetches[2 + i].wait()
         parts = [part for r in range(2) for part in split_two(held[i, r])]
@@ -145,15 +146,19 @@
             out[:, start : start + per_owner, :] = whole.reshape(devices, per_owner, 128)
 
 
-def pack(tiles, owner_row, slot_row, count, me, devices, mesh_sizes, per_owner):
+def pack(tiles, owner_row, slot_row, count, devices, mesh_sizes, per_owner):
     comps, listed = tiles.shape[1:3]
-    rows = 2 * comps * per_owner + 8
+    rows = 2 * comps * per_owner
+    assert devices * per_owner == 1024
     return pl.pallas_call(
         functools.partial(pack_kernel, devices, mesh_sizes, per_owner),
-        out_shape=pltpu.VMEM((devices, rows, 128), jnp.float32),
-        in_specs=[pl.BlockSpec(memory_space=pltpu.SMEM)] * 2
+        out_shape=(
+            pltpu.VMEM((devices, rows, 128), jnp.float32),
+            jax.ShapeDtypeStruct((8, 128), jnp.float32),
+        ),
+        in_specs=[pl.BlockSpec(memory_space=pltpu.SMEM)]
         + [pl.BlockSpec(memory_space=pltpu.HBM)] * 3,
-        out_specs=pl.BlockSpec(memory_space=pltpu.VMEM),
+        out_specs=(pl.BlockSpec(memory_space=pltpu.VMEM),) * 2,
         scratch_shapes=[
             pltpu.VMEM((comps, 2, listed, 128), jnp.float32),
             pltpu.VMEM((2, 1, listed), jnp.int32),
@@ -163,7 +168,7 @@
         cost_estimate=cost(
             devices * per_owner * listed * 512 * 2 * comps, devices * rows * 1024
         ),
-    )(count, me, *[in_hbm(a) for a in (owner_row, slot_row, tiles)])
+    )(count, *[in_hbm(a) for a in (owner_row, slot_row, tiles)])
 
 
 def complex_table(cos_part, sin_part):
@@ -175,7 +180,9 @@
     ).astype(np.float32)
 
 
-def slab_kernel(count, x_local, blocks, per_owner, table, twist, data, out, *scratch):
+def slab_kernel(
+    count, x_local, blocks, per_owner, order, me, slots, table, twist, data, out, *scratch
+):
     chosen, slab, turned = scratch
     devices = data.shape[0]
     entries = devices * per_owner
@@ -183,10 +190,17 @@
     pairs = blocks // group
     shift = blocks.bit_length() - 1
     every = 128 // per_owner
-    stated = [
-        sum([data[o, data.shape[1] - 8 :][:1] for o in range(start, start + every)])
-        for start in range(0, devices, every)
-    ]
+    lane = lax.broadcasted_iota(jnp.int32, (1, 128), 1)
+    mine = me[0] & (every - 1)
+    row = me[0] >> (every.bit_length() - 1)
+    stated = []
+    for start in range(0, devices, every):
+        whole = None
+        for i in range(every):
+            one = slots[order[start + i] ^ me[1], pl.ds(row, 1), :]
+            one = pltpu.roll(one, ((i + every - mine) & (every - 1)) * per_owner, 1)
+            whole = one if i == 0 else jnp.where(lane // per_owner == i, one, whole)
+        stated.append(whole)
     slot = jnp.concatenate(stated, axis=1).astype(jnp.int32) - 1
     landing = jnp.where(slot >= 0, (slot & (blocks - 1)) * x_local + (slot >> shift), -1)
     slab_rows = blocks * x_local
@@ -244,7 +258,7 @@
             along_y(index, start)
 
 
-def slab_waves(data, x_local, blocks, mesh_sizes, per_owner):
+def slab_waves(data, me, slots, x_local, blocks, mesh_sizes, per_owner):
     devices = data.shape[0]
     count = data.shape[1] // (2 * per_owner)
     fine = angles(128, 128, 128)
@@ -256,9 +270,10 @@
     entries = devices * per_owner
     rows = blocks * x_local * 2
     made = pl.pallas_call(
-        functools.partial(slab_kernel, count, x_local, blocks, per_owner),
+        functools.partial(slab_kernel, count, x_local, blocks, per_owner, order),
         out_shape=pltpu.VMEM((count * rows, 128), jnp.float32),
-        in_specs=[pl.BlockSpec(memory_space=pltpu.VMEM)] * 3,
+        in_specs=[pl.BlockSpec(memory_space=pltpu.SMEM)]
+        + [pl.BlockSpec(memory_space=pltpu.VMEM)] * 4,
         out_specs=pl.BlockSpec(memory_space=pltpu.VMEM),
         scratch_shapes=[
             pltpu.VMEM((blocks * x_local, entries), jnp.bfloat16),
@@ -270,7 +285,7 @@
             count * blocks * x_local * (entries * 1024 + 512 * 1024),
             count * (entries * 1024 + rows * 512),
         ),
-    )(jnp.asarray(table), jnp.asarray(twist), in_vmem(data))
+    )(me, slots, jnp.asarray(table), jnp.asarray(twist), in_vmem(data))
     return made.reshape(devices, count * rows // devices, 128)
 
 
@@ -444,7 +459,7 @@
 
 def field(data, green, devices, x_local, y_local, y_cells, mesh_sizes):
     x_cells = devices * x_local
-    pieces = 16
+    pieces = 8
     sizes = (devices, x_local, y_local, y_cells // 128, owner_order(mesh_sizes))
     plane = (y_local, x_cells)
     return pl.pallas_call(
@@ -466,7 +481,16 @@
     )(*x_tables(devices, x_local, y_cells), in_vmem(data), in_hbm(green))
 
 
-places = ("gl", "gy", "gz", "core")
+places = ("gl", "gx", "gz")
+
+
+def gather_tables(table, axes, devices):
+    tables, mask = table[None], 1
+    while mask < devices:
+        pairs = [(d, d ^ mask) for d in range(devices)]
+        tables = jnp.concatenate([tables, lax.ppermute(tables, axes, pairs)])
+        mask *= 2
+    return tables
 
 
 def exchange(data):
@@ -475,7 +499,7 @@
 
 def per_device(tiles, tile_owner, tile_slot, tile_count, green):
     count_gl = lax.axis_size("gl")
-    mesh_sizes = (lax.axis_size("gy") * 2, count_gl)
+    mesh_sizes = (lax.axis_size("gx"), count_gl)
     devices = 4 * mesh_sizes[0] * count_gl
     tile_total, tile_len = tiles.shape[2], tiles.shape[3]
     planes, y_local, x_cells = green.shape[2:]
@@ -486,10 +510,12 @@
     assert planes == 1 and tile_len == 128
     owner_row, slot_row = tile_owner.reshape(1, tile_total), tile_slot.reshape(1, tile_total)
     green = green.reshape(2, 6, y_local, x_cells)
-    me = lax.axis_index(places).reshape(1).astype(jnp.int32)
-    lists = (owner_row, slot_row, tile_count, me)
-    arrived = exchange(pack(tiles, *lists, devices, mesh_sizes, per_owner))
-    moved = exchange(slab_waves(arrived, x_local, blocks, mesh_sizes, per_owner))
+    owners = ("gx", "gz", "gl")
+    me = jnp.stack([lax.axis_index(places), lax.axis_index(owners)]).astype(jnp.int32)
+    lists = (owner_row, slot_row, tile_count)
+    packed, slots = pack(tiles, *lists, devices, mesh_sizes, per_owner)
+    arrived, slots = exchange(packed), gather_tables(slots, owners, devices)
+    moved = exchange(slab_waves(arrived, me, slots, x_local, blocks, mesh_sizes, per_owner))
     mixed = field(moved, green, devices, x_local, y_local, y_cells, mesh_sizes)
     return mixed.reshape(2, 3, planes, y_local, x_cells)
 
@@ -497,9 +523,9 @@
 def solution(mesh):
     count_gx, count_gy = mesh.devices.shape
     fine_mesh = jax.sharding.Mesh(
-        mesh.devices.reshape(count_gx // 2, 2, 4, count_gy // 4), ("gy", "core", "gz", "gl")
+        mesh.devices.reshape(count_gx, 4, count_gy // 4), ("gx", "gz", "gl")
     )
-    every = ("gy", "core", "gz", "gl")
+    every = ("gx", "gz", "gl")
     in_specs = (
         P(None, None, every, None),
         P(every, None),

time: 175 us -> 180 us (1.029)
  blocking collectives: 157 us -> 73.4 us
  waiting for transfers between devices: 0 us -> 65.9 us
  starting transfers between devices: 0 us -> 16.7 us
  local copies, waits for them, and re-layouts: 0.03 us -> 5.39 us
    all_to_all x2 -> x1, blocking collectives: 157 us -> 73.4 us  [exchange(): return lax.all_to_all(data, places, split_axis=0, concat_axis=0, tiled=True)]
    ppermute x0 -> x5, waiting for transfers between devices: none -> 65.9 us  [gather_tables(): tables = jnp.concatenate([tables, lax.ppermute(tables, axes, pairs)])]
    ppermute x0 -> x5, starting transfers between devices: none -> 9.35 us  [gather_tables(): tables = jnp.concatenate([tables, lax.ppermute(tables, axes, pairs)])]
    all_to_all x0 -> x1, starting transfers between devices: none -> 7.3 us  [exchange(): return lax.all_to_all(data, places, split_axis=0, concat_axis=0, tiled=True)]
    unnamed x8 -> x14, local copies, waits for them, and re-layouts: 0.03 us -> 4.77 us
  transfers between devices with their start and end apart: 0 -> 6, of which waited for: 0 -> 5; matrix products, arithmetic and copies ran while one was open for 0% -> 2% of each run, Pallas kernels for 0% -> 0%
where the time goes in v8:
time: 180 us; the launch traced here: 179 us
  blocking collectives  73.4 us (41%)
  waiting for transfers between devices  65.9 us (37%)
  Pallas kernels  16.8 us (9%)
  starting transfers between devices  16.7 us (9%)
  local copies, waits for them, and re-layouts  5.39 us (3%)
    all_to_all x1, blocking collectives, exchange(): return lax.all_to_all(data, places, split_axis=0, concat_axis=0, tiled=True)  73.4 us
    ppermute x5, waiting for transfers between devices, gather_tables(): tables = jnp.concatenate([tables, lax.ppermute(tables, axes, pairs)])  65.9 us
    ppermute x5, starting transfers between devices, gather_tables(): tables = jnp.concatenate([tables, lax.ppermute(tables, axes, pairs)])  9.35 us
    all_to_all x1, starting transfers between devices, exchange(): return lax.all_to_all(data, places, split_axis=0, concat_axis=0, tiled=True)  7.3 us
    pallas_call x1, Pallas kernels, field(): pl.pallas_call(functools.partial(field_kernel, sizes), out_shape=pltpu.HB...  7.3 us
    pallas_call x1, Pallas kernels, slab_waves(): pl.pallas_call(functools.partial(slab_kernel, count, x_local, blocks, per...  5.95 us
    unnamed x14, local copies, waits for them, and re-layouts  4.77 us
  transfers between devices with their start and end apart: 6, of which 5 were waited for; matrix products, arithmetic and copies ran while one was open for 2% of the time, Pallas kernels for 0%

profile of v8, /device:TPU:0, one launch (start us, length us, event | category | flops | bytes accessed | tf_op | source)
XLA Modules:
  0.0 179.1 jit_solution(15085674816546997612)
XLA Ops:
  0.7 3.5 %shard_map.91 = (f32[32,192,128]{2,1,0:T(8,128)S(1)}, f32[8,128]{1,0:T(8,128)S(1)}) custom-call(s32[1]{0:T(128)S(6)} %copy.20.count, s32[1,512]{1,0:T(1,128)} %bitcast.18, s32[1,512]{1,0:T(1,128)} %bitcast.19, f32[2,3,512,128]{3,2,1,0:T(8,128)} %tiles.1), custom_call_target="tpu_custom_call" | custom-call | flops 1610612736 | bytes 6291456 | tf_op jit(solution)/shard_map/pallas_call | solution.py:153
  4.2 0.0 copy-start
  4.2 1.7 copy-done
  5.9 0.0 copy-start.3
  5.9 7.3 %all-to-all-start = ((f32[32,192,128]{2,1,0:T(8,128)}), f32[32,192,128]{2,1,0:T(8,128)S(1)}, u32[]{:S(2)}, u32[]{:S(2)}) async-start(f32[32,192,128]{2,1,0:T(8,128)} %copy-done), calls=%async_computation | async-start | bytes 6291456 | tf_op jit(solution)/shard_map/all_to_all | solution.py:497
  13.2 1.8 %collective-permute-start = (f32[1,8,128]{2,1,0:T(8,128)S(1)}, f32[1,8,128]{2,1,0:T(8,128)S(1)}, u32[]{:S(2)}, u32[]{:S(2)}) collective-permute-start(f32[1,8,128]{2,1,0:T(8,128)S(1)} %bitcast.13), channel_id=1, source_target_pairs={{0,1},{1,0},{2,3},{3,2},{4,5},{5,4},{6,7},{7,6},{8,9},{9,8},{10,11... | collective-permute-start | bytes 12296 | tf_op jit(solution)/shard_map/ppermute | solution.py:491
  15.0 0.6 constant_dynamic-update-slice_fusion.4
  15.6 12.9 %collective-permute-done = f32[1,8,128]{2,1,0:T(8,128)S(1)} collective-permute-done((f32[1,8,128]{2,1,0:T(8,128)S(1)}, f32[1,8,128]{2,1,0:T(8,128)S(1)}, u32[]{:S(2)}, u32[]{:S(2)}) %collective-permute-start) | collective-permute-done | bytes 4128 | tf_op jit(solution)/shard_map/ppermute | solution.py:491
  28.5 1.9 %collective-permute-start.1 = (f32[2,8,128]{2,1,0:T(8,128)S(1)}, f32[2,8,128]{2,1,0:T(8,128)S(1)}, u32[]{:S(2)}, u32[]{:S(2)}) collective-permute-start(f32[2,8,128]{2,1,0:T(8,128)S(1)} %pad_maximum_fusion.2), channel_id=1, source_target_pairs={{0,2},{1,3},{2,0},{3,1},{4,6},{5,7},{6,4},{7,5},{8,10},{9,11},{10,... | collective-permute-start | bytes 24584 | tf_op jit(solution)/shard_map/ppermute | solution.py:491
  30.4 0.6 constant_dynamic-update-slice_fusion.3
  31.0 34.7 %collective-permute-done.1 = f32[2,8,128]{2,1,0:T(8,128)S(1)} collective-permute-done((f32[2,8,128]{2,1,0:T(8,128)S(1)}, f32[2,8,128]{2,1,0:T(8,128)S(1)}, u32[]{:S(2)}, u32[]{:S(2)}) %collective-permute-start.1) | collective-permute-done | bytes 8224 | tf_op jit(solution)/shard_map/ppermute | solution.py:491
  65.7 4.1 %collective-permute-start.2 = (f32[4,8,128]{2,1,0:T(8,128)S(1)}, f32[4,8,128]{2,1,0:T(8,128)S(1)}, u32[]{:S(2)}, u32[]{:S(2)}) collective-permute-start(f32[4,8,128]{2,1,0:T(8,128)S(1)} %pad_maximum_fusion.1), channel_id=1, source_target_pairs={{0,4},{1,5},{2,6},{3,7},{4,0},{5,1},{6,2},{7,3},{8,12},{9,13},{10,... | collective-permute-start | bytes 49160 | tf_op jit(solution)/shard_map/ppermute | solution.py:491
  69.8 0.6 constant_dynamic-update-slice_fusion.2
  70.4 14.8 %collective-permute-done.2 = f32[4,8,128]{2,1,0:T(8,128)S(1)} collective-permute-done((f32[4,8,128]{2,1,0:T(8,128)S(1)}, f32[4,8,128]{2,1,0:T(8,128)S(1)}, u32[]{:S(2)}, u32[]{:S(2)}) %collective-permute-start.2) | collective-permute-done | bytes 16416 | tf_op jit(solution)/shard_map/ppermute | solution.py:491
  85.2 0.0 collective-permute-start.3
  85.2 0.6 constant_dynamic-update-slice_fusion.1
  85.8 0.6 collective-permute-done.3
  86.4 0.6 constant_dynamic-update-slice_fusion
  87.0 1.5 collective-permute-start.4
  88.5 0.1 pad_add_fusion.me
  88.6 2.9 %collective-permute-done.4 = f32[16,8,128]{2,1,0:T(8,128)S(1)} collective-permute-done((f32[16,8,128]{2,1,0:T(8,128)}, f32[16,8,128]{2,1,0:T(8,128)S(1)}, u32[]{:S(2)}, u32[]{:S(2)}) %collective-permute-start.4) | collective-permute-done | bytes 65568 | tf_op jit(solution)/shard_map/ppermute | solution.py:491
  91.5 0.0 all-to-all-done.data
  91.5 0.0 copy-done.3
  91.5 0.0 copy-start.4
  91.5 0.7 copy-done.4
  92.2 5.9 %shard_map.92 = f32[6144,128]{1,0:T(8,128)S(1)} custom-call(s32[2]{0:T(128)S(1)} %pad_add_fusion.me, f32[32,8,128]{2,1,0:T(8,128)S(1)} %constant_dynamic-update-slice_fusion.5.slots, f32[256,256]{1,0:T(8,128)S(1)} %copy-done.3, f32[2,16,128]{2,1,0:T(8,128)S(1)} %copy-done.4, f32[32,192,128]{2,1,0:T(8,128)S(1)} %all-to-all-done.data), custom_call_target="tpu_custom_call" | custom-call | flops 4831838208 | bytes 6291456 | tf_op jit(solution)/shard_map/pallas_call | solution.py:272
  98.2 0.0 copy-start.1
  98.2 0.0 copy-start.2
  98.2 73.4 %all_to_all.10.data = f32[32,192,128]{2,1,0:T(8,128)S(1)} all-to-all(f32[32,192,128]{2,1,0:T(8,128)S(1)} %bitcast.12), channel_id=1, replica_groups=mesh['gx'=4,'gz'=4,'gl'=2] {'gl','gx','gz'}, dimensions={0} | all-to-all | bytes 6291456 | tf_op jit(solution)/shard_map/all_to_all | solution.py:497
  171.6 0.0 copy-done.1
  171.6 0.0 copy-done.2
  171.6 7.3 %shard_map.93 = f32[2,3,64,2048]{3,2,1,0:T(8,128)} custom-call(f32[2,32,128]{2,1,0:T(8,128)S(1)} %copy-done.2, f32[256,256]{1,0:T(8,128)S(1)} %copy-done.1, f32[32,192,128]{2,1,0:T(8,128)S(1)} %all_to_all.10.data, f32[2,6,64,2048]{3,2,1,0:T(8,128)} %bitcast.17), custom_call_target="tpu_custom_call" | custom-call | flops 613416960 | bytes 12582912 | tf_op jit(solution)/shard_map/pallas_call | solution.py:465
  (4 shorter events, 0.0 us)
Async XLA Ops:
  4.2 1.7 copy-start
  5.9 85.6 %copy-start.3 = (f32[256,256]{1,0:T(8,128)S(1)}, f32[256,256]{1,0:T(8,128)}, u32[]{:S(2)}) copy-start(f32[256,256]{1,0:T(8,128)} %constant.27.clone.table) | copy-start | bytes 786436
  5.9 85.6 %all-to-all-start = ((f32[32,192,128]{2,1,0:T(8,128)}), f32[32,192,128]{2,1,0:T(8,128)S(1)}, u32[]{:S(2)}, u32[]{:S(2)}) async-start(f32[32,192,128]{2,1,0:T(8,128)} %copy-done), calls=%async_computation | async-start | bytes 6291456 | tf_op jit(solution)/shard_map/all_to_all | solution.py:497
  13.2 15.4 %collective-permute-start = (f32[1,8,128]{2,1,0:T(8,128)S(1)}, f32[1,8,128]{2,1,0:T(8,128)S(1)}, u32[]{:S(2)}, u32[]{:S(2)}) collective-permute-start(f32[1,8,128]{2,1,0:T(8,128)S(1)} %bitcast.13), channel_id=1, source_target_pairs={{0,1},{1,0},{2,3},{3,2},{4,5},{5,4},{6,7},{7,6},{8,9},{9,8},{10,11... | collective-permute-start | bytes 12296 | tf_op jit(solution)/shard_map/ppermute | solution.py:491
  28.5 37.2 %collective-permute-start.1 = (f32[2,8,128]{2,1,0:T(8,128)S(1)}, f32[2,8,128]{2,1,0:T(8,128)S(1)}, u32[]{:S(2)}, u32[]{:S(2)}) collective-permute-start(f32[2,8,128]{2,1,0:T(8,128)S(1)} %pad_maximum_fusion.2), channel_id=1, source_target_pairs={{0,2},{1,3},{2,0},{3,1},{4,6},{5,7},{6,4},{7,5},{8,10},{9,11},{10,... | collective-permute-start | bytes 24584 | tf_op jit(solution)/shard_map/ppermute | solution.py:491
  65.7 19.5 %collective-permute-start.2 = (f32[4,8,128]{2,1,0:T(8,128)S(1)}, f32[4,8,128]{2,1,0:T(8,128)S(1)}, u32[]{:S(2)}, u32[]{:S(2)}) collective-permute-start(f32[4,8,128]{2,1,0:T(8,128)S(1)} %pad_maximum_fusion.1), channel_id=1, source_target_pairs={{0,4},{1,5},{2,6},{3,7},{4,0},{5,1},{6,2},{7,3},{8,12},{9,13},{10,... | collective-permute-start | bytes 49160 | tf_op jit(solution)/shard_map/ppermute | solution.py:491
  85.2 1.2 collective-permute-start.3
  87.0 4.5 %collective-permute-start.4 = (f32[16,8,128]{2,1,0:T(8,128)}, f32[16,8,128]{2,1,0:T(8,128)S(1)}, u32[]{:S(2)}, u32[]{:S(2)}) collective-permute-start(f32[16,8,128]{2,1,0:T(8,128)} %get-tuple-element.9), channel_id=1, source_target_pairs={{0,16},{1,17},{2,18},{3,19},{4,20},{5,21},{6,22},{7,23},{8,24},{9,... | collective-permute-start | bytes 196616 | tf_op jit(solution)/shard_map/ppermute | solution.py:491
  91.5 0.7 copy-start.4
  98.2 73.4 %copy-start.1 = (f32[256,256]{1,0:T(8,128)S(1)}, f32[256,256]{1,0:T(8,128)}, u32[]{:S(2)}) copy-start(f32[256,256]{1,0:T(8,128)} %constant.30.clone.table) | copy-start | bytes 786436
  98.2 73.4 %copy-start.2 = (f32[2,32,128]{2,1,0:T(8,128)S(1)}, f32[2,32,128]{2,1,0:T(8,128)}, u32[]{:S(2)}) copy-start(f32[2,32,128]{2,1,0:T(8,128)} %constant.29.clone.twist) | copy-start | bytes 98308

commit v9 on v7

--- a/solution.py
+++ b/solution.py
@@ -82,8 +82,8 @@
 def place_of(owner, sizes):
     count_gx, count_gl = sizes
     shift = count_gl.bit_length() - 1
-    z, gx = (owner >> shift) & 3, owner >> (shift + 2)
-    return ((owner & (count_gl - 1)) * (count_gx // 2) + (gx >> 1)) * 8 + z * 2 + (gx & 1)
+    z = (owner >> shift) & 3
+    return ((owner & (count_gl - 1)) * count_gx + (owner >> (shift + 2))) * 4 + z
 
 
 def owner_order(sizes):
@@ -190,8 +190,6 @@
     slot = jnp.concatenate(stated, axis=1).astype(jnp.int32) - 1
     landing = jnp.where(slot >= 0, (slot & (blocks - 1)) * x_local + (slot >> shift), -1)
     slab_rows = blocks * x_local
-    place = lax.broadcasted_iota(jnp.int32, (slab_rows, entries), 0)
-    chosen[...] = jnp.where(place == landing, 1.0, 0.0).astype(jnp.bfloat16)
     stacked = stacked_halves(table)
     step_rows = slab_rows // 2
 
@@ -231,8 +229,17 @@
                 base = (index * 2 + r) * pairs + start + k
                 out[pl.ds(base, 128, stride=count * 2 * pairs), :] = one
 
+    def choose(half):
+        start = half * step_rows
+        place = start + lax.broadcasted_iota(jnp.int32, (step_rows, entries), 0)
+        chosen[pl.ds(start, step_rows), :] = jnp.where(place == landing, 1.0, 0.0).astype(
+            jnp.bfloat16
+        )
+
     steps = x_local // 8
+    choose(0)
     scatter(0, 0)
+    choose(1)
     scatter(0, 1)
     for index in range(count):
         for half in range(2):
@@ -392,7 +399,8 @@
     groups = devices // together
     blocks_each = x_cells // 128 // groups
     for comp in range(3):
-        pl.loop(0, steps)(lambda i: x_first(sizes, comp, i, twist, data, turned))
+        unroll = 2 if steps % 2 == 0 else 1
+        pl.loop(0, steps, unroll=unroll)(lambda i: x_first(sizes, comp, i, twist, data, turned))
         for i in range(groups):
             x_second(sizes, comp, i, together, stacked, turned, columns)
             for block in range(i * blocks_each, (i + 1) * blocks_each):
@@ -444,7 +452,7 @@
 
 def field(data, green, devices, x_local, y_local, y_cells, mesh_sizes):
     x_cells = devices * x_local
-    pieces = 16
+    pieces = 8
     sizes = (devices, x_local, y_local, y_cells // 128, owner_order(mesh_sizes))
     plane = (y_local, x_cells)
     return pl.pallas_call(
@@ -466,7 +474,7 @@
     )(*x_tables(devices, x_local, y_cells), in_vmem(data), in_hbm(green))
 
 
-places = ("gl", "gy", "gz", "core")
+places = ("gl", "gx", "gz")
 
 
 def exchange(data):
@@ -475,7 +483,7 @@
 
 def per_device(tiles, tile_owner, tile_slot, tile_count, green):
     count_gl = lax.axis_size("gl")
-    mesh_sizes = (lax.axis_size("gy") * 2, count_gl)
+    mesh_sizes = (lax.axis_size("gx"), count_gl)
     devices = 4 * mesh_sizes[0] * count_gl
     tile_total, tile_len = tiles.shape[2], tiles.shape[3]
     planes, y_local, x_cells = green.shape[2:]
@@ -497,9 +505,9 @@
 def solution(mesh):
     count_gx, count_gy = mesh.devices.shape
     fine_mesh = jax.sharding.Mesh(
-        mesh.devices.reshape(count_gx // 2, 2, 4, count_gy // 4), ("gy", "core", "gz", "gl")
+        mesh.devices.reshape(count_gx, 4, count_gy // 4), ("gx", "gz", "gl")
     )
-    every = ("gy", "core", "gz", "gl")
+    every = ("gx", "gz", "gl")
     in_specs = (
         P(None, None, every, None),
         P(every, None),

time: 175 us -> 173 us (0.989)
  blocking collectives: 157 us -> 154 us
    all_to_all x2, blocking collectives: 157 us -> 154 us  [exchange(): return lax.all_to_all(data, places, split_axis=0, concat_axis=0, tiled=True)]
where the time goes in v9:
time: 173 us; the launch traced here: 172 us
  blocking collectives  154 us (89%)
  Pallas kernels  16.2 us (9%)
    all_to_all x2, blocking collectives, exchange(): return lax.all_to_all(data, places, split_axis=0, concat_axis=0, tiled=True)  154 us
    pallas_call x1, Pallas kernels, field(): pl.pallas_call(functools.partial(field_kernel, sizes), out_shape=pltpu.HB...  7.24 us
    pallas_call x1, Pallas kernels, slab_waves(): pl.pallas_call(functools.partial(slab_kernel, count, x_local, blocks, per...  5.39 us
    pallas_call x1, Pallas kernels, pack(): pl.pallas_call(functools.partial(pack_kernel, devices, mesh_sizes, per_ow...  3.56 us

profile of v9, /device:TPU:0, one launch (start us, length us, event | category | flops | bytes accessed | tf_op | source)
XLA Modules:
  0.0 171.6 jit_solution(1827522025646785812)
XLA Ops:
  0.7 3.6 %shard_map.91 = f32[32,200,128]{2,1,0:T(8,128)S(1)} custom-call(s32[1]{0:T(128)S(6)} %copy.11.count, s32[1]{0:T(128)} %bitcast.me, s32[1,512]{1,0:T(1,128)} %bitcast.10, s32[1,512]{1,0:T(1,128)} %bitcast.11, f32[2,3,512,128]{3,2,1,0:T(8,128)} %tiles.1), custom_call_target="tpu_custom_call" | custom-call | flops 1610612736 | bytes 6553600 | tf_op jit(solution)/shard_map/pallas_call | solution.py:151
  4.2 0.0 copy-start.2
  4.2 0.0 copy-start.3
  4.2 82.2 %all_to_all.10.data = f32[32,200,128]{2,1,0:T(8,128)S(1)} all-to-all(f32[32,200,128]{2,1,0:T(8,128)S(1)} %shard_map.91), channel_id=1, replica_groups=mesh['gx'=4,'gz'=4,'gl'=2] {'gl','gx','gz'}, dimensions={0} | all-to-all | bytes 6553600 | tf_op jit(solution)/shard_map/all_to_all | solution.py:481
  86.4 0.0 copy-done.2
  86.4 0.0 copy-done.3
  86.4 5.4 %shard_map.92 = f32[6144,128]{1,0:T(8,128)S(1)} custom-call(f32[256,256]{1,0:T(8,128)S(1)} %copy-done.2, f32[2,16,128]{2,1,0:T(8,128)S(1)} %copy-done.3, f32[32,200,128]{2,1,0:T(8,128)S(1)} %all_to_all.10.data), custom_call_target="tpu_custom_call" | custom-call | flops 4831838208 | bytes 6291456 | tf_op jit(solution)/shard_map/pallas_call | solution.py:265
  91.8 0.0 copy-start
  91.8 0.0 copy-start.1
  91.8 72.3 %all_to_all.11.data = f32[32,192,128]{2,1,0:T(8,128)S(1)} all-to-all(f32[32,192,128]{2,1,0:T(8,128)S(1)} %bitcast.8), channel_id=1, replica_groups=mesh['gx'=4,'gz'=4,'gl'=2] {'gl','gx','gz'}, dimensions={0} | all-to-all | bytes 6291456 | tf_op jit(solution)/shard_map/all_to_all | solution.py:481
  164.1 0.0 copy-done
  164.2 0.0 copy-done.1
  164.2 7.2 %shard_map.93 = f32[2,3,64,2048]{3,2,1,0:T(8,128)} custom-call(f32[2,32,128]{2,1,0:T(8,128)S(1)} %copy-done.1, f32[256,256]{1,0:T(8,128)S(1)} %copy-done, f32[32,192,128]{2,1,0:T(8,128)S(1)} %all_to_all.11.data, f32[2,6,64,2048]{3,2,1,0:T(8,128)} %bitcast.9), custom_call_target="tpu_custom_call" | custom-call | flops 613416960 | bytes 12582912 | tf_op jit(solution)/shard_map/pallas_call | solution.py:458
Async XLA Ops:
  4.2 82.2 %copy-start.2 = (f32[256,256]{1,0:T(8,128)S(1)}, f32[256,256]{1,0:T(8,128)}, u32[]{:S(2)}) copy-start(f32[256,256]{1,0:T(8,128)} %constant.23.clone.table) | copy-start | bytes 786436
  4.2 82.2 %copy-start.3 = (f32[2,16,128]{2,1,0:T(8,128)S(1)}, f32[2,16,128]{2,1,0:T(8,128)}, u32[]{:S(2)}) copy-start(f32[2,16,128]{2,1,0:T(8,128)} %constant.24.clone.twist) | copy-start | bytes 49156
  91.8 72.3 %copy-start = (f32[256,256]{1,0:T(8,128)S(1)}, f32[256,256]{1,0:T(8,128)}, u32[]{:S(2)}) copy-start(f32[256,256]{1,0:T(8,128)} %constant.26.clone.table) | copy-start | bytes 786436
  91.8 72.3 %copy-start.1 = (f32[2,32,128]{2,1,0:T(8,128)S(1)}, f32[2,32,128]{2,1,0:T(8,128)}, u32[]{:S(2)}) copy-start(f32[2,32,128]{2,1,0:T(8,128)} %constant.25.clone.twist) | copy-start | bytes 98308

commit v10 on v9

--- a/solution.py
+++ b/solution.py
@@ -191,19 +191,17 @@
     landing = jnp.where(slot >= 0, (slot & (blocks - 1)) * x_local + (slot >> shift), -1)
     slab_rows = blocks * x_local
     stacked = stacked_halves(table)
-    step_rows = slab_rows // 2
-
-    def scatter(index, half):
+
+    def scatter(index):
         parts = []
         for r in range(2):
             start = (2 * index + r) * per_owner
             parts.extend(split_two(data[:, start : start + per_owner, :].reshape(entries, 128)))
-        rows = pl.ds(half * step_rows, step_rows)
         got = jnp.dot(
-            chosen[rows, :], jnp.concatenate(parts, axis=1), preferred_element_type=jnp.float32
+            chosen[...], jnp.concatenate(parts, axis=1), preferred_element_type=jnp.float32
         )
         for r in range(2):
-            slab[index, r, rows, :] = (
+            slab[index, r] = (
                 got[:, 256 * r : 256 * r + 128] + got[:, 256 * r + 128 : 256 * r + 256]
             )
 
@@ -229,24 +227,14 @@
                 base = (index * 2 + r) * pairs + start + k
                 out[pl.ds(base, 128, stride=count * 2 * pairs), :] = one
 
-    def choose(half):
-        start = half * step_rows
-        place = start + lax.broadcasted_iota(jnp.int32, (step_rows, entries), 0)
-        chosen[pl.ds(start, step_rows), :] = jnp.where(place == landing, 1.0, 0.0).astype(
-            jnp.bfloat16
-        )
-
-    steps = x_local // 8
-    choose(0)
-    scatter(0, 0)
-    choose(1)
-    scatter(0, 1)
+    place = lax.broadcasted_iota(jnp.int32, (slab_rows, entries), 0)
+    chosen[...] = jnp.where(place == landing, 1.0, 0.0).astype(jnp.bfloat16)
+    scatter(0)
     for index in range(count):
-        for half in range(2):
-            if index + 1 < count:
-                scatter(index + 1, half)
-            for step in range(half * steps // 2, (half + 1) * steps // 2):
-                transform(index, step)
+        if index + 1 < count:
+            scatter(index + 1)
+        for step in range(x_local // 8):
+            transform(index, step)
         for start in range(0, pairs, 2):
             along_y(index, start)
 

time: 173 us -> 173 us (level)
  no operation moved by 1% of the time
where the time goes in v10:
time: 173 us; the launch traced here: 172 us
  blocking collectives  154 us (89%)
  Pallas kernels  16.2 us (9%)
    all_to_all x2, blocking collectives, exchange(): return lax.all_to_all(data, places, split_axis=0, concat_axis=0, tiled=True)  154 us
    pallas_call x1, Pallas kernels, field(): pl.pallas_call(functools.partial(field_kernel, sizes), out_shape=pltpu.HB...  7.24 us
    pallas_call x1, Pallas kernels, slab_waves(): pl.pallas_call(functools.partial(slab_kernel, count, x_local, blocks, per...  5.4 us
    pallas_call x1, Pallas kernels, pack(): pl.pallas_call(functools.partial(pack_kernel, devices, mesh_sizes, per_ow...  3.56 us

profile of v10, /device:TPU:0, one launch (start us, length us, event | category | flops | bytes accessed | tf_op | source)
XLA Modules:
  0.0 171.6 jit_solution(14752690218435057999)
XLA Ops:
  0.7 3.6 %shard_map.91 = f32[32,200,128]{2,1,0:T(8,128)S(1)} custom-call(s32[1]{0:T(128)S(6)} %copy.11.count, s32[1]{0:T(128)} %bitcast.me, s32[1,512]{1,0:T(1,128)} %bitcast.10, s32[1,512]{1,0:T(1,128)} %bitcast.11, f32[2,3,512,128]{3,2,1,0:T(8,128)} %tiles.1), custom_call_target="tpu_custom_call" | custom-call | flops 1610612736 | bytes 6553600 | tf_op jit(solution)/shard_map/pallas_call | solution.py:151
  4.2 0.0 copy-start.2
  4.2 0.0 copy-start.3
  4.2 82.2 %all_to_all.10.data = f32[32,200,128]{2,1,0:T(8,128)S(1)} all-to-all(f32[32,200,128]{2,1,0:T(8,128)S(1)} %shard_map.91), channel_id=1, replica_groups=mesh['gx'=4,'gz'=4,'gl'=2] {'gl','gx','gz'}, dimensions={0} | all-to-all | bytes 6553600 | tf_op jit(solution)/shard_map/all_to_all | solution.py:469
  86.4 0.0 copy-done.2
  86.4 0.0 copy-done.3
  86.4 5.4 %shard_map.92 = f32[6144,128]{1,0:T(8,128)S(1)} custom-call(f32[256,256]{1,0:T(8,128)S(1)} %copy-done.2, f32[2,16,128]{2,1,0:T(8,128)S(1)} %copy-done.3, f32[32,200,128]{2,1,0:T(8,128)S(1)} %all_to_all.10.data), custom_call_target="tpu_custom_call" | custom-call | flops 4831838208 | bytes 6291456 | tf_op jit(solution)/shard_map/pallas_call | solution.py:253
  91.8 0.0 copy-start
  91.8 0.0 copy-start.1
  91.8 72.3 %all_to_all.11.data = f32[32,192,128]{2,1,0:T(8,128)S(1)} all-to-all(f32[32,192,128]{2,1,0:T(8,128)S(1)} %bitcast.8), channel_id=1, replica_groups=mesh['gx'=4,'gz'=4,'gl'=2] {'gl','gx','gz'}, dimensions={0} | all-to-all | bytes 6291456 | tf_op jit(solution)/shard_map/all_to_all | solution.py:469
  164.2 0.0 copy-done
  164.2 0.0 copy-done.1
  164.2 7.2 %shard_map.93 = f32[2,3,64,2048]{3,2,1,0:T(8,128)} custom-call(f32[2,32,128]{2,1,0:T(8,128)S(1)} %copy-done.1, f32[256,256]{1,0:T(8,128)S(1)} %copy-done, f32[32,192,128]{2,1,0:T(8,128)S(1)} %all_to_all.11.data, f32[2,6,64,2048]{3,2,1,0:T(8,128)} %bitcast.9), custom_call_target="tpu_custom_call" | custom-call | flops 613416960 | bytes 12582912 | tf_op jit(solution)/shard_map/pallas_call | solution.py:446
Async XLA Ops:
  4.2 82.2 %copy-start.2 = (f32[256,256]{1,0:T(8,128)S(1)}, f32[256,256]{1,0:T(8,128)}, u32[]{:S(2)}) copy-start(f32[256,256]{1,0:T(8,128)} %constant.23.clone.table) | copy-start | bytes 786436
  4.2 82.2 %copy-start.3 = (f32[2,16,128]{2,1,0:T(8,128)S(1)}, f32[2,16,128]{2,1,0:T(8,128)}, u32[]{:S(2)}) copy-start(f32[2,16,128]{2,1,0:T(8,128)} %constant.24.clone.twist) | copy-start | bytes 49156
  91.8 72.3 %copy-start = (f32[256,256]{1,0:T(8,128)S(1)}, f32[256,256]{1,0:T(8,128)}, u32[]{:S(2)}) copy-start(f32[256,256]{1,0:T(8,128)} %constant.26.clone.table) | copy-start | bytes 786436
  91.8 72.3 %copy-start.1 = (f32[2,32,128]{2,1,0:T(8,128)S(1)}, f32[2,32,128]{2,1,0:T(8,128)}, u32[]{:S(2)}) copy-start(f32[2,32,128]{2,1,0:T(8,128)} %constant.25.clone.twist) | copy-start | bytes 98308

commit v11 on v10

--- a/solution.py
+++ b/solution.py
@@ -131,8 +131,7 @@
     coarse = (named * (stated >> 5).astype(jnp.float32)).astype(jnp.bfloat16)
     fine = (named * (stated & 31).astype(jnp.float32)).astype(jnp.bfloat16)
     slots = 32.0 * dot_rows(coarse, laned) + dot_rows(fine, laned)
-    start = 2 * len(comps) * per_owner
-    out[:, start:, :] = jnp.broadcast_to(slots[:, None, :], (devices, 8, 128))
+    out[:, out.shape[1] - 1] = jnp.broadcast_to(slots[:, None, :], (devices, 4, 128))
     for i in range(len(comps)):
         fetches[2 + i].wait()
         parts = [part for r in range(2) for part in split_two(held[i, r])]
@@ -141,16 +140,18 @@
         )
         for r in range(2):
             whole = got[:, 256 * r : 256 * r + 128] + got[:, 256 * r + 128 : 256 * r + 256]
-            start = (2 * i + r) * per_owner
-            out[:, start : start + per_owner, :] = whole.reshape(devices, per_owner, 128)
+            start = (2 * i + r) * per_owner // 4
+            out[:, start : start + per_owner // 4] = whole.reshape(
+                devices, per_owner // 4, 4, 128
+            )
 
 
 def pack(tiles, owner_row, slot_row, count, me, devices, mesh_sizes, per_owner):
     comps, listed = tiles.shape[1:3]
-    rows = 2 * comps * per_owner + 8
+    rows = 2 * comps * per_owner + 4
     return pl.pallas_call(
         functools.partial(pack_kernel, devices, mesh_sizes, per_owner),
-        out_shape=pltpu.VMEM((devices, rows, 128), jnp.float32),
+        out_shape=pltpu.VMEM((devices, rows // 4, 4, 128), jnp.float32),
         in_specs=[pl.BlockSpec(memory_space=pltpu.SMEM)] * 2
         + [pl.BlockSpec(memory_space=pltpu.HBM)] * 3,
         out_specs=pl.BlockSpec(memory_space=pltpu.VMEM),
@@ -184,7 +185,7 @@
     shift = blocks.bit_length() - 1
     every = 128 // per_owner
     stated = [
-        sum([data[o, data.shape[1] - 8 :][:1] for o in range(start, start + every)])
+        sum([data[o, data.shape[1] - 1, :1] for o in range(start, start + every)])
         for start in range(0, devices, every)
     ]
     slot = jnp.concatenate(stated, axis=1).astype(jnp.int32) - 1
@@ -195,8 +196,9 @@
     def scatter(index):
         parts = []
         for r in range(2):
-            start = (2 * index + r) * per_owner
-            parts.extend(split_two(data[:, start : start + per_owner, :].reshape(entries, 128)))
+            start = (2 * index + r) * per_owner // 4
+            one = data[:, start : start + per_owner // 4]
+            parts.extend(split_two(one.reshape(entries, 128)))
         got = jnp.dot(
             chosen[...], jnp.concatenate(parts, axis=1), preferred_element_type=jnp.float32
         )
@@ -241,7 +243,7 @@
 
 def slab_waves(data, x_local, blocks, mesh_sizes, per_owner):
     devices = data.shape[0]
-    count = data.shape[1] // (2 * per_owner)
+    count = data.shape[1] * 4 // (2 * per_owner)
     fine = angles(128, 128, 128)
     order = owner_order(mesh_sizes)
     fine = fine.reshape(devices, 128 // devices, 128)[order].reshape(128, 128)

time: 173 us -> 172 us (level)
  no operation moved by 1% of the time
where the time goes in v11:
time: 172 us; the launch traced here: 170 us
  blocking collectives  153 us (89%)
  Pallas kernels  16.2 us (9%)
    all_to_all x2, blocking collectives, exchange(): return lax.all_to_all(data, places, split_axis=0, concat_axis=0, tiled=True)  153 us
    pallas_call x1, Pallas kernels, field(): pl.pallas_call(functools.partial(field_kernel, sizes), out_shape=pltpu.HB...  7.24 us
    pallas_call x1, Pallas kernels, slab_waves(): pl.pallas_call(functools.partial(slab_kernel, count, x_local, blocks, per...  5.43 us
    pallas_call x1, Pallas kernels, pack(): pl.pallas_call(functools.partial(pack_kernel, devices, mesh_sizes, per_ow...  3.56 us

profile of v11, /device:TPU:0, one launch (start us, length us, event | category | flops | bytes accessed | tf_op | source)
XLA Modules:
  0.0 170.2 jit_solution(8563328888272076596)
XLA Ops:
  0.7 3.6 %shard_map.91 = f32[32,49,4,128]{3,2,1,0:T(4,128)S(1)} custom-call(s32[1]{0:T(128)S(6)} %copy.11.count, s32[1]{0:T(128)} %bitcast.me, s32[1,512]{1,0:T(1,128)} %bitcast.10, s32[1,512]{1,0:T(1,128)} %bitcast.11, f32[2,3,512,128]{3,2,1,0:T(8,128)} %tiles.1), custom_call_target="tpu_custom_call" | custom-call | flops 1610612736 | bytes 6422528 | tf_op jit(solution)/shard_map/pallas_call | solution.py:152
  4.2 0.0 copy-start.2
  4.2 0.0 copy-start.3
  4.2 81.2 %all_to_all.10.data = f32[32,49,4,128]{3,2,1,0:T(4,128)S(1)} all-to-all(f32[32,49,4,128]{3,2,1,0:T(4,128)S(1)} %shard_map.91), channel_id=1, replica_groups=mesh['gx'=4,'gz'=4,'gl'=2] {'gl','gx','gz'}, dimensions={0} | all-to-all | bytes 6422528 | tf_op jit(solution)/shard_map/all_to_all | solution.py:471
  85.5 0.0 copy-done.2
  85.5 0.0 copy-done.3
  85.5 5.4 %shard_map.92 = f32[6144,128]{1,0:T(8,128)S(1)} custom-call(f32[256,256]{1,0:T(8,128)S(1)} %copy-done.2, f32[2,16,128]{2,1,0:T(8,128)S(1)} %copy-done.3, f32[32,49,4,128]{3,2,1,0:T(4,128)S(1)} %all_to_all.10.data), custom_call_target="tpu_custom_call" | custom-call | flops 4831838208 | bytes 6291456 | tf_op jit(solution)/shard_map/pallas_call | solution.py:255
  90.9 0.0 copy-start
  90.9 0.0 copy-start.1
  90.9 71.9 %all_to_all.11.data = f32[32,192,128]{2,1,0:T(8,128)S(1)} all-to-all(f32[32,192,128]{2,1,0:T(8,128)S(1)} %bitcast.8), channel_id=1, replica_groups=mesh['gx'=4,'gz'=4,'gl'=2] {'gl','gx','gz'}, dimensions={0} | all-to-all | bytes 6291456 | tf_op jit(solution)/shard_map/all_to_all | solution.py:471
  162.8 0.0 copy-done
  162.8 0.0 copy-done.1
  162.8 7.2 %shard_map.93 = f32[2,3,64,2048]{3,2,1,0:T(8,128)} custom-call(f32[2,32,128]{2,1,0:T(8,128)S(1)} %copy-done.1, f32[256,256]{1,0:T(8,128)S(1)} %copy-done, f32[32,192,128]{2,1,0:T(8,128)S(1)} %all_to_all.11.data, f32[2,6,64,2048]{3,2,1,0:T(8,128)} %bitcast.9), custom_call_target="tpu_custom_call" | custom-call | flops 613416960 | bytes 12582912 | tf_op jit(solution)/shard_map/pallas_call | solution.py:448
Async XLA Ops:
  4.2 81.2 %copy-start.2 = (f32[256,256]{1,0:T(8,128)S(1)}, f32[256,256]{1,0:T(8,128)}, u32[]{:S(2)}) copy-start(f32[256,256]{1,0:T(8,128)} %constant.23.clone.table) | copy-start | bytes 786436
  4.2 81.2 %copy-start.3 = (f32[2,16,128]{2,1,0:T(8,128)S(1)}, f32[2,16,128]{2,1,0:T(8,128)}, u32[]{:S(2)}) copy-start(f32[2,16,128]{2,1,0:T(8,128)} %constant.24.clone.twist) | copy-start | bytes 49156
  90.9 71.9 %copy-start = (f32[256,256]{1,0:T(8,128)S(1)}, f32[256,256]{1,0:T(8,128)}, u32[]{:S(2)}) copy-start(f32[256,256]{1,0:T(8,128)} %constant.26.clone.table) | copy-start | bytes 786436
  90.9 71.9 %copy-start.1 = (f32[2,32,128]{2,1,0:T(8,128)S(1)}, f32[2,32,128]{2,1,0:T(8,128)}, u32[]{:S(2)}) copy-start(f32[2,32,128]{2,1,0:T(8,128)} %constant.25.clone.twist) | copy-start | bytes 98308

commit v12 on v11

--- a/solution.py
+++ b/solution.py
@@ -131,7 +131,7 @@
     coarse = (named * (stated >> 5).astype(jnp.float32)).astype(jnp.bfloat16)
     fine = (named * (stated & 31).astype(jnp.float32)).astype(jnp.bfloat16)
     slots = 32.0 * dot_rows(coarse, laned) + dot_rows(fine, laned)
-    out[:, out.shape[1] - 1] = jnp.broadcast_to(slots[:, None, :], (devices, 4, 128))
+    out[:, out.shape[1] - 1] = jnp.broadcast_to(slots[:, None, :], (devices, 2, 128))
     for i in range(len(comps)):
         fetches[2 + i].wait()
         parts = [part for r in range(2) for part in split_two(held[i, r])]
@@ -140,18 +140,18 @@
         )
         for r in range(2):
             whole = got[:, 256 * r : 256 * r + 128] + got[:, 256 * r + 128 : 256 * r + 256]
-            start = (2 * i + r) * per_owner // 4
-            out[:, start : start + per_owner // 4] = whole.reshape(
-                devices, per_owner // 4, 4, 128
+            start = (2 * i + r) * per_owner // 2
+            out[:, start : start + per_owner // 2] = whole.reshape(
+                devices, per_owner // 2, 2, 128
             )
 
 
 def pack(tiles, owner_row, slot_row, count, me, devices, mesh_sizes, per_owner):
     comps, listed = tiles.shape[1:3]
-    rows = 2 * comps * per_owner + 4
+    rows = 2 * comps * per_owner + 2
     return pl.pallas_call(
         functools.partial(pack_kernel, devices, mesh_sizes, per_owner),
-        out_shape=pltpu.VMEM((devices, rows // 4, 4, 128), jnp.float32),
+        out_shape=pltpu.VMEM((devices, rows // 2, 2, 128), jnp.float32),
         in_specs=[pl.BlockSpec(memory_space=pltpu.SMEM)] * 2
         + [pl.BlockSpec(memory_space=pltpu.HBM)] * 3,
         out_specs=pl.BlockSpec(memory_space=pltpu.VMEM),
@@ -196,8 +196,8 @@
     def scatter(index):
         parts = []
         for r in range(2):
-            start = (2 * index + r) * per_owner // 4
-            one = data[:, start : start + per_owner // 4]
+            start = (2 * index + r) * per_owner // 2
+            one = data[:, start : start + per_owner // 2]
             parts.extend(split_two(one.reshape(entries, 128)))
         got = jnp.dot(
             chosen[...], jnp.concatenate(parts, axis=1), preferred_element_type=jnp.float32
@@ -243,7 +243,7 @@
 
 def slab_waves(data, x_local, blocks, mesh_sizes, per_owner):
     devices = data.shape[0]
-    count = data.shape[1] * 4 // (2 * per_owner)
+    count = data.shape[1] * 2 // (2 * per_owner)
     fine = angles(128, 128, 128)
     order = owner_order(mesh_sizes)
     fine = fine.reshape(devices, 128 // devices, 128)[order].reshape(128, 128)

time: 172 us -> 171 us (level)
  no operation moved by 1% of the time
where the time goes in v12:
time: 171 us; the launch traced here: 170 us
  blocking collectives  153 us (89%)
  Pallas kernels  16.7 us (10%)
    all_to_all x2, blocking collectives, exchange(): return lax.all_to_all(data, places, split_axis=0, concat_axis=0, tiled=True)  153 us
    pallas_call x1, Pallas kernels, field(): pl.pallas_call(functools.partial(field_kernel, sizes), out_shape=pltpu.HB...  7.24 us
    pallas_call x1, Pallas kernels, slab_waves(): pl.pallas_call(functools.partial(slab_kernel, count, x_local, blocks, per...  5.74 us
    pallas_call x1, Pallas kernels, pack(): pl.pallas_call(functools.partial(pack_kernel, devices, mesh_sizes, per_ow...  3.75 us

profile of v12, /device:TPU:0, one launch (start us, length us, event | category | flops | bytes accessed | tf_op | source)
XLA Modules:
  0.0 170.1 jit_solution(15718057003466375502)
XLA Ops:
  0.7 3.8 %shard_map.91 = f32[32,97,2,128]{3,2,1,0:T(2,128)S(1)} custom-call(s32[1]{0:T(128)S(6)} %copy.11.count, s32[1]{0:T(128)} %bitcast.me, s32[1,512]{1,0:T(1,128)} %bitcast.10, s32[1,512]{1,0:T(1,128)} %bitcast.11, f32[2,3,512,128]{3,2,1,0:T(8,128)} %tiles.1), custom_call_target="tpu_custom_call" | custom-call | flops 1610612736 | bytes 6356992 | tf_op jit(solution)/shard_map/pallas_call | solution.py:152
  4.4 0.0 copy-start.2
  4.4 0.0 copy-start.3
  4.4 80.7 %all_to_all.10.data = f32[32,97,2,128]{3,2,1,0:T(2,128)S(1)} all-to-all(f32[32,97,2,128]{3,2,1,0:T(2,128)S(1)} %shard_map.91), channel_id=1, replica_groups=mesh['gx'=4,'gz'=4,'gl'=2] {'gl','gx','gz'}, dimensions={0} | all-to-all | bytes 6356992 | tf_op jit(solution)/shard_map/all_to_all | solution.py:471
  85.1 0.0 copy-done.2
  85.1 0.0 copy-done.3
  85.1 5.7 %shard_map.92 = f32[6144,128]{1,0:T(8,128)S(1)} custom-call(f32[256,256]{1,0:T(8,128)S(1)} %copy-done.2, f32[2,16,128]{2,1,0:T(8,128)S(1)} %copy-done.3, f32[32,97,2,128]{3,2,1,0:T(2,128)S(1)} %all_to_all.10.data), custom_call_target="tpu_custom_call" | custom-call | flops 4831838208 | bytes 6291456 | tf_op jit(solution)/shard_map/pallas_call | solution.py:255
  90.8 0.0 copy-start
  90.9 0.0 copy-start.1
  90.9 71.9 %all_to_all.11.data = f32[32,192,128]{2,1,0:T(8,128)S(1)} all-to-all(f32[32,192,128]{2,1,0:T(8,128)S(1)} %bitcast.8), channel_id=1, replica_groups=mesh['gx'=4,'gz'=4,'gl'=2] {'gl','gx','gz'}, dimensions={0} | all-to-all | bytes 6291456 | tf_op jit(solution)/shard_map/all_to_all | solution.py:471
  162.7 0.0 copy-done
  162.7 0.0 copy-done.1
  162.7 7.2 %shard_map.93 = f32[2,3,64,2048]{3,2,1,0:T(8,128)} custom-call(f32[2,32,128]{2,1,0:T(8,128)S(1)} %copy-done.1, f32[256,256]{1,0:T(8,128)S(1)} %copy-done, f32[32,192,128]{2,1,0:T(8,128)S(1)} %all_to_all.11.data, f32[2,6,64,2048]{3,2,1,0:T(8,128)} %bitcast.9), custom_call_target="tpu_custom_call" | custom-call | flops 613416960 | bytes 12582912 | tf_op jit(solution)/shard_map/pallas_call | solution.py:448
Async XLA Ops:
  4.4 80.7 %copy-start.2 = (f32[256,256]{1,0:T(8,128)S(1)}, f32[256,256]{1,0:T(8,128)}, u32[]{:S(2)}) copy-start(f32[256,256]{1,0:T(8,128)} %constant.23.clone.table) | copy-start | bytes 786436
  4.4 80.7 %copy-start.3 = (f32[2,16,128]{2,1,0:T(8,128)S(1)}, f32[2,16,128]{2,1,0:T(8,128)}, u32[]{:S(2)}) copy-start(f32[2,16,128]{2,1,0:T(8,128)} %constant.24.clone.twist) | copy-start | bytes 49156
  90.8 71.9 %copy-start = (f32[256,256]{1,0:T(8,128)S(1)}, f32[256,256]{1,0:T(8,128)}, u32[]{:S(2)}) copy-start(f32[256,256]{1,0:T(8,128)} %constant.26.clone.table) | copy-start | bytes 786436
  90.9 71.9 %copy-start.1 = (f32[2,32,128]{2,1,0:T(8,128)S(1)}, f32[2,32,128]{2,1,0:T(8,128)}, u32[]{:S(2)}) copy-start(f32[2,32,128]{2,1,0:T(8,128)} %constant.25.clone.twist) | copy-start | bytes 98308
